TPU v7x, 32 devices: a whole 2x2x4 slice. The times are simulated.
32 devices in a mesh: beam: 8 (over y, x, core), seg: 4 (over z).
Axes of the slice: x: 2, y: 2, z: 4, core: 2. Of those that a mesh axis runs over, the one named last changes fastest.
Arguments:
- voltages: bfloat16 [2, 128, 4, 65536], P(None, 'beam', 'seg'), may hold values from -6 to 6
- surv_taps: bfloat16 [32], replicated, may hold values from -1 to 1
- ref_taps: bfloat16 [32], replicated, may hold values from -1 to 1
- tx_owner: int32 [4], replicated, may hold values from 0 to 127
- delay_start: int32 [4], replicated, may hold values from 0 to 384
- doppler_start: int32 [4], replicated, may hold values from 0 to 128
Outputs:
- maps: float32 [4, 128, 128, 128], P(None, 'beam', 'seg')
All inputs are finite; a program needn't handle non-finite values.
Results may differ from a plain program's by a relative error of at most 0.0027.
Values may be sent and summed in bfloat16 or wider, within the bound.
No kernel may reach another device: no remote copies, remote signals or barrier semaphores. Data moves between devices by JAX's collectives and lax.ppermute only.
A program may use at most 128 MiB of HBM per device.

v0:
```python
import functools

import jax
import jax.numpy as jnp
import ml_dtypes
import numpy as np
from jax import lax
from jax.experimental import pallas as pl
from jax.experimental.pallas import tpu as pltpu
from jax.sharding import PartitionSpec as P

TX = 4
DECIM = 4
TAPS = 32
BLOCK_LEN = 64
BLOCKS = 256
DELAYS = 128
DOPPLER = 128
FFT = 256
STRIDE = DECIM * BLOCK_LEN
LEAD = 128
REACH = LEAD + STRIDE
GROUPS = 4
VMEM_LIMIT = 50 * 1024 * 1024


def split_bf16(table):
    hi = table.astype(ml_dtypes.bfloat16)
    lo = (table - hi.astype(np.float64)).astype(ml_dtypes.bfloat16)
    return hi, lo


def fourier(samples):
    angle = 2 * np.pi / FFT * (np.outer(np.arange(FFT), samples) % FFT)
    cos, sin = np.cos(angle), np.sin(angle)
    return np.block([[cos, sin], [-sin, cos]])


def surv_fourier():
    hi, lo = split_bf16(fourier(np.arange(BLOCK_LEN)))
    return np.concatenate([hi, lo], axis=1)


def ref_fourier():
    parts = [fourier(np.arange(BLOCK_LEN) + BLOCK_LEN * e) for e in range(4)]
    hi, lo = split_bf16(np.concatenate(parts, axis=1))
    return np.concatenate([hi, lo], axis=1)


def lag_table():
    lags = 191 - np.arange(192)
    angle = 2 * np.pi / FFT * (np.outer(lags, np.arange(FFT)) % FFT)
    cos, sin = np.cos(angle), np.sin(angle)
    scale = 1.0 / (FFT * np.sqrt(BLOCK_LEN))
    both = np.stack([np.concatenate([cos, sin], 1), np.concatenate([-sin, cos], 1)])
    return (both.astype(ml_dtypes.bfloat16).astype(np.float64) * scale).astype(
        ml_dtypes.bfloat16
    )


def doppler_tables(f_lo):
    ells = jnp.arange(BLOCKS, dtype=jnp.int32)
    freqs = f_lo + jnp.arange(DOPPLER, dtype=jnp.int32) - BLOCKS // 2
    phase = ells[:, None] * freqs[None, :] % BLOCKS
    angle = 2.0 * jnp.pi / BLOCKS * phase.astype(jnp.float32)
    cos = jnp.cos(angle).astype(jnp.bfloat16)
    sin = jnp.sin(angle).astype(jnp.bfloat16)
    return jnp.concatenate(
        [jnp.concatenate([cos, -sin], 1), jnp.concatenate([sin, cos], 1)], 0
    )


def nt_dot(left, right):
    return lax.dot_general(
        left, right, (((1,), (1,)), ((), ())), preferred_element_type=jnp.float32
    )


def decimate_kernel(
    beams, rows, local_ref, mine_ref, taps_ref, prev_ref, x_ref, s_ref, r_ref, band, keep_s, keep_r
):
    step = pl.program_id(0)

    @pl.when(step == 0)
    def _():
        shape = (REACH, 2 * BLOCK_LEN)
        q = lax.broadcasted_iota(jnp.int32, shape, 0)
        lane = lax.broadcasted_iota(jnp.int32, shape, 1)
        tap = LEAD + DECIM * (lane % BLOCK_LEN) - q
        first = lane < BLOCK_LEN
        both = jnp.zeros(shape, jnp.float32)
        for t in range(TAPS):
            value = jnp.where(first, taps_ref[0, t], taps_ref[1, t])
            both = jnp.where(tap == t, value, both)
        turned = pltpu.roll(both, BLOCK_LEN, 1)
        zero = jnp.zeros(shape, jnp.float32)
        half = 2 * BLOCK_LEN
        band[:REACH, :half] = jnp.where(first, both, zero).astype(jnp.bfloat16)
        band[REACH:, :half] = jnp.where(first, zero, turned).astype(jnp.bfloat16)
        band[:REACH, half:] = jnp.where(first, turned, zero).astype(jnp.bfloat16)
        band[REACH:, half:] = jnp.where(first, zero, both).astype(jnp.bfloat16)

    prev = prev_ref[...] * (step > 0).astype(jnp.bfloat16)
    x = jnp.concatenate([prev, x_ref[...]], axis=2)
    parts = []
    for c in range(2):
        parts.append(
            jnp.concatenate([x[c, :, l * STRIDE : l * STRIDE + REACH] for l in range(rows)], axis=0)
        )
    lhs = jnp.concatenate(parts, axis=1)
    out = jnp.dot(lhs, band[...], preferred_element_type=jnp.float32)
    keep_s[...] = out[:, : 2 * BLOCK_LEN]
    keep_r[...] = out[:, 2 * BLOCK_LEN :]
    for b in range(beams):
        s_ref[b] = keep_s[pl.ds(b, rows, stride=beams), :].astype(jnp.bfloat16)
    for k in range(TX):
        picked = keep_r[pl.ds(local_ref[k], rows, stride=beams), :]
        r_ref[k] = jnp.where(mine_ref[k] > 0, picked, 0.0).astype(jnp.bfloat16)


def decimate(volts, taps, local, mine):
    beams, raw = volts.shape[1:]
    rows = 32
    steps = raw // (rows * STRIDE)
    wide = rows * STRIDE
    blocks = raw // STRIDE
    return pl.pallas_call(
        functools.partial(decimate_kernel, beams, rows),
        grid=(steps,),
        in_specs=[
            pl.BlockSpec(memory_space=pltpu.SMEM),
            pl.BlockSpec(memory_space=pltpu.SMEM),
            pl.BlockSpec(memory_space=pltpu.SMEM),
            pl.BlockSpec(
                (2, beams, LEAD), lambda i: (0, 0, jnp.maximum(i * (wide // LEAD) - 1, 0))
            ),
            pl.BlockSpec((2, beams, wide), lambda i: (0, 0, i)),
        ],
        out_specs=[
            pl.BlockSpec((beams, rows, 2 * BLOCK_LEN), lambda i: (0, i, 0)),
            pl.BlockSpec((TX, rows, 2 * BLOCK_LEN), lambda i: (0, i, 0)),
        ],
        out_shape=[
            jax.ShapeDtypeStruct((beams, blocks, 2 * BLOCK_LEN), jnp.bfloat16),
            jax.ShapeDtypeStruct((TX, blocks, 2 * BLOCK_LEN), jnp.bfloat16),
        ],
        scratch_shapes=[
            pltpu.VMEM((2 * REACH, 4 * BLOCK_LEN), jnp.bfloat16),
            pltpu.VMEM((rows * beams, 2 * BLOCK_LEN), jnp.float32),
            pltpu.VMEM((rows * beams, 2 * BLOCK_LEN), jnp.float32),
        ],
        compiler_params=pltpu.CompilerParams(vmem_limit_bytes=VMEM_LIMIT),
        name="decimate",
    )(local, mine, taps, volts, volts)


PAD = 8


def spectra_kernel(shift_ref, table_ref, r_ref, out_ref, padded):
    k = pl.program_id(0)
    padded[:PAD] = jnp.zeros((PAD, 2 * BLOCK_LEN), jnp.float32)
    padded[PAD + BLOCKS :] = jnp.zeros((PAD, 2 * BLOCK_LEN), jnp.float32)
    padded[PAD : PAD + BLOCKS] = r_ref[0].astype(jnp.float32)
    start = PAD - 1 - shift_ref[k]
    window = jnp.concatenate(
        [padded[pl.ds(start + e, BLOCKS), :].astype(jnp.bfloat16) for e in range(4)], axis=1
    )
    both = jnp.concatenate([window, window], axis=1)
    out_ref[0] = nt_dot(table_ref[...], both)


def ref_spectra(shift, ref):
    table = jnp.asarray(ref_fourier())
    return pl.pallas_call(
        spectra_kernel,
        grid=(TX,),
        in_specs=[
            pl.BlockSpec(memory_space=pltpu.SMEM),
            pl.BlockSpec(table.shape, lambda k: (0, 0)),
            pl.BlockSpec((1, BLOCKS, 2 * BLOCK_LEN), lambda k: (k, 0, 0)),
        ],
        out_specs=pl.BlockSpec((1, 2 * FFT, BLOCKS), lambda k: (k, 0, 0)),
        out_shape=jax.ShapeDtypeStruct((TX, 2 * FFT, BLOCKS), jnp.float32),
        scratch_shapes=[pltpu.VMEM((BLOCKS + 2 * PAD, 2 * BLOCK_LEN), jnp.float32)],
        compiler_params=pltpu.CompilerParams(vmem_limit_bytes=VMEM_LIMIT),
        name="ref_spectra",
    )(shift, table, ref)


def power_kernel(chunks, table_ref, s_ref, r_ref, lag_ref, dop_ref, out_ref):
    s = s_ref[0]
    spec = nt_dot(table_ref[...], jnp.concatenate([s, s], axis=1))
    s_re, s_im = spec[:FFT], spec[FFT:]
    each = DELAYS // chunks
    for k in range(TX):
        r_re, r_im = r_ref[k, :FFT], r_ref[k, FFT:]
        p_re = (s_re * r_re + s_im * r_im).astype(jnp.bfloat16)
        p_im = (s_im * r_re - s_re * r_im).astype(jnp.bfloat16)
        prod = jnp.concatenate([p_re, p_im], axis=0)
        corr = jnp.dot(lag_ref[k], prod, preferred_element_type=jnp.float32)
        corr = corr.astype(jnp.bfloat16)
        corr = jnp.concatenate([corr[:DELAYS], corr[DELAYS:]], axis=1)
        x = jnp.dot(corr, dop_ref[k], preferred_element_type=jnp.float32)
        x_re, x_im = x[:, :DOPPLER], x[:, DOPPLER:]
        power = (x_re * x_re + x_im * x_im) * (1.0 / (4 * BLOCKS))
        for g in range(chunks):
            out_ref[g, k, 0] = power[g * each : (g + 1) * each].astype(jnp.bfloat16)


def powers(surv, first, count, spectra, lags, dops, chunks):
    table = jnp.asarray(surv_fourier())
    each = DELAYS // chunks
    return pl.pallas_call(
        functools.partial(power_kernel, chunks),
        grid=(count,),
        in_specs=[
            pl.BlockSpec(table.shape, lambda b: (0, 0)),
            pl.BlockSpec((1, BLOCKS, 2 * BLOCK_LEN), lambda b: (first + b, 0, 0)),
            pl.BlockSpec(spectra.shape, lambda b: (0, 0, 0)),
            pl.BlockSpec(lags.shape, lambda b: (0, 0, 0)),
            pl.BlockSpec(dops.shape, lambda b: (0, 0, 0)),
        ],
        out_specs=pl.BlockSpec((chunks, TX, 1, each, DOPPLER), lambda b: (0, 0, b, 0, 0)),
        out_shape=jax.ShapeDtypeStruct((chunks, TX, count, each, DOPPLER), jnp.bfloat16),
        compiler_params=pltpu.CompilerParams(vmem_limit_bytes=VMEM_LIMIT),
        cost_estimate=pl.CostEstimate(
            flops=count * TX * 2 * 768 * 65536, bytes_accessed=6 << 20, transcendentals=0
        ),
        name="powers",
    )(table, surv, spectra, lags, dops)


def shards(voltages, surv_taps, ref_taps, tx_owner, delay_start, doppler_start):
    beams_here = voltages.shape[1]
    n_beam = lax.axis_size("beam")
    n_seg = lax.axis_size("seg")
    me = lax.axis_index("beam")
    seg = lax.axis_index("seg")
    segments_all = n_seg * voltages.shape[2]
    volts = voltages.reshape(2, beams_here, voltages.shape[3])
    taps = jnp.stack([surv_taps, ref_taps]).astype(jnp.float32)
    mine = (tx_owner // beams_here == me).astype(jnp.int32)
    surv, ref = decimate(volts, taps, tx_owner % beams_here, mine)
    hop = 1
    while hop < n_beam:
        ref = ref + lax.ppermute(ref, "beam", [(i, i ^ hop) for i in range(n_beam)])
        hop *= 2
    lead = delay_start + (DELAYS - 1)
    spectra = ref_spectra(lead // BLOCK_LEN, ref)
    table = jnp.asarray(lag_table())
    lags = jnp.stack(
        [
            lax.dynamic_slice_in_dim(table, lead[k] % BLOCK_LEN, DELAYS, 1).reshape(
                2 * DELAYS, 2 * FFT
            )
            for k in range(TX)
        ]
    )
    dops = jnp.stack([doppler_tables(doppler_start[k]) for k in range(TX)])
    count = beams_here // GROUPS
    maps = []
    for g in range(GROUPS):
        part = powers(surv, g * count, count, spectra, lags, dops, n_seg)
        total = lax.dynamic_index_in_dim(part, seg, 0, keepdims=False).astype(jnp.float32)
        for turn in range(1, n_seg):
            send = lax.dynamic_index_in_dim(part, (seg + turn) % n_seg, 0, keepdims=False)
            got = lax.ppermute(send, "seg", [(i, (i + turn) % n_seg) for i in range(n_seg)])
            total = total + got.astype(jnp.float32)
        maps.append(total / segments_all)
    return jnp.concatenate(maps, axis=1)


def solution(mesh):
    return jax.shard_map(
        shards,
        mesh=mesh,
        in_specs=(P(None, "beam", "seg", None), P(), P(), P(), P(), P()),
        out_specs=P(None, "beam", "seg", None),
        check_vma=False,
    )
```

profile of v0, /device:TPU:0, one launch (start us, length us, event | category | flops | bytes accessed | tf_op | source)
XLA Modules:
  0.0 126.6 jit_solution(8745393267346437937)
XLA Ops:
  0.0 0.7 and_select_fusion.2.local_ref
  0.7 0.7 compare_convert_fusion.mine_ref
  1.3 0.7 maximum_convert_fusion.taps_ref
  2.0 7.4 %decimate.1 = (bf16[16,256,128]{2,1,0:T(8,128)(2,1)S(1)}, bf16[4,256,128]{2,1,0:T(8,128)(2,1)S(1)}) custom-call(s32[4]{0:T(128)S(1)} %and_select_fusion.2.local_ref, s32[4]{0:T(128)S(1)} %compare_convert_fusion.mine_ref, f32[2,32]{1,0:T(2,128)S(1)} %maximum_convert_fusion.taps_ref, bf16[2,16,65536]{2,1,0:T(8,128)(2,1)} %bitcast.59, ...), custom_call_target="tpu_custom_call" | custom-call | tf_op jit(solution)/shard_map/decimate/pallas_call | solution.py:127
  9.4 0.5 collective-permute-start
  9.9 0.7 fusion.40
  10.6 0.6 add_add_fusion.3
  11.2 0.5 fusion.36
  11.7 0.5 sine_convert_fusion.3
  12.3 0.7 add_add_fusion
  13.0 0.5 fusion.39
  13.5 0.5 sine_convert_fusion
  14.0 0.7 add_add_fusion.1
  14.7 0.5 fusion.38
  15.2 0.5 sine_convert_fusion.1
  15.8 0.6 add_add_fusion.2
  16.4 0.5 fusion.37
  16.9 0.7 fusion.41
  25.3 0.5 sine_convert_fusion.2
  26.0 2.6 %collective-permute-start.1 = (bf16[4,256,128]{2,1,0:T(8,128)(2,1)S(1)}, bf16[4,256,128]{2,1,0:T(8,128)(2,1)S(1)}, u32[]{:S(2)}, u32[]{:S(2)}) collective-permute-start(bf16[4,256,128]{2,1,0:T(8,128)(2,1)S(1)} %add.222), channel_id=1, source_target_pairs={{0,8},{4,12},{8,0},{12,4},{16,24},{20,28},{24,16},{28,20},{1,9},{5... | collective-permute-start | bytes 786440 | tf_op jit(solution)/shard_map/ppermute | solution.py:247
  28.6 0.1 pad_maximum_fusion.1.dop_ref
  28.7 6.8 %collective-permute-done.1 = bf16[4,256,128]{2,1,0:T(8,128)(2,1)S(1)} collective-permute-done((bf16[4,256,128]{2,1,0:T(8,128)(2,1)S(1)}, bf16[4,256,128]{2,1,0:T(8,128)(2,1)S(1)}, u32[]{:S(2)}, u32[]{:S(2)}) %collective-permute-start.1) | collective-permute-done | bytes 262176 | tf_op jit(solution)/shard_map/ppermute | solution.py:247
  35.6 1.8 %collective-permute-start.2 = (bf16[4,256,128]{2,1,0:T(8,128)(2,1)S(1)}, bf16[4,256,128]{2,1,0:T(8,128)(2,1)S(1)}, u32[]{:S(2)}, u32[]{:S(2)}) collective-permute-start(bf16[4,256,128]{2,1,0:T(8,128)(2,1)S(1)} %add.223), channel_id=1, source_target_pairs={{0,16},{4,20},{8,24},{12,28},{16,0},{20,4},{24,8},{28,12},{1,17},{... | collective-permute-start | bytes 786440 | tf_op jit(solution)/shard_map/ppermute | solution.py:247
  37.4 0.3 constant_dynamic-slice_fusion.3
  37.7 0.1 pad_maximum_fusion.lag_ref
  37.8 5.9 %collective-permute-done.2 = bf16[4,256,128]{2,1,0:T(8,128)(2,1)S(1)} collective-permute-done((bf16[4,256,128]{2,1,0:T(8,128)(2,1)S(1)}, bf16[4,256,128]{2,1,0:T(8,128)(2,1)S(1)}, u32[]{:S(2)}, u32[]{:S(2)}) %collective-permute-start.2) | collective-permute-done | bytes 262176 | tf_op jit(solution)/shard_map/ppermute | solution.py:247
  43.9 2.6 %ref_spectra.1.r_ref = f32[4,512,256]{2,1,0:T(8,128)S(1)} custom-call(s32[4]{0:T(128)S(1)} %get-tuple-element.42.shift_ref, bf16[512,1024]{1,0:T(8,128)(2,1)S(1)} %copy-done.2, bf16[4,256,128]{2,1,0:T(8,128)(2,1)S(1)} %add.224.r_ref), custom_call_target="tpu_custom_call" | custom-call | tf_op jit(solution)/shard_map/ref_spectra/pallas_call | solution.py:175
  46.4 1.3 %copy-done = f32[4,512,256]{2,1,0:T(8,128)} copy-done((f32[4,512,256]{2,1,0:T(8,128)}, f32[4,512,256]{2,1,0:T(8,128)S(1)}, u32[]{:S(2)}) %copy-start) | copy-done | bytes 2097176
  47.8 7.3 %powers.7 = bf16[4,4,4,32,128]{4,3,2,1,0:T(8,128)(2,1)S(1)} custom-call(bf16[512,256]{1,0:T(8,128)(2,1)S(1)} %copy-done.1, bf16[16,256,128]{2,1,0:T(8,128)(2,1)S(1)} %get-tuple-element.7.s_ref, f32[4,512,256]{2,1,0:T(8,128)} %copy-done, bf16[4,256,512]{2,1,0:T(8,128)(2,1)S(1)} %pad_maximum_fusion.lag_ref, bf16[4,512,256]{2,1,0:T(8,128)(2,1)S(1)} %pad_maximum_fusion.1.dop_ref), custom_call_target="tpu_custom_call" | custom-call | flops 1610612736 | bytes 6291456 | tf_op jit(solution)/shard_map/powers/pallas_call | solution.py:214
  55.0 7.3 %powers.6 = bf16[4,4,4,32,128]{4,3,2,1,0:T(8,128)(2,1)S(1)} custom-call(bf16[512,256]{1,0:T(8,128)(2,1)S(1)} %copy-done.1, bf16[16,256,128]{2,1,0:T(8,128)(2,1)S(1)} %get-tuple-element.7.s_ref, f32[4,512,256]{2,1,0:T(8,128)} %copy-done, bf16[4,256,512]{2,1,0:T(8,128)(2,1)S(1)} %pad_maximum_fusion.lag_ref, bf16[4,512,256]{2,1,0:T(8,128)(2,1)S(1)} %pad_maximum_fusion.1.dop_ref), custom_call_target="tpu_custom_call" | custom-call | flops 1610612736 | bytes 6291456 | tf_op jit(solution)/shard_map/powers/pallas_call | solution.py:214
  62.3 7.3 %powers.5 = bf16[4,4,4,32,128]{4,3,2,1,0:T(8,128)(2,1)S(1)} custom-call(bf16[512,256]{1,0:T(8,128)(2,1)S(1)} %copy-done.1, bf16[16,256,128]{2,1,0:T(8,128)(2,1)S(1)} %get-tuple-element.7.s_ref, f32[4,512,256]{2,1,0:T(8,128)} %copy-done, bf16[4,256,512]{2,1,0:T(8,128)(2,1)S(1)} %pad_maximum_fusion.lag_ref, bf16[4,512,256]{2,1,0:T(8,128)(2,1)S(1)} %pad_maximum_fusion.1.dop_ref), custom_call_target="tpu_custom_call" | custom-call | flops 1610612736 | bytes 6291456 | tf_op jit(solution)/shard_map/powers/pallas_call | solution.py:214
  69.6 7.3 %powers.4 = bf16[4,4,4,32,128]{4,3,2,1,0:T(8,128)(2,1)S(1)} custom-call(bf16[512,256]{1,0:T(8,128)(2,1)S(1)} %copy-done.1, bf16[16,256,128]{2,1,0:T(8,128)(2,1)S(1)} %get-tuple-element.7.s_ref, f32[4,512,256]{2,1,0:T(8,128)} %copy-done, bf16[4,256,512]{2,1,0:T(8,128)(2,1)S(1)} %pad_maximum_fusion.lag_ref, bf16[4,512,256]{2,1,0:T(8,128)(2,1)S(1)} %pad_maximum_fusion.1.dop_ref), custom_call_target="tpu_custom_call" | custom-call | flops 1610612736 | bytes 6291456 | tf_op jit(solution)/shard_map/powers/pallas_call | solution.py:214
  77.0 1.7 %collective-permute-start.12 = (bf16[4,4,32,128]{3,2,1,0:T(8,128)(2,1)S(1)}, bf16[4,4,32,128]{3,2,1,0:T(8,128)(2,1)S(1)}, u32[]{:S(2)}, u32[]{:S(2)}) collective-permute-start(bf16[4,4,32,128]{3,2,1,0:T(8,128)(2,1)S(1)} %get-tuple-element.18), channel_id=1, source_target_pairs={{0,1},{1,2},{2,3},{3,0},{4,5},{5,6},{6,7},{7,4},{8,9},{9,10},{10,1... | collective-permute-start | bytes 393224 | tf_op jit(solution)/shard_map/ppermute | solution.py:268
  78.7 2.2 %collective-permute-start.14 = (bf16[4,4,32,128]{3,2,1,0:T(8,128)(2,1)S(1)}, bf16[4,4,32,128]{3,2,1,0:T(8,128)(2,1)S(1)}, u32[]{:S(2)}, u32[]{:S(2)}) collective-permute-start(bf16[4,4,32,128]{3,2,1,0:T(8,128)(2,1)S(1)} %get-tuple-element.19), channel_id=1, source_target_pairs={{0,3},{1,0},{2,1},{3,2},{4,7},{5,4},{6,5},{7,6},{8,11},{9,8},{10,9... | collective-permute-start | bytes 393224 | tf_op jit(solution)/shard_map/ppermute | solution.py:268
  80.9 0.8 collective-permute-start.13
  81.7 1.6 %collective-permute-start.9 = (bf16[4,4,32,128]{3,2,1,0:T(8,128)(2,1)S(1)}, bf16[4,4,32,128]{3,2,1,0:T(8,128)(2,1)S(1)}, u32[]{:S(2)}, u32[]{:S(2)}) collective-permute-start(bf16[4,4,32,128]{3,2,1,0:T(8,128)(2,1)S(1)} %get-tuple-element.15), channel_id=1, source_target_pairs={{0,1},{1,2},{2,3},{3,0},{4,5},{5,6},{6,7},{7,4},{8,9},{9,10},{10,1... | collective-permute-start | bytes 393224 | tf_op jit(solution)/shard_map/ppermute | solution.py:268
  83.4 2.2 %collective-permute-start.11 = (bf16[4,4,32,128]{3,2,1,0:T(8,128)(2,1)S(1)}, bf16[4,4,32,128]{3,2,1,0:T(8,128)(2,1)S(1)}, u32[]{:S(2)}, u32[]{:S(2)}) collective-permute-start(bf16[4,4,32,128]{3,2,1,0:T(8,128)(2,1)S(1)} %get-tuple-element.16), channel_id=1, source_target_pairs={{0,3},{1,0},{2,1},{3,2},{4,7},{5,4},{6,5},{7,6},{8,11},{9,8},{10,9... | collective-permute-start | bytes 393224 | tf_op jit(solution)/shard_map/ppermute | solution.py:268
  85.7 5.6 %collective-permute-start.10 = (bf16[4,4,32,128]{3,2,1,0:T(8,128)(2,1)S(1)}, bf16[4,4,32,128]{3,2,1,0:T(8,128)(2,1)S(1)}, u32[]{:S(2)}, u32[]{:S(2)}) collective-permute-start(bf16[4,4,32,128]{3,2,1,0:T(8,128)(2,1)S(1)} %get-tuple-element.17), channel_id=1, source_target_pairs={{0,2},{1,3},{2,0},{3,1},{4,6},{5,7},{6,4},{7,5},{8,10},{9,11},{10,... | collective-permute-start | bytes 393224 | tf_op jit(solution)/shard_map/ppermute | solution.py:268
  91.3 1.0 collective-permute-start.3
  92.3 7.9 %collective-permute-done.13 = bf16[4,4,32,128]{3,2,1,0:T(8,128)(2,1)S(1)} collective-permute-done((bf16[4,4,32,128]{3,2,1,0:T(8,128)(2,1)S(1)}, bf16[4,4,32,128]{3,2,1,0:T(8,128)(2,1)S(1)}, u32[]{:S(2)}, u32[]{:S(2)}) %collective-permute-start.13) | collective-permute-done | bytes 131104 | tf_op jit(solution)/shard_map/ppermute | solution.py:268
  100.2 0.4 collective-permute-start.5
  100.7 6.2 %collective-permute-start.4 = (bf16[4,4,32,128]{3,2,1,0:T(8,128)(2,1)S(1)}, bf16[4,4,32,128]{3,2,1,0:T(8,128)(2,1)S(1)}, u32[]{:S(2)}, u32[]{:S(2)}) collective-permute-start(bf16[4,4,32,128]{3,2,1,0:T(8,128)(2,1)S(1)} %get-tuple-element.11), channel_id=1, source_target_pairs={{0,2},{1,3},{2,0},{3,1},{4,6},{5,7},{6,4},{7,5},{8,10},{9,11},{10,... | collective-permute-start | bytes 393224 | tf_op jit(solution)/shard_map/ppermute | solution.py:268
  106.9 1.9 %collective-permute-start.6 = (bf16[4,4,32,128]{3,2,1,0:T(8,128)(2,1)S(1)}, bf16[4,4,32,128]{3,2,1,0:T(8,128)(2,1)S(1)}, u32[]{:S(2)}, u32[]{:S(2)}) collective-permute-start(bf16[4,4,32,128]{3,2,1,0:T(8,128)(2,1)S(1)} %get-tuple-element.12), channel_id=1, source_target_pairs={{0,1},{1,2},{2,3},{3,0},{4,5},{5,6},{6,7},{7,4},{8,9},{9,10},{10,1... | collective-permute-start | bytes 393224 | tf_op jit(solution)/shard_map/ppermute | solution.py:268
  108.8 2.2 %collective-permute-done.10 = bf16[4,4,32,128]{3,2,1,0:T(8,128)(2,1)S(1)} collective-permute-done((bf16[4,4,32,128]{3,2,1,0:T(8,128)(2,1)S(1)}, bf16[4,4,32,128]{3,2,1,0:T(8,128)(2,1)S(1)}, u32[]{:S(2)}, u32[]{:S(2)}) %collective-permute-start.10) | collective-permute-done | bytes 131104 | tf_op jit(solution)/shard_map/ppermute | solution.py:268
  111.1 4.2 %collective-permute-start.7 = (bf16[4,4,32,128]{3,2,1,0:T(8,128)(2,1)S(1)}, bf16[4,4,32,128]{3,2,1,0:T(8,128)(2,1)S(1)}, u32[]{:S(2)}, u32[]{:S(2)}) collective-permute-start(bf16[4,4,32,128]{3,2,1,0:T(8,128)(2,1)S(1)} %get-tuple-element.14), channel_id=1, source_target_pairs={{0,2},{1,3},{2,0},{3,1},{4,6},{5,7},{6,4},{7,5},{8,10},{9,11},{10,... | collective-permute-start | bytes 393224 | tf_op jit(solution)/shard_map/ppermute | solution.py:268
  115.3 5.5 %collective-permute-done.4 = bf16[4,4,32,128]{3,2,1,0:T(8,128)(2,1)S(1)} collective-permute-done((bf16[4,4,32,128]{3,2,1,0:T(8,128)(2,1)S(1)}, bf16[4,4,32,128]{3,2,1,0:T(8,128)(2,1)S(1)}, u32[]{:S(2)}, u32[]{:S(2)}) %collective-permute-start.4) | collective-permute-done | bytes 131104 | tf_op jit(solution)/shard_map/ppermute | solution.py:268
  120.9 4.5 %collective-permute-done.7 = bf16[4,4,32,128]{3,2,1,0:T(8,128)(2,1)S(1)} collective-permute-done((bf16[4,4,32,128]{3,2,1,0:T(8,128)(2,1)S(1)}, bf16[4,4,32,128]{3,2,1,0:T(8,128)(2,1)S(1)}, u32[]{:S(2)}, u32[]{:S(2)}) %collective-permute-start.7) | collective-permute-done | bytes 131104 | tf_op jit(solution)/shard_map/ppermute | solution.py:268
  125.5 1.1 pad_maximum_fusion.2
  (35 shorter events, 0.8 us)
Async XLA Ops:
  2.0 7.9 %copy-start.4 = (s32[4]{0:T(128)S(1)}, s32[4]{0:T(128)}, u32[]{:S(2)}) copy-start(s32[4]{0:T(128)} %param.17) | copy-start | bytes 52
  2.0 13.8 %copy-start.5 = (s32[4]{0:T(128)S(1)}, s32[4]{0:T(128)}, u32[]{:S(2)}) copy-start(s32[4]{0:T(128)} %param.16) | copy-start | bytes 52
  9.4 28.0 %copy-start.3 = (bf16[2,192,512]{2,1,0:T(8,128)(2,1)S(1)}, bf16[2,192,512]{2,1,0:T(8,128)(2,1)}, u32[]{:S(2)}) copy-start(bf16[2,192,512]{2,1,0:T(8,128)(2,1)} %constant.198.clone) | copy-start | bytes 1179652
  9.4 16.5 %collective-permute-start = (bf16[4,256,128]{2,1,0:T(8,128)(2,1)S(1)}, bf16[4,256,128]{2,1,0:T(8,128)(2,1)S(1)}, u32[]{:S(2)}, u32[]{:S(2)}) collective-permute-start(bf16[4,256,128]{2,1,0:T(8,128)(2,1)S(1)} %get-tuple-element.8), channel_id=1, source_target_pairs={{0,4},{4,0},{8,12},{12,8},{16,20},{20,16},{24,28},{28,24},{1,5},{5... | collective-permute-start | bytes 786440 | tf_op jit(solution)/shard_map/ppermute | solution.py:247
  26.0 9.5 %collective-permute-start.1 = (bf16[4,256,128]{2,1,0:T(8,128)(2,1)S(1)}, bf16[4,256,128]{2,1,0:T(8,128)(2,1)S(1)}, u32[]{:S(2)}, u32[]{:S(2)}) collective-permute-start(bf16[4,256,128]{2,1,0:T(8,128)(2,1)S(1)} %add.222), channel_id=1, source_target_pairs={{0,8},{4,12},{8,0},{12,4},{16,24},{20,28},{24,16},{28,20},{1,9},{5... | collective-permute-start | bytes 786440 | tf_op jit(solution)/shard_map/ppermute | solution.py:247
  28.5 15.3 %copy-start.2 = (bf16[512,1024]{1,0:T(8,128)(2,1)S(1)}, bf16[512,1024]{1,0:T(8,128)(2,1)}, u32[]{:S(2)}) copy-start(bf16[512,1024]{1,0:T(8,128)(2,1)} %constant.197.clone.table_ref) | copy-start | bytes 3145732
  35.6 12.2 %copy-start.1 = (bf16[512,256]{1,0:T(8,128)(2,1)S(1)}, bf16[512,256]{1,0:T(8,128)(2,1)}, u32[]{:S(2)}) copy-start(bf16[512,256]{1,0:T(8,128)(2,1)} %constant.199.clone.table_ref) | copy-start | bytes 786436
  35.6 8.2 %collective-permute-start.2 = (bf16[4,256,128]{2,1,0:T(8,128)(2,1)S(1)}, bf16[4,256,128]{2,1,0:T(8,128)(2,1)S(1)}, u32[]{:S(2)}, u32[]{:S(2)}) collective-permute-start(bf16[4,256,128]{2,1,0:T(8,128)(2,1)S(1)} %add.223), channel_id=1, source_target_pairs={{0,16},{4,20},{8,24},{12,28},{16,0},{20,4},{24,8},{28,12},{1,17},{... | collective-permute-start | bytes 786440 | tf_op jit(solution)/shard_map/ppermute | solution.py:247
  46.4 1.3 %copy-start = (f32[4,512,256]{2,1,0:T(8,128)}, f32[4,512,256]{2,1,0:T(8,128)S(1)}, u32[]{:S(2)}) copy-start(f32[4,512,256]{2,1,0:T(8,128)S(1)} %ref_spectra.1.r_ref) | copy-start | bytes 6291460
  77.0 8.7 %collective-permute-start.12 = (bf16[4,4,32,128]{3,2,1,0:T(8,128)(2,1)S(1)}, bf16[4,4,32,128]{3,2,1,0:T(8,128)(2,1)S(1)}, u32[]{:S(2)}, u32[]{:S(2)}) collective-permute-start(bf16[4,4,32,128]{3,2,1,0:T(8,128)(2,1)S(1)} %get-tuple-element.18), channel_id=1, source_target_pairs={{0,1},{1,2},{2,3},{3,0},{4,5},{5,6},{6,7},{7,4},{8,9},{9,10},{10,1... | collective-permute-start | bytes 393224 | tf_op jit(solution)/shard_map/ppermute | solution.py:268
  78.7 12.6 %collective-permute-start.14 = (bf16[4,4,32,128]{3,2,1,0:T(8,128)(2,1)S(1)}, bf16[4,4,32,128]{3,2,1,0:T(8,128)(2,1)S(1)}, u32[]{:S(2)}, u32[]{:S(2)}) collective-permute-start(bf16[4,4,32,128]{3,2,1,0:T(8,128)(2,1)S(1)} %get-tuple-element.19), channel_id=1, source_target_pairs={{0,3},{1,0},{2,1},{3,2},{4,7},{5,4},{6,5},{7,6},{8,11},{9,8},{10,9... | collective-permute-start | bytes 393224 | tf_op jit(solution)/shard_map/ppermute | solution.py:268
  80.9 19.3 %collective-permute-start.13 = (bf16[4,4,32,128]{3,2,1,0:T(8,128)(2,1)S(1)}, bf16[4,4,32,128]{3,2,1,0:T(8,128)(2,1)S(1)}, u32[]{:S(2)}, u32[]{:S(2)}) collective-permute-start(bf16[4,4,32,128]{3,2,1,0:T(8,128)(2,1)S(1)} %get-tuple-element.20), channel_id=1, source_target_pairs={{0,2},{1,3},{2,0},{3,1},{4,6},{5,7},{6,4},{7,5},{8,10},{9,11},{10,... | collective-permute-start | bytes 393224 | tf_op jit(solution)/shard_map/ppermute | solution.py:268
  81.7 19.0 %collective-permute-start.9 = (bf16[4,4,32,128]{3,2,1,0:T(8,128)(2,1)S(1)}, bf16[4,4,32,128]{3,2,1,0:T(8,128)(2,1)S(1)}, u32[]{:S(2)}, u32[]{:S(2)}) collective-permute-start(bf16[4,4,32,128]{3,2,1,0:T(8,128)(2,1)S(1)} %get-tuple-element.15), channel_id=1, source_target_pairs={{0,1},{1,2},{2,3},{3,0},{4,5},{5,6},{6,7},{7,4},{8,9},{9,10},{10,1... | collective-permute-start | bytes 393224 | tf_op jit(solution)/shard_map/ppermute | solution.py:268
  83.4 23.5 %collective-permute-start.11 = (bf16[4,4,32,128]{3,2,1,0:T(8,128)(2,1)S(1)}, bf16[4,4,32,128]{3,2,1,0:T(8,128)(2,1)S(1)}, u32[]{:S(2)}, u32[]{:S(2)}) collective-permute-start(bf16[4,4,32,128]{3,2,1,0:T(8,128)(2,1)S(1)} %get-tuple-element.16), channel_id=1, source_target_pairs={{0,3},{1,0},{2,1},{3,2},{4,7},{5,4},{6,5},{7,6},{8,11},{9,8},{10,9... | collective-permute-start | bytes 393224 | tf_op jit(solution)/shard_map/ppermute | solution.py:268
  85.7 25.3 %collective-permute-start.10 = (bf16[4,4,32,128]{3,2,1,0:T(8,128)(2,1)S(1)}, bf16[4,4,32,128]{3,2,1,0:T(8,128)(2,1)S(1)}, u32[]{:S(2)}, u32[]{:S(2)}) collective-permute-start(bf16[4,4,32,128]{3,2,1,0:T(8,128)(2,1)S(1)} %get-tuple-element.17), channel_id=1, source_target_pairs={{0,2},{1,3},{2,0},{3,1},{4,6},{5,7},{6,4},{7,5},{8,10},{9,11},{10,... | collective-permute-start | bytes 393224 | tf_op jit(solution)/shard_map/ppermute | solution.py:268
  91.3 19.8 %collective-permute-start.3 = (bf16[4,4,32,128]{3,2,1,0:T(8,128)(2,1)S(1)}, bf16[4,4,32,128]{3,2,1,0:T(8,128)(2,1)S(1)}, u32[]{:S(2)}, u32[]{:S(2)}) collective-permute-start(bf16[4,4,32,128]{3,2,1,0:T(8,128)(2,1)S(1)} %get-tuple-element.9), channel_id=1, source_target_pairs={{0,1},{1,2},{2,3},{3,0},{4,5},{5,6},{6,7},{7,4},{8,9},{9,10},{10,1... | collective-permute-start | bytes 393224 | tf_op jit(solution)/shard_map/ppermute | solution.py:268
  100.2 15.1 %collective-permute-start.5 = (bf16[4,4,32,128]{3,2,1,0:T(8,128)(2,1)S(1)}, bf16[4,4,32,128]{3,2,1,0:T(8,128)(2,1)S(1)}, u32[]{:S(2)}, u32[]{:S(2)}) collective-permute-start(bf16[4,4,32,128]{3,2,1,0:T(8,128)(2,1)S(1)} %get-tuple-element.10), channel_id=1, source_target_pairs={{0,3},{1,0},{2,1},{3,2},{4,7},{5,4},{6,5},{7,6},{8,11},{9,8},{10,9... | collective-permute-start | bytes 393224 | tf_op jit(solution)/shard_map/ppermute | solution.py:268
  100.7 20.1 %collective-permute-start.4 = (bf16[4,4,32,128]{3,2,1,0:T(8,128)(2,1)S(1)}, bf16[4,4,32,128]{3,2,1,0:T(8,128)(2,1)S(1)}, u32[]{:S(2)}, u32[]{:S(2)}) collective-permute-start(bf16[4,4,32,128]{3,2,1,0:T(8,128)(2,1)S(1)} %get-tuple-element.11), channel_id=1, source_target_pairs={{0,2},{1,3},{2,0},{3,1},{4,6},{5,7},{6,4},{7,5},{8,10},{9,11},{10,... | collective-permute-start | bytes 393224 | tf_op jit(solution)/shard_map/ppermute | solution.py:268
  106.9 14.0 %collective-permute-start.6 = (bf16[4,4,32,128]{3,2,1,0:T(8,128)(2,1)S(1)}, bf16[4,4,32,128]{3,2,1,0:T(8,128)(2,1)S(1)}, u32[]{:S(2)}, u32[]{:S(2)}) collective-permute-start(bf16[4,4,32,128]{3,2,1,0:T(8,128)(2,1)S(1)} %get-tuple-element.12), channel_id=1, source_target_pairs={{0,1},{1,2},{2,3},{3,0},{4,5},{5,6},{6,7},{7,4},{8,9},{9,10},{10,1... | collective-permute-start | bytes 393224 | tf_op jit(solution)/shard_map/ppermute | solution.py:268
  111.0 9.9 %collective-permute-start.8 = (bf16[4,4,32,128]{3,2,1,0:T(8,128)(2,1)S(1)}, bf16[4,4,32,128]{3,2,1,0:T(8,128)(2,1)S(1)}, u32[]{:S(2)}, u32[]{:S(2)}) collective-permute-start(bf16[4,4,32,128]{3,2,1,0:T(8,128)(2,1)S(1)} %get-tuple-element.13), channel_id=1, source_target_pairs={{0,3},{1,0},{2,1},{3,2},{4,7},{5,4},{6,5},{7,6},{8,11},{9,8},{10,9... | collective-permute-start | bytes 393224 | tf_op jit(solution)/shard_map/ppermute | solution.py:268
  111.1 14.3 %collective-permute-start.7 = (bf16[4,4,32,128]{3,2,1,0:T(8,128)(2,1)S(1)}, bf16[4,4,32,128]{3,2,1,0:T(8,128)(2,1)S(1)}, u32[]{:S(2)}, u32[]{:S(2)}) collective-permute-start(bf16[4,4,32,128]{3,2,1,0:T(8,128)(2,1)S(1)} %get-tuple-element.14), channel_id=1, source_target_pairs={{0,2},{1,3},{2,0},{3,1},{4,6},{5,7},{6,4},{7,5},{8,10},{9,11},{10,... | collective-permute-start | bytes 393224 | tf_op jit(solution)/shard_map/ppermute | solution.py:268
where the time goes:
time: 127 us
  Pallas kernels  39 us (31%)
  starting transfers between devices  32.8 us (26%)
  waiting for transfers between devices  32.8 us (26%)
  other arithmetic  10.8 us (9%)
  between operations  8.04 us (6%)
  local copies, waits for them, and re-layouts  3.07 us (2%)
    pallas_call x4, Pallas kernels, powers(): pl.pallas_call(functools.partial(power_kernel, chunks), grid=(count,), in...  29.1 us
    ppermute x12, starting transfers between devices, shards(): lax.ppermute(send, 'seg', [(i, (i + turn) % n_seg) for i in range(n_seg)])  27.9 us
    ppermute x12, waiting for transfers between devices, shards(): lax.ppermute(send, 'seg', [(i, (i + turn) % n_seg) for i in range(n_seg)])  20.1 us
    ppermute x3, waiting for transfers between devices, shards(): ref = ref + lax.ppermute(ref, 'beam', [(i, i ^ hop) for i in range(n_beam)])  12.7 us
    pallas_call x1, Pallas kernels, decimate(): pl.pallas_call(functools.partial(decimate_kernel, beams, rows), grid=(ste...  7.35 us
    ppermute x3, starting transfers between devices, shards(): ref = ref + lax.ppermute(ref, 'beam', [(i, i ^ hop) for i in range(n_beam)])  4.92 us
    sub x4, other arithmetic, doppler_tables(): freqs = f_lo + jnp.arange(DOPPLER, dtype=jnp.int32) - BLOCKS // 2  2.57 us
    pallas_call x1, Pallas kernels, ref_spectra(): pl.pallas_call(spectra_kernel, grid=(TX,), in_specs=[pl.BlockSpec(memory_...  2.56 us
  transfers between devices with their start and end apart: 15, of which 6 were waited for; matrix products, arithmetic and copies ran while one was open for 7% of the time, Pallas kernels for 0%

commit v1 on v0

v1 whole, which is shorter than its diff:
```python
import functools

import jax
import jax.numpy as jnp
import ml_dtypes
import numpy as np
from jax import lax
from jax.experimental import pallas as pl
from jax.experimental.pallas import tpu as pltpu
from jax.sharding import PartitionSpec as P

TX = 4
HALF_TX = TX // 2
DECIM = 4
TAPS = 32
BLOCK_LEN = 64
BLOCKS = 256
DELAYS = 128
DOPPLER = 128
FFT = 256
STRIDE = DECIM * BLOCK_LEN
LEAD = 128
REACH = LEAD + STRIDE
PAIR = 2 * BLOCK_LEN
GROUPS = 4
LANES = 128
LANE_BLOCKS = 2 * FFT // LANES
HALF_DELAYS = DELAYS // 2
VMEM_LIMIT = 24 * 1024 * 1024

SMEM = pl.BlockSpec(memory_space=pltpu.SMEM)
VMEM = pl.BlockSpec(memory_space=pltpu.VMEM)


def split_bf16(table):
    hi = table.astype(ml_dtypes.bfloat16)
    lo = (table - hi.astype(np.float64)).astype(ml_dtypes.bfloat16)
    return hi, lo


def fourier(samples):
    angle = 2 * np.pi / FFT * (np.outer(np.arange(FFT), samples) % FFT)
    cos, sin = np.cos(angle), np.sin(angle)
    return np.block([[cos, sin], [-sin, cos]])


def surv_fourier():
    hi, lo = split_bf16(fourier(np.arange(BLOCK_LEN)))
    return np.concatenate([hi, lo], axis=1)


def ref_fourier():
    parts = [fourier(np.arange(BLOCK_LEN) + BLOCK_LEN * e) for e in range(4)]
    hi, lo = split_bf16(np.concatenate(parts, axis=1))
    return np.concatenate([hi, lo], axis=1)


def in_lane_blocks(both):
    parts, rows, _ = both.shape
    return both.astype(np.float32).reshape(parts, rows, LANE_BLOCKS, LANES).swapaxes(1, 2)


def lag_table():
    lags = 191 - np.arange(192)
    angle = 2 * np.pi / FFT * (np.outer(lags, np.arange(FFT)) % FFT)
    cos, sin = np.cos(angle), np.sin(angle)
    scale = 1.0 / (FFT * np.sqrt(BLOCK_LEN))
    both = np.stack([np.concatenate([cos, sin], 1), np.concatenate([-sin, cos], 1)])
    both = both.astype(ml_dtypes.bfloat16).astype(np.float64) * scale
    return in_lane_blocks(both)


def doppler_table():
    freqs = np.arange(BLOCKS) - BLOCKS // 2
    angle = 2 * np.pi / BLOCKS * (np.outer(freqs, np.arange(BLOCKS)) % BLOCKS)
    cos, sin = np.cos(angle), np.sin(angle)
    both = np.stack([np.concatenate([cos, sin], 1), np.concatenate([-sin, cos], 1)])
    return in_lane_blocks(both.astype(ml_dtypes.bfloat16))


def nt_dot(left, right):
    return lax.dot_general(
        left, right, (((1,), (1,)), ((), ())), preferred_element_type=jnp.float32
    )


def dot(left, right):
    return jnp.dot(left, right, preferred_element_type=jnp.float32)


def decimate_kernel(beams, rows, ids, owner, staps, rtaps, prev_ref, x_ref, *refs):
    s_refs, (keep_ref, send_ref, band, all_s, all_r) = refs[:GROUPS], refs[GROUPS:]
    step = pl.program_id(0)

    @pl.when(step == 0)
    def _():
        shape = (REACH, PAIR)
        q = lax.broadcasted_iota(jnp.int32, shape, 0)
        lane = lax.broadcasted_iota(jnp.int32, shape, 1)
        tap = LEAD + DECIM * (lane % BLOCK_LEN) - q
        first = lane < BLOCK_LEN
        one, two = staps[...].astype(jnp.float32), rtaps[...].astype(jnp.float32)
        both = jnp.zeros(shape, jnp.float32)
        for t in range(TAPS):
            row = jnp.where(first[:1], one[:, t : t + 1], two[:, t : t + 1])
            both = jnp.where(tap == t, row, both)
        turned = pltpu.roll(both, BLOCK_LEN, 1)
        zero = jnp.zeros(shape, jnp.float32)
        band[:REACH, :PAIR] = jnp.where(first, both, zero).astype(jnp.bfloat16)
        band[REACH:, :PAIR] = jnp.where(first, zero, turned).astype(jnp.bfloat16)
        band[:REACH, PAIR:] = jnp.where(first, turned, zero).astype(jnp.bfloat16)
        band[REACH:, PAIR:] = jnp.where(first, zero, both).astype(jnp.bfloat16)

    prev = prev_ref[...] * (step > 0).astype(jnp.bfloat16)
    x = jnp.concatenate([prev, x_ref[...]], axis=2)
    parts = []
    for c in range(2):
        parts.append(
            jnp.concatenate([x[c, :, l * STRIDE : l * STRIDE + REACH] for l in range(rows)], axis=0)
        )
    out = dot(jnp.concatenate(parts, axis=1), band[...])
    all_s[...] = out[:, :PAIR]
    all_r[...] = out[:, PAIR:]
    count = beams // GROUPS
    for b in range(beams):
        picked = all_s[pl.ds(b, rows, stride=beams), :]
        s_refs[b // count][b % count] = picked.astype(jnp.bfloat16)
    core = ids[0] % 2
    for ref, first_tx in ((keep_ref, core * HALF_TX), (send_ref, (1 - core) * HALF_TX)):
        for k in range(HALF_TX):
            beam = owner[first_tx + k]
            picked = all_r[pl.ds(beam % beams, rows, stride=beams), :]
            ref[k] = jnp.where(beam // beams == ids[0], picked, 0.0).astype(jnp.bfloat16)


def decimate(volts, staps, rtaps, ids, owner):
    beams, raw = volts.shape[1:]
    rows = 64
    wide = rows * STRIDE
    blocks = raw // STRIDE
    count = beams // GROUPS
    block = lambda n: pl.BlockSpec((n, rows, PAIR), lambda i: (0, i, 0))
    shape = lambda n: jax.ShapeDtypeStruct((n, blocks, PAIR), jnp.bfloat16)
    return pl.pallas_call(
        functools.partial(decimate_kernel, beams, rows),
        grid=(raw // wide,),
        in_specs=[
            SMEM,
            SMEM,
            pl.BlockSpec((1, TAPS), lambda i: (0, 0)),
            pl.BlockSpec((1, TAPS), lambda i: (0, 0)),
            pl.BlockSpec(
                (2, beams, LEAD), lambda i: (0, 0, jnp.maximum(i * (wide // LEAD) - 1, 0))
            ),
            pl.BlockSpec((2, beams, wide), lambda i: (0, 0, i)),
        ],
        out_specs=[block(count)] * GROUPS + [block(HALF_TX)] * 2,
        out_shape=[shape(count)] * GROUPS + [shape(HALF_TX)] * 2,
        scratch_shapes=[
            pltpu.VMEM((2 * REACH, 2 * PAIR), jnp.bfloat16),
            pltpu.VMEM((rows * beams, PAIR), jnp.float32),
            pltpu.VMEM((rows * beams, PAIR), jnp.float32),
        ],
        compiler_params=pltpu.CompilerParams(vmem_limit_bytes=VMEM_LIMIT),
        name="decimate",
    )(ids, owner, staps, rtaps, volts, volts)


def tables_kernel(chunks, ids, delay, doppler, lag_ref, dop_ref, lags, dops):
    each = DELAYS // chunks
    for k in range(TX):
        base = (delay[k] + DELAYS - 1) % BLOCK_LEN
        for part in range(2):
            for n in range(chunks // 2):
                chunk = ids[1] ^ (2 * n)
                at = part * HALF_DELAYS + n * each
                for q in range(LANE_BLOCKS):
                    picked = lag_ref[part, q, pl.ds(base + chunk * each, each), :]
                    lags[k, at : at + each, q * LANES : (q + 1) * LANES] = picked.astype(jnp.bfloat16)
            for q in range(LANE_BLOCKS):
                picked = dop_ref[part, q, pl.ds(doppler[k], DOPPLER), :].T.astype(jnp.bfloat16)
                dops[k, q * LANES : (q + 1) * LANES, part * DOPPLER : (part + 1) * DOPPLER] = picked


def make_tables(ids, delay, doppler, chunks):
    return pl.pallas_call(
        functools.partial(tables_kernel, chunks),
        in_specs=[SMEM, SMEM, SMEM, VMEM, VMEM],
        out_specs=[VMEM, VMEM],
        out_shape=[
            jax.ShapeDtypeStruct((TX, DELAYS, 2 * FFT), jnp.bfloat16),
            jax.ShapeDtypeStruct((TX, 2 * BLOCKS, 2 * DOPPLER), jnp.bfloat16),
        ],
        compiler_params=pltpu.CompilerParams(vmem_limit_bytes=VMEM_LIMIT),
        name="tables",
    )(ids, delay, doppler, jnp.asarray(lag_table()), jnp.asarray(doppler_table()))


PAD = 8


def spectra_kernel(ids, delay, table_ref, mine_ref, other_ref, out_ref, padded):
    core = ids[0] % 2
    padded[:PAD] = jnp.zeros((PAD, PAIR), jnp.float32)
    padded[PAD + BLOCKS :] = jnp.zeros((PAD, PAIR), jnp.float32)
    for k in range(TX):
        here = core == k // HALF_TX
        ref = jnp.where(here, mine_ref[k % HALF_TX], other_ref[k % HALF_TX])
        padded[PAD : PAD + BLOCKS] = ref.astype(jnp.float32)
        start = PAD - 1 - (delay[k] + DELAYS - 1) // BLOCK_LEN
        window = jnp.concatenate(
            [padded[pl.ds(start + e, BLOCKS), :].astype(jnp.bfloat16) for e in range(4)], axis=1
        )
        out_ref[k] = nt_dot(table_ref[...], jnp.concatenate([window, window], axis=1))


def ref_spectra(ids, delay, mine, other):
    return pl.pallas_call(
        spectra_kernel,
        in_specs=[SMEM, SMEM, VMEM, VMEM, VMEM],
        out_specs=VMEM,
        out_shape=jax.ShapeDtypeStruct((TX, 2 * FFT, BLOCKS), jnp.float32),
        scratch_shapes=[pltpu.VMEM((BLOCKS + 2 * PAD, PAIR), jnp.float32)],
        compiler_params=pltpu.CompilerParams(vmem_limit_bytes=VMEM_LIMIT),
        name="ref_spectra",
    )(ids, delay, jnp.asarray(ref_fourier()), mine, other)


def power_kernel(
    chunks, table_ref, here_ref, there_ref, r_here, r_there, lag_ref, dop_ref, own_ref, send_ref, spec, prods, corrs
):
    count = here_ref.shape[0]
    each = DELAYS // chunks
    for n, ref in enumerate((here_ref, there_ref)):
        s = ref[...].reshape(count * BLOCKS, PAIR)
        spec[n] = nt_dot(table_ref[...], jnp.concatenate([s, s], axis=1))
    for k in range(TX):
        for n, r_ref in enumerate((r_here, r_there)):
            r_re, r_im = r_ref[k, :FFT], r_ref[k, FFT:]
            prod, corr = prods.at[n], corrs.at[k % 2]
            for b in range(count):
                cols = slice(b * BLOCKS, (b + 1) * BLOCKS)
                s_re, s_im = spec[n, :FFT, cols], spec[n, FFT:, cols]
                prod[:FFT, cols] = (s_re * r_re + s_im * r_im).astype(jnp.bfloat16)
                prod[FFT:, cols] = (s_im * r_re - s_re * r_im).astype(jnp.bfloat16)
            out = dot(lag_ref[k], prod[...]).astype(jnp.bfloat16)
            for b in range(count):
                cols = slice(b * BLOCKS, (b + 1) * BLOCKS)
                rows = slice((n * count + b) * HALF_DELAYS, (n * count + b + 1) * HALF_DELAYS)
                corr[rows, :BLOCKS] = out[:HALF_DELAYS, cols]
                corr[rows, BLOCKS:] = out[HALF_DELAYS:, cols]
        x = dot(corrs[k % 2], dop_ref[k])
        x_re, x_im = x[:, :DOPPLER], x[:, DOPPLER:]
        power = (x_re * x_re + x_im * x_im) * (1.0 / (4 * BLOCKS))
        power = power[: count * HALF_DELAYS] + power[count * HALF_DELAYS :]
        power = power.reshape(count, HALF_DELAYS, DOPPLER)
        own_ref[k] = power[:, :each]
        for n in range(1, chunks // 2):
            send_ref[n - 1, k] = power[:, n * each : (n + 1) * each].astype(jnp.bfloat16)


def powers(here, there, r_here, r_there, lags, dops, chunks):
    count = here.shape[0]
    each = DELAYS // chunks
    return pl.pallas_call(
        functools.partial(power_kernel, chunks),
        in_specs=[VMEM] * 7,
        out_specs=[VMEM] * 2,
        out_shape=[
            jax.ShapeDtypeStruct((TX, count, each, DOPPLER), jnp.float32),
            jax.ShapeDtypeStruct((chunks // 2 - 1, TX, count, each, DOPPLER), jnp.bfloat16),
        ],
        scratch_shapes=[
            pltpu.VMEM((2, 2 * FFT, count * BLOCKS), jnp.float32),
            pltpu.VMEM((2, 2 * FFT, count * BLOCKS), jnp.bfloat16),
            pltpu.VMEM((2, 2 * count * HALF_DELAYS, 2 * BLOCKS), jnp.bfloat16),
        ],
        compiler_params=pltpu.CompilerParams(vmem_limit_bytes=VMEM_LIMIT),
        cost_estimate=pl.CostEstimate(
            flops=2 * count * TX * 4 * 768 * 65536, bytes_accessed=6 << 20, transcendentals=0
        ),
        name="powers",
    )(jnp.asarray(surv_fourier()), here, there, r_here, r_there, lags, dops)


def swap(value, axis, flip):
    size = lax.axis_size(axis)
    return lax.ppermute(value, axis, [(i, i ^ flip) for i in range(size)])


def shards(voltages, surv_taps, ref_taps, tx_owner, delay_start, doppler_start):
    beams_here = voltages.shape[1]
    n_beam = lax.axis_size("beam")
    n_seg = lax.axis_size("seg")
    segments_all = n_seg * voltages.shape[2]
    ids = jnp.stack([lax.axis_index("beam"), lax.axis_index("seg")]).astype(jnp.int32)
    volts = voltages.reshape(2, beams_here, voltages.shape[3])
    out = decimate(volts, surv_taps.reshape(1, TAPS), ref_taps.reshape(1, TAPS), ids, tx_owner)
    surv, (keep, send) = out[:GROUPS], out[GROUPS:]
    half = keep + swap(send, "beam", 1)
    half, surv, ids = lax.optimization_barrier((half, surv, ids))
    got = [swap(half, "beam", flip) for flip in range(2, n_beam, 2)]
    there = [swap(s, "seg", 1) for s in surv]
    lags, dops = make_tables(ids, delay_start, doppler_start, n_seg)
    half = functools.reduce(jnp.add, got, half)
    far = swap(half, "seg", 1)
    r_here = ref_spectra(ids, delay_start, half, swap(half, "beam", 1))
    r_there = ref_spectra(ids, delay_start, far, swap(far, "beam", 1))
    maps = []
    for g in range(GROUPS):
        total, outgoing = powers(surv[g], there[g], r_here, r_there, lags, dops, n_seg)
        for n in range(1, n_seg // 2):
            total = total + swap(outgoing[n - 1], "seg", 2 * n).astype(jnp.float32)
        maps.append(total / segments_all)
    return jnp.concatenate(maps, axis=1)


def solution(mesh):
    return jax.shard_map(
        shards,
        mesh=mesh,
        in_specs=(P(None, "beam", "seg", None), P(), P(), P(), P(), P()),
        out_specs=P(None, "beam", "seg", None),
        check_vma=False,
    )
```

time: 127 us -> 71.1 us (0.56)
  starting transfers between devices: 32.8 us -> 17 us
  Pallas kernels: 39 us -> 26.8 us
  waiting for transfers between devices: 32.8 us -> 21.6 us
  other arithmetic: 10.8 us -> 1.31 us
  between operations: 8.04 us -> 0.14 us
    ppermute x15, starting transfers between devices: 32.8 us -> 17 us  [swap(): return lax.ppermute(value, axis, [(i, i ^ flip) for i in range(size)])]
    pallas_call x6 -> x8, Pallas kernels: 39 us -> 26.8 us  [the longest x4 17.5 us: powers(): pl.pallas_call(functools.partial(power_kernel, chunks), in_specs=[VMEM] *...]
    ppermute x15, waiting for transfers between devices: 32.8 us -> 21.6 us  [swap(): return lax.ppermute(value, axis, [(i, i ^ flip) for i in range(size)])]
    convert_element_type x6 -> x0, other arithmetic: 3.51 us -> none  [the longest x4 2.16 us: doppler_tables(): sin = jnp.sin(angle).astype(jnp.bfloat16)]
    unnamed x12 -> x20, local copies, waits for them, and re-layouts: 1.37 us -> 4.18 us
    sub x4 -> x0, other arithmetic: 2.57 us -> none  [doppler_tables(): freqs = f_lo + jnp.arange(DOPPLER, dtype=jnp.int32) - BLOCKS // 2]
    neg x4 -> x0, other arithmetic: 2.04 us -> none  [doppler_tables(): -sin]
    slice x2 -> x0, local copies, waits for them, and re-layouts: 1.31 us -> none  [the longest x1 0.66 us: shards(): lead[k] % BLOCK_LEN]
  transfers between devices with their start and end apart: 15 -> 15, of which waited for: 6 -> 7; matrix products, arithmetic and copies ran while one was open for 7% -> 0% of each run, Pallas kernels for 0% -> 31%
where the time goes in v1:
time: 71.1 us; the launch traced here: 71 us
  Pallas kernels  26.8 us (38%)
  waiting for transfers between devices  21.6 us (30%)
  starting transfers between devices  17 us (24%)
  local copies, waits for them, and re-layouts  4.18 us (6%)
  other arithmetic  1.31 us (2%)
    ppermute x15, waiting for transfers between devices, swap(): return lax.ppermute(value, axis, [(i, i ^ flip) for i in range(size)])  21.6 us
    pallas_call x4, Pallas kernels, powers(): pl.pallas_call(functools.partial(power_kernel, chunks), in_specs=[VMEM] *...  17.5 us
    ppermute x15, starting transfers between devices, swap(): return lax.ppermute(value, axis, [(i, i ^ flip) for i in range(size)])  17 us
    pallas_call x1, Pallas kernels, decimate(): pl.pallas_call(functools.partial(decimate_kernel, beams, rows), grid=(raw...  4.53 us
    unnamed x20, local copies, waits for them, and re-layouts  4.18 us
    pallas_call x2, Pallas kernels, ref_spectra(): pl.pallas_call(spectra_kernel, in_specs=[SMEM, SMEM, VMEM, VMEM, VMEM], o...  3.85 us
  transfers between devices with their start and end apart: 15, of which 7 were waited for; matrix products, arithmetic and copies ran while one was open for 0% of the time, Pallas kernels for 31%

profile of v1, /device:TPU:0, one launch (start us, length us, event | category | flops | bytes accessed | tf_op | source)
XLA Modules:
  0.0 71.0 jit_solution(8419339918702849315)
XLA Ops:
  0.0 0.1 pad_add_fusion.ids
  0.1 2.2 %copy-done = bf16[2,16,1,65536]{3,1,2,0:T(8,128)(2,1)S(1)} copy-done((bf16[2,16,1,65536]{3,1,2,0:T(8,128)(2,1)S(1)}, bf16[2,16,1,65536]{3,1,2,0:T(8,128)(2,1)}, u32[]{:S(2)}) %copy-start) | copy-done | bytes 4194328
  2.3 0.7 copy-done.5
  2.9 0.7 copy-done.6
  3.6 0.7 copy-done.7
  4.2 4.5 %decimate.1 = (bf16[4,256,128]{2,1,0:T(8,128)(2,1)S(1)}, bf16[4,256,128]{2,1,0:T(8,128)(2,1)S(1)}, bf16[4,256,128]{2,1,0:T(8,128)(2,1)S(1)}, bf16[4,256,128]{2,1...) custom-call(s32[2]{0:T(128)S(1)} %pad_add_fusion.ids, s32[4]{0:T(128)S(1)} %copy-done.5, ...), custom_call_target="tpu_custom_call" | custom-call | tf_op jit(solution)/shard_map/decimate/pallas_call | solution.py:144
  8.8 0.0 copy-start.1
  8.8 0.5 collective-permute-start
  9.3 1.0 %collective-permute-done = bf16[2,256,128]{2,1,0:T(8,128)(2,1)S(1)} collective-permute-done((bf16[2,256,128]{2,1,0:T(8,128)(2,1)S(1)}, bf16[2,256,128]{2,1,0:T(8,128)(2,1)S(1)}, u32[]{:S(2)}, u32[]{:S(2)}) %collective-permute-start) | collective-permute-done | bytes 131104 | tf_op jit(solution)/shard_map/ppermute | solution.py:288
  10.4 2.9 %collective-permute-start.2 = (bf16[2,256,128]{2,1,0:T(8,128)(2,1)S(1)}, bf16[2,256,128]{2,1,0:T(8,128)(2,1)S(1)}, u32[]{:S(2)}, u32[]{:S(2)}) collective-permute-start(bf16[2,256,128]{2,1,0:T(8,128)(2,1)S(1)} %add.24), channel_id=1, source_target_pairs={{0,8},{4,12},{8,0},{12,4},{16,24},{20,28},{24,16},{28,20},{1,9},{5... | collective-permute-start | bytes 393224 | tf_op jit(solution)/shard_map/ppermute | solution.py:288
  13.3 1.5 %collective-permute-start.3 = (bf16[2,256,128]{2,1,0:T(8,128)(2,1)S(1)}, bf16[2,256,128]{2,1,0:T(8,128)(2,1)S(1)}, u32[]{:S(2)}, u32[]{:S(2)}) collective-permute-start(bf16[2,256,128]{2,1,0:T(8,128)(2,1)S(1)} %add.24), channel_id=1, source_target_pairs={{0,16},{4,20},{8,24},{12,28},{16,0},{20,4},{24,8},{28,12},{1,17},{... | collective-permute-start | bytes 393224 | tf_op jit(solution)/shard_map/ppermute | solution.py:288
  14.8 0.0 collective-permute-start.4
  14.8 2.4 %collective-permute-done.2 = bf16[2,256,128]{2,1,0:T(8,128)(2,1)S(1)} collective-permute-done((bf16[2,256,128]{2,1,0:T(8,128)(2,1)S(1)}, bf16[2,256,128]{2,1,0:T(8,128)(2,1)S(1)}, u32[]{:S(2)}, u32[]{:S(2)}) %collective-permute-start.2) | collective-permute-done | bytes 131104 | tf_op jit(solution)/shard_map/ppermute | solution.py:288
  17.2 4.2 %collective-permute-done.3 = bf16[2,256,128]{2,1,0:T(8,128)(2,1)S(1)} collective-permute-done((bf16[2,256,128]{2,1,0:T(8,128)(2,1)S(1)}, bf16[2,256,128]{2,1,0:T(8,128)(2,1)S(1)}, u32[]{:S(2)}, u32[]{:S(2)}) %collective-permute-start.3) | collective-permute-done | bytes 131104 | tf_op jit(solution)/shard_map/ppermute | solution.py:288
  21.3 0.0 collective-permute-done.4
  21.4 1.6 %collective-permute-start.6 = (bf16[2,256,128]{2,1,0:T(8,128)(2,1)S(1)}, bf16[2,256,128]{2,1,0:T(8,128)(2,1)S(1)}, u32[]{:S(2)}, u32[]{:S(2)}) collective-permute-start(bf16[2,256,128]{2,1,0:T(8,128)(2,1)S(1)} %add_add_fusion.mine_ref), channel_id=1, source_target_pairs={{0,1},{1,0},{2,3},{3,2},{4,5},{5,4},{6,7},{7,6},{8,9},{9,8},{10,11... | collective-permute-start | bytes 393224 | tf_op jit(solution)/shard_map/ppermute | solution.py:288
  23.0 0.5 collective-permute-start.1
  23.5 0.0 collective-permute-start.5
  23.5 4.4 %collective-permute-done.6.mine_ref = bf16[2,256,128]{2,1,0:T(8,128)(2,1)S(1)} collective-permute-done((bf16[2,256,128]{2,1,0:T(8,128)(2,1)S(1)}, bf16[2,256,128]{2,1,0:T(8,128)(2,1)S(1)}, u32[]{:S(2)}, u32[]{:S(2)}) %collective-permute-start.6) | collective-permute-done | bytes 131104 | tf_op jit(solution)/shard_map/ppermute | solution.py:288
  27.9 0.0 collective-permute-start.7
  27.9 1.6 %collective-permute-start.9 = (bf16[4,256,128]{2,1,0:T(8,128)(2,1)S(1)}, bf16[4,256,128]{2,1,0:T(8,128)(2,1)S(1)}, u32[]{:S(2)}, u32[]{:S(2)}) collective-permute-start(bf16[4,256,128]{2,1,0:T(8,128)(2,1)S(1)} %get-tuple-element.40.here_ref), channel_id=1, source_target_pairs={{0,1},{1,0},{2,3},{3,2},{4,5},{5,4},{6,7},{7,6},{8,9},{9,8},{10,11... | collective-permute-start | bytes 786440 | tf_op jit(solution)/shard_map/ppermute | solution.py:288
  29.5 0.5 collective-permute-start.11
  29.9 0.0 copy-done.8
  29.9 0.9 %tables.1 = (bf16[4,128,512]{2,1,0:T(8,128)(2,1)S(1)}, bf16[4,512,256]{2,1,0:T(8,128)(2,1)S(1)}) custom-call(s32[2]{0:T(128)S(1)} %pad_add_fusion.ids, s32[4]{0:T(128)S(1)} %copy-done.4, s32[4]{0:T(128)S(1)} %copy-done.8, f32[2,4,192,128]{3,2,1,0:T(8,128)S(1)} %copy-done.3, f32[2,4,256,128]{3,2,1,0:T(8,128)S(1)} %copy-done.2), custom_call_target="tpu_custom_call" | custom-call | tf_op jit(solution)/shard_map/tables/pallas_call | solution.py:186
  30.9 0.0 collective-permute-done.5.other_ref
  30.9 1.6 %collective-permute-start.13 = (bf16[4,256,128]{2,1,0:T(8,128)(2,1)S(1)}, bf16[4,256,128]{2,1,0:T(8,128)(2,1)S(1)}, u32[]{:S(2)}, u32[]{:S(2)}) collective-permute-start(bf16[4,256,128]{2,1,0:T(8,128)(2,1)S(1)} %get-tuple-element.46.here_ref), channel_id=1, source_target_pairs={{0,1},{1,0},{2,3},{3,2},{4,5},{5,4},{6,7},{7,6},{8,9},{9,8},{10,11... | collective-permute-start | bytes 786440 | tf_op jit(solution)/shard_map/ppermute | solution.py:288
  32.5 0.0 copy-done.1
  32.5 1.9 %ref_spectra.2.r_here = f32[4,512,256]{2,1,0:T(8,128)S(1)} custom-call(s32[2]{0:T(128)S(1)} %pad_add_fusion.ids, s32[4]{0:T(128)S(1)} %copy-done.4, bf16[512,1024]{1,0:T(8,128)(2,1)S(1)} %copy-done.1, bf16[2,256,128]{2,1,0:T(8,128)(2,1)S(1)} %add_add_fusion.mine_ref, bf16[2,256,128]{2,1,0:T(8,128)(2,1)S(1)} %collective-permute-done.5.other_ref), custom_call_target="tpu_custom_call" | custom-call | tf_op jit(solution)/shard_map/ref_spectra/pallas_call | solution.py:218
  34.4 0.0 copy-start.9
  34.4 0.0 collective-permute-done.7.other_ref
  34.5 1.9 %ref_spectra.3.r_there = f32[4,512,256]{2,1,0:T(8,128)S(1)} custom-call(s32[2]{0:T(128)S(1)} %pad_add_fusion.ids, s32[4]{0:T(128)S(1)} %copy-done.4, bf16[512,1024]{1,0:T(8,128)(2,1)S(1)} %copy-done.1, bf16[2,256,128]{2,1,0:T(8,128)(2,1)S(1)} %collective-permute-done.6.mine_ref, bf16[2,256,128]{2,1,0:T(8,128)(2,1)S(1)} %collective-permute-done.7.other_ref), custom_call_target="tpu_custom_call" | custom-call | tf_op jit(solution)/shard_map/ref_spectra/pallas_call | solution.py:218
  36.4 0.0 collective-permute-done.1.there_ref
  36.4 4.4 %powers.4 = (f32[4,4,32,128]{3,2,1,0:T(8,128)S(1)}, bf16[1,4,4,32,128]{4,3,2,1,0:T(8,128)(2,1)S(1)}) custom-call(bf16[512,256]{1,0:T(8,128)(2,1)S(1)} %copy-done.9, bf16[4,256,128]{2,1,0:T(8,128)(2,1)S(1)} %get-tuple-element.33.here_ref, bf16[4,256,128]{2,1,0:T(8,128)(2,1)S(1)} %collective-permute-done.1.there_ref, f32[4,512,256]{2,1,0:T(8,128)S(1)} %ref_spectra.2.r_here, ...), custom_call_target="tpu_custom_call" | custom-call | flops 6442450944 | bytes 6291456 | tf_op jit(solution)/shard_map/powers/pallas_call | solution.py:265
  40.8 2.7 %collective-permute-start.8 = (bf16[4,4,32,128]{3,2,1,0:T(8,128)(2,1)S(1)}, bf16[4,4,32,128]{3,2,1,0:T(8,128)(2,1)S(1)}, u32[]{:S(2)}, u32[]{:S(2)}) collective-permute-start(bf16[4,4,32,128]{3,2,1,0:T(8,128)(2,1)S(1)} %bitcast.13), channel_id=1, source_target_pairs={{0,2},{1,3},{2,0},{3,1},{4,6},{5,7},{6,4},{7,5},{8,10},{9,11},{10,... | collective-permute-start | bytes 393224 | tf_op jit(solution)/shard_map/ppermute | solution.py:288
  43.4 0.0 collective-permute-done.9.there_ref
  43.5 4.4 %powers.5 = (f32[4,4,32,128]{3,2,1,0:T(8,128)S(1)}, bf16[1,4,4,32,128]{4,3,2,1,0:T(8,128)(2,1)S(1)}) custom-call(bf16[512,256]{1,0:T(8,128)(2,1)S(1)} %copy-done.9, bf16[4,256,128]{2,1,0:T(8,128)(2,1)S(1)} %get-tuple-element.40.here_ref, bf16[4,256,128]{2,1,0:T(8,128)(2,1)S(1)} %collective-permute-done.9.there_ref, f32[4,512,256]{2,1,0:T(8,128)S(1)} %ref_spectra.2.r_here, ...), custom_call_target="tpu_custom_call" | custom-call | flops 6442450944 | bytes 6291456 | tf_op jit(solution)/shard_map/powers/pallas_call | solution.py:265
  47.8 0.6 collective-permute-start.10
  48.4 0.0 collective-permute-done.11.there_ref
  48.4 4.4 %powers.6 = (f32[4,4,32,128]{3,2,1,0:T(8,128)S(1)}, bf16[1,4,4,32,128]{4,3,2,1,0:T(8,128)(2,1)S(1)}) custom-call(bf16[512,256]{1,0:T(8,128)(2,1)S(1)} %copy-done.9, bf16[4,256,128]{2,1,0:T(8,128)(2,1)S(1)} %get-tuple-element.43.here_ref, bf16[4,256,128]{2,1,0:T(8,128)(2,1)S(1)} %collective-permute-done.11.there_ref, f32[4,512,256]{2,1,0:T(8,128)S(1)} %ref_spectra.2.r_here, ...), custom_call_target="tpu_custom_call" | custom-call | flops 6442450944 | bytes 6291456 | tf_op jit(solution)/shard_map/powers/pallas_call | solution.py:265
  52.8 2.7 %collective-permute-start.12 = (bf16[4,4,32,128]{3,2,1,0:T(8,128)(2,1)S(1)}, bf16[4,4,32,128]{3,2,1,0:T(8,128)(2,1)S(1)}, u32[]{:S(2)}, u32[]{:S(2)}) collective-permute-start(bf16[4,4,32,128]{3,2,1,0:T(8,128)(2,1)S(1)} %bitcast.15), channel_id=1, source_target_pairs={{0,2},{1,3},{2,0},{3,1},{4,6},{5,7},{6,4},{7,5},{8,10},{9,11},{10,... | collective-permute-start | bytes 393224 | tf_op jit(solution)/shard_map/ppermute | solution.py:288
  55.4 0.0 collective-permute-done.13.there_ref
  55.4 4.4 %powers.7 = (f32[4,4,32,128]{3,2,1,0:T(8,128)S(1)}, bf16[1,4,4,32,128]{4,3,2,1,0:T(8,128)(2,1)S(1)}) custom-call(bf16[512,256]{1,0:T(8,128)(2,1)S(1)} %copy-done.9, bf16[4,256,128]{2,1,0:T(8,128)(2,1)S(1)} %get-tuple-element.46.here_ref, bf16[4,256,128]{2,1,0:T(8,128)(2,1)S(1)} %collective-permute-done.13.there_ref, f32[4,512,256]{2,1,0:T(8,128)S(1)} %ref_spectra.2.r_here, ...), custom_call_target="tpu_custom_call" | custom-call | flops 6442450944 | bytes 6291456 | tf_op jit(solution)/shard_map/powers/pallas_call | solution.py:265
  59.8 0.4 collective-permute-start.14
  60.2 0.0 collective-permute-done.8
  60.2 1.3 %collective-permute-done.10 = bf16[4,4,32,128]{3,2,1,0:T(8,128)(2,1)S(1)} collective-permute-done((bf16[4,4,32,128]{3,2,1,0:T(8,128)(2,1)S(1)}, bf16[4,4,32,128]{3,2,1,0:T(8,128)(2,1)S(1)}, u32[]{:S(2)}, u32[]{:S(2)}) %collective-permute-start.10) | collective-permute-done | bytes 131104 | tf_op jit(solution)/shard_map/ppermute | solution.py:288
  61.6 5.6 %collective-permute-done.12 = bf16[4,4,32,128]{3,2,1,0:T(8,128)(2,1)S(1)} collective-permute-done((bf16[4,4,32,128]{3,2,1,0:T(8,128)(2,1)S(1)}, bf16[4,4,32,128]{3,2,1,0:T(8,128)(2,1)S(1)}, u32[]{:S(2)}, u32[]{:S(2)}) %collective-permute-start.12) | collective-permute-done | bytes 131104 | tf_op jit(solution)/shard_map/ppermute | solution.py:288
  67.2 2.7 %collective-permute-done.14 = bf16[4,4,32,128]{3,2,1,0:T(8,128)(2,1)S(1)} collective-permute-done((bf16[4,4,32,128]{3,2,1,0:T(8,128)(2,1)S(1)}, bf16[4,4,32,128]{3,2,1,0:T(8,128)(2,1)S(1)}, u32[]{:S(2)}, u32[]{:S(2)}) %collective-permute-start.14) | collective-permute-done | bytes 131104 | tf_op jit(solution)/shard_map/ppermute | solution.py:288
  69.9 1.0 %pad_maximum_fusion = f32[4,16,32,128]{3,2,1,0:T(8,128)} fusion(f32[4,4,32,128]{3,2,1,0:T(8,128)S(1)} %add_multiply_fusion, f32[4,4,32,128]{3,2,1,0:T(8,128)S(1)} %add_multiply_fusion.1, f32[4,4,32,128]{3,2,1,0:T(8,128)S(1)} %add_multiply_fusion.2, f32[4,4,32,128]{3,2,1,0:T(8,128)S(1)} %add_multiply_fusion.3), kind=kLoop, calls=%fused_computation | loop fusion | flops 786432 | bytes 2097152 | tf_op jit(solution)/shard_map/concatenate | solution.py:315
  (18 shorter events, 0.2 us)
Async XLA Ops:
  0.1 2.2 %copy-start = (bf16[2,16,1,65536]{3,1,2,0:T(8,128)(2,1)S(1)}, bf16[2,16,1,65536]{3,1,2,0:T(8,128)(2,1)}, u32[]{:S(2)}) copy-start(bf16[2,16,1,65536]{3,1,2,0:T(8,128)(2,1)} %param.14) | copy-start | bytes 12582916
  2.3 0.7 copy-start.5
  2.9 0.7 copy-start.6
  3.6 0.7 copy-start.7
  4.2 25.7 %copy-start.2 = (f32[2,4,256,128]{3,2,1,0:T(8,128)S(1)}, f32[2,4,256,128]{3,2,1,0:T(8,128)}, u32[]{:S(2)}) copy-start(f32[2,4,256,128]{3,2,1,0:T(8,128)} %constant.24.clone.dop_ref) | copy-start | bytes 3145732
  4.2 25.7 %copy-start.3 = (f32[2,4,192,128]{3,2,1,0:T(8,128)S(1)}, f32[2,4,192,128]{3,2,1,0:T(8,128)}, u32[]{:S(2)}) copy-start(f32[2,4,192,128]{3,2,1,0:T(8,128)} %constant.23.clone.lag_ref) | copy-start | bytes 2359300
  4.2 25.7 %copy-start.4 = (s32[4]{0:T(128)S(1)}, s32[4]{0:T(128)}, u32[]{:S(2)}) copy-start(s32[4]{0:T(128)} %delay.5) | copy-start | bytes 52
  4.2 25.7 %copy-start.8 = (s32[4]{0:T(128)S(1)}, s32[4]{0:T(128)}, u32[]{:S(2)}) copy-start(s32[4]{0:T(128)} %doppler.1) | copy-start | bytes 52
  8.8 23.7 %copy-start.1 = (bf16[512,1024]{1,0:T(8,128)(2,1)S(1)}, bf16[512,1024]{1,0:T(8,128)(2,1)}, u32[]{:S(2)}) copy-start(bf16[512,1024]{1,0:T(8,128)(2,1)} %constant.25.clone.table_ref) | copy-start | bytes 3145732
  8.8 1.5 %collective-permute-start = (bf16[2,256,128]{2,1,0:T(8,128)(2,1)S(1)}, bf16[2,256,128]{2,1,0:T(8,128)(2,1)S(1)}, u32[]{:S(2)}, u32[]{:S(2)}) collective-permute-start(bf16[2,256,128]{2,1,0:T(8,128)(2,1)S(1)} %get-tuple-element.28), channel_id=1, source_target_pairs={{0,4},{4,0},{8,12},{12,8},{16,20},{20,16},{24,28},{28,24},{1,5},{5... | collective-permute-start | bytes 393224 | tf_op jit(solution)/shard_map/ppermute | solution.py:288
  10.4 6.8 %collective-permute-start.2 = (bf16[2,256,128]{2,1,0:T(8,128)(2,1)S(1)}, bf16[2,256,128]{2,1,0:T(8,128)(2,1)S(1)}, u32[]{:S(2)}, u32[]{:S(2)}) collective-permute-start(bf16[2,256,128]{2,1,0:T(8,128)(2,1)S(1)} %add.24), channel_id=1, source_target_pairs={{0,8},{4,12},{8,0},{12,4},{16,24},{20,28},{24,16},{28,20},{1,9},{5... | collective-permute-start | bytes 393224 | tf_op jit(solution)/shard_map/ppermute | solution.py:288
  13.3 8.1 %collective-permute-start.3 = (bf16[2,256,128]{2,1,0:T(8,128)(2,1)S(1)}, bf16[2,256,128]{2,1,0:T(8,128)(2,1)S(1)}, u32[]{:S(2)}, u32[]{:S(2)}) collective-permute-start(bf16[2,256,128]{2,1,0:T(8,128)(2,1)S(1)} %add.24), channel_id=1, source_target_pairs={{0,16},{4,20},{8,24},{12,28},{16,0},{20,4},{24,8},{28,12},{1,17},{... | collective-permute-start | bytes 393224 | tf_op jit(solution)/shard_map/ppermute | solution.py:288
  14.8 6.6 %collective-permute-start.4 = (bf16[2,256,128]{2,1,0:T(8,128)(2,1)S(1)}, bf16[2,256,128]{2,1,0:T(8,128)(2,1)S(1)}, u32[]{:S(2)}, u32[]{:S(2)}) collective-permute-start(bf16[2,256,128]{2,1,0:T(8,128)(2,1)S(1)} %add.24), channel_id=1, source_target_pairs={{0,24},{4,28},{8,16},{12,20},{16,8},{20,12},{24,0},{28,4},{1,25},{... | collective-permute-start | bytes 393224 | tf_op jit(solution)/shard_map/ppermute | solution.py:288
  21.4 6.5 %collective-permute-start.6 = (bf16[2,256,128]{2,1,0:T(8,128)(2,1)S(1)}, bf16[2,256,128]{2,1,0:T(8,128)(2,1)S(1)}, u32[]{:S(2)}, u32[]{:S(2)}) collective-permute-start(bf16[2,256,128]{2,1,0:T(8,128)(2,1)S(1)} %add_add_fusion.mine_ref), channel_id=1, source_target_pairs={{0,1},{1,0},{2,3},{3,2},{4,5},{5,4},{6,7},{7,6},{8,9},{9,8},{10,11... | collective-permute-start | bytes 393224 | tf_op jit(solution)/shard_map/ppermute | solution.py:288
  23.0 13.4 %collective-permute-start.1 = (bf16[4,256,128]{2,1,0:T(8,128)(2,1)S(1)}, bf16[4,256,128]{2,1,0:T(8,128)(2,1)S(1)}, u32[]{:S(2)}, u32[]{:S(2)}) collective-permute-start(bf16[4,256,128]{2,1,0:T(8,128)(2,1)S(1)} %get-tuple-element.33.here_ref), channel_id=1, source_target_pairs={{0,1},{1,0},{2,3},{3,2},{4,5},{5,4},{6,7},{7,6},{8,9},{9,8},{10,11... | collective-permute-start | bytes 786440 | tf_op jit(solution)/shard_map/ppermute | solution.py:288
  23.5 7.4 %collective-permute-start.5 = (bf16[2,256,128]{2,1,0:T(8,128)(2,1)S(1)}, bf16[2,256,128]{2,1,0:T(8,128)(2,1)S(1)}, u32[]{:S(2)}, u32[]{:S(2)}) collective-permute-start(bf16[2,256,128]{2,1,0:T(8,128)(2,1)S(1)} %add_add_fusion.mine_ref), channel_id=1, source_target_pairs={{0,4},{4,0},{8,12},{12,8},{16,20},{20,16},{24,28},{28,24},{1,5},{5... | collective-permute-start | bytes 393224 | tf_op jit(solution)/shard_map/ppermute | solution.py:288
  27.9 6.6 %collective-permute-start.7 = (bf16[2,256,128]{2,1,0:T(8,128)(2,1)S(1)}, bf16[2,256,128]{2,1,0:T(8,128)(2,1)S(1)}, u32[]{:S(2)}, u32[]{:S(2)}) collective-permute-start(bf16[2,256,128]{2,1,0:T(8,128)(2,1)S(1)} %collective-permute-done.6.mine_ref), channel_id=1, source_target_pairs={{0,4},{4,0},{8,12},{12,8},{16,20},{20,16},{24,28},{28,24},{1,5},{5... | collective-permute-start | bytes 393224 | tf_op jit(solution)/shard_map/ppermute | solution.py:288
  27.9 15.6 %collective-permute-start.9 = (bf16[4,256,128]{2,1,0:T(8,128)(2,1)S(1)}, bf16[4,256,128]{2,1,0:T(8,128)(2,1)S(1)}, u32[]{:S(2)}, u32[]{:S(2)}) collective-permute-start(bf16[4,256,128]{2,1,0:T(8,128)(2,1)S(1)} %get-tuple-element.40.here_ref), channel_id=1, source_target_pairs={{0,1},{1,0},{2,3},{3,2},{4,5},{5,4},{6,7},{7,6},{8,9},{9,8},{10,11... | collective-permute-start | bytes 786440 | tf_op jit(solution)/shard_map/ppermute | solution.py:288
  29.5 18.9 %collective-permute-start.11 = (bf16[4,256,128]{2,1,0:T(8,128)(2,1)S(1)}, bf16[4,256,128]{2,1,0:T(8,128)(2,1)S(1)}, u32[]{:S(2)}, u32[]{:S(2)}) collective-permute-start(bf16[4,256,128]{2,1,0:T(8,128)(2,1)S(1)} %get-tuple-element.43.here_ref), channel_id=1, source_target_pairs={{0,1},{1,0},{2,3},{3,2},{4,5},{5,4},{6,7},{7,6},{8,9},{9,8},{10,11... | collective-permute-start | bytes 786440 | tf_op jit(solution)/shard_map/ppermute | solution.py:288
  30.9 24.6 %collective-permute-start.13 = (bf16[4,256,128]{2,1,0:T(8,128)(2,1)S(1)}, bf16[4,256,128]{2,1,0:T(8,128)(2,1)S(1)}, u32[]{:S(2)}, u32[]{:S(2)}) collective-permute-start(bf16[4,256,128]{2,1,0:T(8,128)(2,1)S(1)} %get-tuple-element.46.here_ref), channel_id=1, source_target_pairs={{0,1},{1,0},{2,3},{3,2},{4,5},{5,4},{6,7},{7,6},{8,9},{9,8},{10,11... | collective-permute-start | bytes 786440 | tf_op jit(solution)/shard_map/ppermute | solution.py:288
  34.4 2.0 %copy-start.9 = (bf16[512,256]{1,0:T(8,128)(2,1)S(1)}, bf16[512,256]{1,0:T(8,128)(2,1)}, u32[]{:S(2)}) copy-start(bf16[512,256]{1,0:T(8,128)(2,1)} %constant.26.clone.table_ref) | copy-start | bytes 786436
  40.8 19.4 %collective-permute-start.8 = (bf16[4,4,32,128]{3,2,1,0:T(8,128)(2,1)S(1)}, bf16[4,4,32,128]{3,2,1,0:T(8,128)(2,1)S(1)}, u32[]{:S(2)}, u32[]{:S(2)}) collective-permute-start(bf16[4,4,32,128]{3,2,1,0:T(8,128)(2,1)S(1)} %bitcast.13), channel_id=1, source_target_pairs={{0,2},{1,3},{2,0},{3,1},{4,6},{5,7},{6,4},{7,5},{8,10},{9,11},{10,... | collective-permute-start | bytes 393224 | tf_op jit(solution)/shard_map/ppermute | solution.py:288
  47.8 13.8 %collective-permute-start.10 = (bf16[4,4,32,128]{3,2,1,0:T(8,128)(2,1)S(1)}, bf16[4,4,32,128]{3,2,1,0:T(8,128)(2,1)S(1)}, u32[]{:S(2)}, u32[]{:S(2)}) collective-permute-start(bf16[4,4,32,128]{3,2,1,0:T(8,128)(2,1)S(1)} %bitcast.14), channel_id=1, source_target_pairs={{0,2},{1,3},{2,0},{3,1},{4,6},{5,7},{6,4},{7,5},{8,10},{9,11},{10,... | collective-permute-start | bytes 393224 | tf_op jit(solution)/shard_map/ppermute | solution.py:288
  52.8 14.4 %collective-permute-start.12 = (bf16[4,4,32,128]{3,2,1,0:T(8,128)(2,1)S(1)}, bf16[4,4,32,128]{3,2,1,0:T(8,128)(2,1)S(1)}, u32[]{:S(2)}, u32[]{:S(2)}) collective-permute-start(bf16[4,4,32,128]{3,2,1,0:T(8,128)(2,1)S(1)} %bitcast.15), channel_id=1, source_target_pairs={{0,2},{1,3},{2,0},{3,1},{4,6},{5,7},{6,4},{7,5},{8,10},{9,11},{10,... | collective-permute-start | bytes 393224 | tf_op jit(solution)/shard_map/ppermute | solution.py:288
  59.8 10.1 %collective-permute-start.14 = (bf16[4,4,32,128]{3,2,1,0:T(8,128)(2,1)S(1)}, bf16[4,4,32,128]{3,2,1,0:T(8,128)(2,1)S(1)}, u32[]{:S(2)}, u32[]{:S(2)}) collective-permute-start(bf16[4,4,32,128]{3,2,1,0:T(8,128)(2,1)S(1)} %bitcast.16), channel_id=1, source_target_pairs={{0,2},{1,3},{2,0},{3,1},{4,6},{5,7},{6,4},{7,5},{8,10},{9,11},{10,... | collective-permute-start | bytes 393224 | tf_op jit(solution)/shard_map/ppermute | solution.py:288

commit v2 on v1

v2 whole, which is shorter than its diff:
```python
import functools

import jax
import jax.numpy as jnp
import ml_dtypes
import numpy as np
from jax import lax
from jax.experimental import pallas as pl
from jax.experimental.pallas import tpu as pltpu
from jax.sharding import PartitionSpec as P

TX = 4
HALF_TX = TX // 2
DECIM = 4
TAPS = 32
BLOCK_LEN = 64
BLOCKS = 256
DELAYS = 128
DOPPLER = 128
FFT = 256
STRIDE = DECIM * BLOCK_LEN
LEAD = 128
REACH = LEAD + STRIDE
PAIR = 2 * BLOCK_LEN
GROUPS = 4
LANES = 128
LANE_BLOCKS = 2 * FFT // LANES
HALF_DELAYS = DELAYS // 2
VMEM_LIMIT = 24 * 1024 * 1024

SMEM = pl.BlockSpec(memory_space=pltpu.SMEM)
VMEM = pl.BlockSpec(memory_space=pltpu.VMEM)
HBM = pl.BlockSpec(memory_space=pltpu.HBM)


def split_bf16(table):
    hi = table.astype(ml_dtypes.bfloat16)
    lo = (table - hi.astype(np.float64)).astype(ml_dtypes.bfloat16)
    return hi, lo


def fourier(samples):
    angle = 2 * np.pi / FFT * (np.outer(np.arange(FFT), samples) % FFT)
    cos, sin = np.cos(angle), np.sin(angle)
    return np.block([[cos, sin], [-sin, cos]])


def surv_fourier():
    hi, lo = split_bf16(fourier(np.arange(BLOCK_LEN)))
    return np.concatenate([hi, lo], axis=1)


def ref_fourier():
    parts = [fourier(np.arange(BLOCK_LEN) + BLOCK_LEN * e) for e in range(4)]
    hi, lo = split_bf16(np.concatenate(parts, axis=1))
    return np.concatenate([hi, lo], axis=1)


def in_lane_blocks(both):
    parts, rows, _ = both.shape
    return both.astype(np.float32).reshape(parts, rows, LANE_BLOCKS, LANES).swapaxes(1, 2)


def lag_table():
    lags = 191 - np.arange(192)
    angle = 2 * np.pi / FFT * (np.outer(lags, np.arange(FFT)) % FFT)
    cos, sin = np.cos(angle), np.sin(angle)
    scale = 1.0 / (FFT * np.sqrt(BLOCK_LEN))
    both = np.stack([np.concatenate([cos, sin], 1), np.concatenate([-sin, cos], 1)])
    both = both.astype(ml_dtypes.bfloat16).astype(np.float64) * scale
    return in_lane_blocks(both)


def doppler_table():
    freqs = np.arange(BLOCKS) - BLOCKS // 2
    angle = 2 * np.pi / BLOCKS * (np.outer(freqs, np.arange(BLOCKS)) % BLOCKS)
    cos, sin = np.cos(angle), np.sin(angle)
    both = np.stack([np.concatenate([cos, sin], 1), np.concatenate([-sin, cos], 1)])
    return in_lane_blocks(both.astype(ml_dtypes.bfloat16))


def nt_dot(left, right):
    return lax.dot_general(
        left, right, (((1,), (1,)), ((), ())), preferred_element_type=jnp.float32
    )


def dot(left, right):
    return jnp.dot(left, right, preferred_element_type=jnp.float32)


def decimate_kernel(beams, ids, owner, delay, doppler, staps, rtaps, volts, *refs):
    s_refs, refs = refs[:GROUPS], refs[GROUPS:]
    keep_ref, send_ref, params, x, taps, small, band, all_s, all_r, sems, small_sems = refs
    chunks = sems.shape[0]
    raw = volts.shape[2]
    wide = raw // chunks
    rows = wide // STRIDE
    blocks = raw // STRIDE
    smalls = [
        pltpu.make_async_copy(ref, small.at[n], small_sems.at[n])
        for n, ref in enumerate((owner, delay, doppler))
    ]
    smalls += [
        pltpu.make_async_copy(ref, taps.at[n], small_sems.at[3 + n])
        for n, ref in enumerate((staps, rtaps))
    ]
    copies = [
        pltpu.make_async_copy(
            volts.at[:, :, pl.ds(n * wide, wide)],
            x.at[:, :, pl.ds(LEAD + n * wide, wide)],
            sems.at[n],
        )
        for n in range(chunks)
    ]
    for copy in smalls + copies:
        copy.start()
    x[:, :, :LEAD] = jnp.zeros((2, beams, LEAD), jnp.bfloat16)
    for copy in smalls:
        copy.wait()

    shape = (REACH, PAIR)
    q = lax.broadcasted_iota(jnp.int32, shape, 0)
    lane = lax.broadcasted_iota(jnp.int32, shape, 1)
    tap = LEAD + DECIM * (lane % BLOCK_LEN) - q
    first = lane < BLOCK_LEN
    one, two = taps[0].astype(jnp.float32), taps[1].astype(jnp.float32)
    both = jnp.zeros(shape, jnp.float32)
    for t in range(TAPS):
        row = jnp.where(first[:1], one[:, t : t + 1], two[:, t : t + 1])
        both = jnp.where(tap == t, row, both)
    turned = pltpu.roll(both, BLOCK_LEN, 1)
    zero = jnp.zeros(shape, jnp.float32)
    band[:REACH, :PAIR] = jnp.where(first, both, zero).astype(jnp.bfloat16)
    band[REACH:, :PAIR] = jnp.where(first, zero, turned).astype(jnp.bfloat16)
    band[:REACH, PAIR:] = jnp.where(first, turned, zero).astype(jnp.bfloat16)
    band[REACH:, PAIR:] = jnp.where(first, zero, both).astype(jnp.bfloat16)
    for k in range(TX):
        params[k] = small[1, k]
        params[TX + k] = small[2, k]
    params[2 * TX] = ids[0]
    params[2 * TX + 1] = ids[1]

    for n in range(chunks):
        copies[n].wait()
        parts = []
        for c in range(2):
            parts.append(
                jnp.concatenate(
                    [x[c, :, l * STRIDE : l * STRIDE + REACH] for l in range(n * rows, (n + 1) * rows)],
                    axis=0,
                )
            )
        out = dot(jnp.concatenate(parts, axis=1), band[...])
        span = slice(n * rows * beams, (n + 1) * rows * beams)
        all_s[span] = out[:, :PAIR]
        all_r[span] = out[:, PAIR:]
    core = ids[0] % 2
    for ref, first_tx in ((keep_ref, core * HALF_TX), (send_ref, (1 - core) * HALF_TX)):
        for k in range(HALF_TX):
            beam = small[0, first_tx + k]
            picked = all_r[pl.ds(beam % beams, blocks, stride=beams), :]
            ref[k] = jnp.where(beam // beams == ids[0], picked, 0.0).astype(jnp.bfloat16)
    count = beams // GROUPS
    for b in range(beams):
        picked = all_s[pl.ds(b, blocks, stride=beams), :]
        s_refs[b // count][b % count] = picked.astype(jnp.bfloat16)


def decimate(volts, staps, rtaps, ids, owner, delay, doppler):
    beams, raw = volts.shape[1:]
    blocks = raw // STRIDE
    count = beams // GROUPS
    chunks = 4
    arrays = (owner, delay, doppler, staps, rtaps, volts)
    shape = lambda n: jax.ShapeDtypeStruct((n, blocks, PAIR), jnp.bfloat16)
    return pl.pallas_call(
        functools.partial(decimate_kernel, beams),
        in_specs=[SMEM] + [HBM] * 6,
        out_specs=[VMEM] * (GROUPS + 2) + [SMEM],
        out_shape=[shape(count)] * GROUPS
        + [shape(HALF_TX)] * 2
        + [jax.ShapeDtypeStruct((2 * TX + 2,), jnp.int32)],
        scratch_shapes=[
            pltpu.VMEM((2, beams, LEAD + raw), jnp.bfloat16),
            pltpu.VMEM((2, 1, TAPS), jnp.bfloat16),
            pltpu.SMEM((3, TX), jnp.int32),
            pltpu.VMEM((2 * REACH, 2 * PAIR), jnp.bfloat16),
            pltpu.VMEM((blocks * beams, PAIR), jnp.float32),
            pltpu.VMEM((blocks * beams, PAIR), jnp.float32),
            pltpu.SemaphoreType.DMA((chunks,)),
            pltpu.SemaphoreType.DMA((5,)),
        ],
        compiler_params=pltpu.CompilerParams(vmem_limit_bytes=VMEM_LIMIT),
        name="decimate",
    )(ids, *(pltpu.with_memory_space_constraint(a, pltpu.HBM) for a in arrays))


def tables_kernel(chunks, params, lag_ref, dop_ref, lags, dops):
    each = DELAYS // chunks
    for k in range(TX):
        base = (params[k] + DELAYS - 1) % BLOCK_LEN
        for part in range(2):
            for n in range(chunks // 2):
                chunk = params[2 * TX + 1] ^ (2 * n)
                at = part * HALF_DELAYS + n * each
                for q in range(LANE_BLOCKS):
                    picked = lag_ref[part, q, pl.ds(base + chunk * each, each), :]
                    lags[k, at : at + each, q * LANES : (q + 1) * LANES] = picked.astype(jnp.bfloat16)
            for q in range(LANE_BLOCKS):
                picked = dop_ref[part, q, pl.ds(params[TX + k], DOPPLER), :].T.astype(jnp.bfloat16)
                dops[k, q * LANES : (q + 1) * LANES, part * DOPPLER : (part + 1) * DOPPLER] = picked


def make_tables(params, chunks):
    return pl.pallas_call(
        functools.partial(tables_kernel, chunks),
        in_specs=[SMEM, VMEM, VMEM],
        out_specs=[VMEM, VMEM],
        out_shape=[
            jax.ShapeDtypeStruct((TX, DELAYS, 2 * FFT), jnp.bfloat16),
            jax.ShapeDtypeStruct((TX, 2 * BLOCKS, 2 * DOPPLER), jnp.bfloat16),
        ],
        compiler_params=pltpu.CompilerParams(vmem_limit_bytes=VMEM_LIMIT),
        name="tables",
    )(params, jnp.asarray(lag_table()), jnp.asarray(doppler_table()))


PAD = 8


def write_ref_spectra(params, table_ref, mine_ref, other_ref, out_ref, padded):
    core = params[2 * TX] % 2
    padded[:PAD] = jnp.zeros((PAD, PAIR), jnp.float32)
    padded[PAD + BLOCKS :] = jnp.zeros((PAD, PAIR), jnp.float32)
    for k in range(TX):
        here = core == k // HALF_TX
        ref = jnp.where(here, mine_ref[k % HALF_TX], other_ref[k % HALF_TX])
        padded[PAD : PAD + BLOCKS] = ref.astype(jnp.float32)
        start = PAD - 1 - (params[k] + DELAYS - 1) // BLOCK_LEN
        window = jnp.concatenate(
            [padded[pl.ds(start + e, BLOCKS), :].astype(jnp.bfloat16) for e in range(4)], axis=1
        )
        out_ref[k] = nt_dot(table_ref[...], jnp.concatenate([window, window], axis=1))


def sum_powers(table_ref, segments, lag_ref, dop_ref, spec, prods, corrs, emit):
    count = segments[0][0].shape[0]
    rows = count * HALF_DELAYS
    for n, (s_ref, _) in enumerate(segments):
        s = s_ref[...].reshape(count * BLOCKS, PAIR)
        spec[n] = nt_dot(table_ref[...], jnp.concatenate([s, s], axis=1))
    for k in range(TX):
        corr = corrs.at[k % 2]
        for n, (_, r_ref) in enumerate(segments):
            r_re, r_im = r_ref[k, :FFT], r_ref[k, FFT:]
            prod = prods.at[n]
            for b in range(count):
                cols = slice(b * BLOCKS, (b + 1) * BLOCKS)
                s_re, s_im = spec[n, :FFT, cols], spec[n, FFT:, cols]
                prod[:FFT, cols] = (s_re * r_re + s_im * r_im).astype(jnp.bfloat16)
                prod[FFT:, cols] = (s_im * r_re - s_re * r_im).astype(jnp.bfloat16)
            out = dot(lag_ref[k], prod[...]).astype(jnp.bfloat16)
            for b in range(count):
                cols = slice(b * BLOCKS, (b + 1) * BLOCKS)
                at = n * rows + b * HALF_DELAYS
                corr[at : at + HALF_DELAYS, :BLOCKS] = out[:HALF_DELAYS, cols]
                corr[at : at + HALF_DELAYS, BLOCKS:] = out[HALF_DELAYS:, cols]
        x = dot(corr[...], dop_ref[k])
        x_re, x_im = x[:, :DOPPLER], x[:, DOPPLER:]
        power = (x_re * x_re + x_im * x_im) * (1.0 / (4 * BLOCKS))
        power = functools.reduce(
            jnp.add, [power[n * rows : (n + 1) * rows] for n in range(len(segments))]
        )
        emit(k, power.reshape(count, HALF_DELAYS, DOPPLER))


def emit_halves(chunks, own_ref, send_ref):
    each = DELAYS // chunks

    def emit(k, power):
        own_ref[k] = power[:, :each]
        for n in range(1, chunks // 2):
            send_ref[n - 1, k] = power[:, n * each : (n + 1) * each].astype(jnp.bfloat16)

    return emit


def first_kernel(
    params, rtab, mine, other, stab, s_ref, lags, dops, r_ref, part_ref, padded, spec, prods, corrs
):
    write_ref_spectra(params, rtab, mine, other, r_ref, padded)

    def emit(k, power):
        part_ref[k] = power

    sum_powers(stab, [(s_ref, r_ref)], lags, dops, spec, prods, corrs, emit)


def second_kernel(
    chunks, params, rtab, mine, other, stab, s_ref, lags, dops, part_ref, r_ref, own_ref, send_ref, padded, spec, prods, corrs
):
    write_ref_spectra(params, rtab, mine, other, r_ref, padded)
    store = emit_halves(chunks, own_ref, send_ref)
    emit = lambda k, power: store(k, power + part_ref[k])
    sum_powers(stab, [(s_ref, r_ref)], lags, dops, spec, prods, corrs, emit)


def both_kernel(
    chunks, stab, here, there, r_here, r_there, lags, dops, own_ref, send_ref, spec, prods, corrs
):
    emit = emit_halves(chunks, own_ref, send_ref)
    sum_powers(stab, [(here, r_here), (there, r_there)], lags, dops, spec, prods, corrs, emit)


def call_powers(kernel, name, args, out_shape, count, segments, spectra):
    padded = [pltpu.VMEM((BLOCKS + 2 * PAD, PAIR), jnp.float32)]
    return pl.pallas_call(
        kernel,
        in_specs=[SMEM if a.ndim == 1 else VMEM for a in args],
        out_specs=[VMEM] * len(out_shape),
        out_shape=out_shape,
        scratch_shapes=(padded if spectra else [])
        + [
            pltpu.VMEM((segments, 2 * FFT, count * BLOCKS), jnp.float32),
            pltpu.VMEM((segments, 2 * FFT, count * BLOCKS), jnp.bfloat16),
            pltpu.VMEM((2, segments * count * HALF_DELAYS, 2 * BLOCKS), jnp.bfloat16),
        ],
        compiler_params=pltpu.CompilerParams(vmem_limit_bytes=VMEM_LIMIT),
        cost_estimate=pl.CostEstimate(
            flops=segments * count * TX * 4 * 768 * 65536, bytes_accessed=6 << 20, transcendentals=0
        ),
        name=name,
    )(*args)


def swap(value, axis, flip):
    size = lax.axis_size(axis)
    return lax.ppermute(value, axis, [(i, i ^ flip) for i in range(size)])


def shards(voltages, surv_taps, ref_taps, tx_owner, delay_start, doppler_start):
    beams_here = voltages.shape[1]
    n_beam = lax.axis_size("beam")
    n_seg = lax.axis_size("seg")
    segments_all = n_seg * voltages.shape[2]
    ids = jnp.stack([lax.axis_index("beam"), lax.axis_index("seg")]).astype(jnp.int32)
    volts = voltages.reshape(2, beams_here, voltages.shape[3])
    out = decimate(
        volts,
        surv_taps.reshape(1, TAPS),
        ref_taps.reshape(1, TAPS),
        ids,
        tx_owner,
        delay_start,
        doppler_start,
    )
    surv, (keep, send, params) = out[:GROUPS], out[GROUPS:]
    half = keep + swap(send, "beam", 1)
    half, surv, params = lax.optimization_barrier((half, surv, params))
    got = [swap(half, "beam", flip) for flip in range(2, n_beam, 2)]
    there = [swap(s, "seg", 1) for s in surv]
    lags, dops = make_tables(params, n_seg)
    got, lags, dops = lax.optimization_barrier((got, lags, dops))
    half = functools.reduce(jnp.add, got, half)
    other = swap(half, "beam", 1)
    leaving, there[0] = lax.optimization_barrier((half, there[0]))
    far = swap(leaving, "seg", 1)
    far_other = swap(other, "seg", 1)
    stab, rtab = jnp.asarray(surv_fourier()), jnp.asarray(ref_fourier())
    count = beams_here // GROUPS
    each = DELAYS // n_seg
    r_shape = jax.ShapeDtypeStruct((TX, 2 * FFT, BLOCKS), jnp.float32)
    part_shape = jax.ShapeDtypeStruct((TX, count, HALF_DELAYS, DOPPLER), jnp.float32)
    halves = [
        jax.ShapeDtypeStruct((TX, count, each, DOPPLER), jnp.float32),
        jax.ShapeDtypeStruct((n_seg // 2 - 1, TX, count, each, DOPPLER), jnp.bfloat16),
    ]
    r_here, part = call_powers(
        first_kernel,
        "first",
        (params, rtab, half, other, stab, surv[0], lags, dops),
        [r_shape, part_shape],
        count,
        1,
        True,
    )
    far, far_other, there[1] = lax.optimization_barrier((far, far_other, there[1]))
    r_there, *sums = call_powers(
        functools.partial(second_kernel, n_seg),
        "second",
        (params, rtab, far, far_other, stab, there[0], lags, dops, part),
        [r_shape] + halves,
        count,
        1,
        True,
    )
    maps = []
    for g in range(GROUPS):
        if g > 0:
            sums = call_powers(
                functools.partial(both_kernel, n_seg),
                "both",
                (stab, surv[g], there[g], r_here, r_there, lags, dops),
                halves,
                count,
                2,
                False,
            )
        total, outgoing = sums
        for n in range(1, n_seg // 2):
            total = total + swap(outgoing[n - 1], "seg", 2 * n).astype(jnp.float32)
        maps.append(total / segments_all)
    return jnp.concatenate(maps, axis=1)


def solution(mesh):
    return jax.shard_map(
        shards,
        mesh=mesh,
        in_specs=(P(None, "beam", "seg", None), P(), P(), P(), P(), P()),
        out_specs=P(None, "beam", "seg", None),
        check_vma=False,
    )
```

time: 71.1 us -> 78.9 us (1.11)
  waiting for transfers between devices: 21.6 us -> 27.9 us
  local copies, waits for them, and re-layouts: 4.18 us -> 0.02 us
  Pallas kernels: 26.8 us -> 30.5 us
  starting transfers between devices: 17 us -> 18.9 us
    ppermute x15, waiting for transfers between devices: 21.6 us -> 27.9 us  [swap(): return lax.ppermute(value, axis, [(i, i ^ flip) for i in range(size)])]
    unnamed x20 -> x8, local copies, waits for them, and re-layouts: 4.18 us -> 0.02 us
    pallas_call x7 -> x6, Pallas kernels: 25.8 us -> 29.6 us  [the longest x5 21.3 us: call_powers(): pl.pallas_call(kernel, in_specs=[SMEM if a.ndim == 1 else VMEM for a in a...]
    ppermute x15, starting transfers between devices: 17 us -> 18.9 us  [swap(): return lax.ppermute(value, axis, [(i, i ^ flip) for i in range(size)])]
  transfers between devices with their start and end apart: 15 -> 15, of which waited for: 7 -> 7; matrix products, arithmetic and copies ran while one was open for 0% -> 0% of each run, Pallas kernels for 31% -> 28%
where the time goes in v2:
time: 78.9 us; the launch traced here: 78.8 us
  Pallas kernels  30.5 us (39%)
  waiting for transfers between devices  27.9 us (35%)
  starting transfers between devices  18.9 us (24%)
  other arithmetic  1.31 us (2%)
    ppermute x15, waiting for transfers between devices, swap(): return lax.ppermute(value, axis, [(i, i ^ flip) for i in range(size)])  27.9 us
    pallas_call x5, Pallas kernels, call_powers(): pl.pallas_call(kernel, in_specs=[SMEM if a.ndim == 1 else VMEM for a in a...  21.3 us
    ppermute x15, starting transfers between devices, swap(): return lax.ppermute(value, axis, [(i, i ^ flip) for i in range(size)])  18.9 us
    pallas_call x1, Pallas kernels, decimate(): pl.pallas_call(functools.partial(decimate_kernel, beams), in_specs=[SMEM]...  8.29 us
  transfers between devices with their start and end apart: 15, of which 7 were waited for; matrix products, arithmetic and copies ran while one was open for 0% of the time, Pallas kernels for 28%

profile of v2, /device:TPU:0, one launch (start us, length us, event | category | flops | bytes accessed | tf_op | source)
XLA Modules:
  0.0 78.8 jit_solution(8254864163321947687)
XLA Ops:
  0.0 0.1 pad_add_fusion.ids
  0.1 0.0 copy-start
  0.1 0.0 copy-start.1
  0.1 8.3 %decimate.1 = (bf16[4,256,128]{2,1,0:T(8,128)(2,1)S(1)}, bf16[4,256,128]{2,1,0:T(8,128)(2,1)S(1)}, bf16[4,256,128]{2,1,0:T(8,128)(2,1)S(1)}, bf16[4,256,128]{2,1...) custom-call(s32[2]{0:T(128)S(1)} %pad_add_fusion.ids, ...), custom_call_target="tpu_custom_call" | custom-call | tf_op jit(solution)/shard_map/decimate/pallas_call | solution.py:177
  8.4 0.0 copy-start.2
  8.4 0.0 copy-start.3
  8.4 0.5 collective-permute-start
  8.9 1.0 %collective-permute-done = bf16[2,256,128]{2,1,0:T(8,128)(2,1)S(1)} collective-permute-done((bf16[2,256,128]{2,1,0:T(8,128)(2,1)S(1)}, bf16[2,256,128]{2,1,0:T(8,128)(2,1)S(1)}, u32[]{:S(2)}, u32[]{:S(2)}) %collective-permute-start) | collective-permute-done | bytes 131104 | tf_op jit(solution)/shard_map/ppermute | solution.py:339
  10.0 2.9 %collective-permute-start.1 = (bf16[2,256,128]{2,1,0:T(8,128)(2,1)S(1)}, bf16[2,256,128]{2,1,0:T(8,128)(2,1)S(1)}, u32[]{:S(2)}, u32[]{:S(2)}) collective-permute-start(bf16[2,256,128]{2,1,0:T(8,128)(2,1)S(1)} %add.24), channel_id=1, source_target_pairs={{0,8},{4,12},{8,0},{12,4},{16,24},{20,28},{24,16},{28,20},{1,9},{5... | collective-permute-start | bytes 393224 | tf_op jit(solution)/shard_map/ppermute | solution.py:339
  12.9 1.5 %collective-permute-start.2 = (bf16[2,256,128]{2,1,0:T(8,128)(2,1)S(1)}, bf16[2,256,128]{2,1,0:T(8,128)(2,1)S(1)}, u32[]{:S(2)}, u32[]{:S(2)}) collective-permute-start(bf16[2,256,128]{2,1,0:T(8,128)(2,1)S(1)} %add.24), channel_id=1, source_target_pairs={{0,16},{4,20},{8,24},{12,28},{16,0},{20,4},{24,8},{28,12},{1,17},{... | collective-permute-start | bytes 393224 | tf_op jit(solution)/shard_map/ppermute | solution.py:339
  14.4 0.0 collective-permute-start.3
  14.4 2.0 %collective-permute-start.4 = (bf16[4,256,128]{2,1,0:T(8,128)(2,1)S(1)}, bf16[4,256,128]{2,1,0:T(8,128)(2,1)S(1)}, u32[]{:S(2)}, u32[]{:S(2)}) collective-permute-start(bf16[4,256,128]{2,1,0:T(8,128)(2,1)S(1)} %get-tuple-element.55.s_ref), channel_id=1, source_target_pairs={{0,1},{1,0},{2,3},{3,2},{4,5},{5,4},{6,7},{7,6},{8,9},{9,8},{10,11... | collective-permute-start | bytes 786440 | tf_op jit(solution)/shard_map/ppermute | solution.py:339
  16.4 0.0 copy-done
  16.4 0.0 copy-done.1
  16.4 0.9 %tables.1 = (bf16[4,128,512]{2,1,0:T(8,128)(2,1)S(1)}, bf16[4,512,256]{2,1,0:T(8,128)(2,1)S(1)}) custom-call(s32[10]{0:T(128)S(1)} %get-tuple-element.48.params, f32[2,4,192,128]{3,2,1,0:T(8,128)S(1)} %copy-done.1, f32[2,4,256,128]{3,2,1,0:T(8,128)S(1)} %copy-done), custom_call_target="tpu_custom_call" | custom-call | tf_op jit(solution)/shard_map/tables/pallas_call | solution.py:216
  17.4 0.0 collective-permute-done.1
  17.4 3.6 %collective-permute-done.2 = bf16[2,256,128]{2,1,0:T(8,128)(2,1)S(1)} collective-permute-done((bf16[2,256,128]{2,1,0:T(8,128)(2,1)S(1)}, bf16[2,256,128]{2,1,0:T(8,128)(2,1)S(1)}, u32[]{:S(2)}, u32[]{:S(2)}) %collective-permute-start.2) | collective-permute-done | bytes 131104 | tf_op jit(solution)/shard_map/ppermute | solution.py:339
  20.9 0.0 collective-permute-done.3
  21.0 0.1 collective-permute-start.6
  21.1 1.6 %collective-permute-start.8 = (bf16[4,256,128]{2,1,0:T(8,128)(2,1)S(1)}, bf16[4,256,128]{2,1,0:T(8,128)(2,1)S(1)}, u32[]{:S(2)}, u32[]{:S(2)}) collective-permute-start(bf16[4,256,128]{2,1,0:T(8,128)(2,1)S(1)} %get-tuple-element.57.here), channel_id=1, source_target_pairs={{0,1},{1,0},{2,3},{3,2},{4,5},{5,4},{6,7},{7,6},{8,9},{9,8},{10,11... | collective-permute-start | bytes 786440 | tf_op jit(solution)/shard_map/ppermute | solution.py:339
  22.7 0.5 collective-permute-start.11
  23.2 1.6 %collective-permute-start.13 = (bf16[4,256,128]{2,1,0:T(8,128)(2,1)S(1)}, bf16[4,256,128]{2,1,0:T(8,128)(2,1)S(1)}, u32[]{:S(2)}, u32[]{:S(2)}) collective-permute-start(bf16[4,256,128]{2,1,0:T(8,128)(2,1)S(1)} %get-tuple-element.74.here), channel_id=1, source_target_pairs={{0,1},{1,0},{2,3},{3,2},{4,5},{5,4},{6,7},{7,6},{8,9},{9,8},{10,11... | collective-permute-start | bytes 786440 | tf_op jit(solution)/shard_map/ppermute | solution.py:339
  24.7 0.0 collective-permute-done.4.s_ref
  24.7 0.5 collective-permute-start.5
  25.2 0.0 collective-permute-done.6.other
  25.2 1.6 %collective-permute-start.7 = (bf16[2,256,128]{2,1,0:T(8,128)(2,1)S(1)}, bf16[2,256,128]{2,1,0:T(8,128)(2,1)S(1)}, u32[]{:S(2)}, u32[]{:S(2)}) collective-permute-start(bf16[2,256,128]{2,1,0:T(8,128)(2,1)S(1)} %collective-permute-done.6.other), channel_id=1, source_target_pairs={{0,1},{1,0},{2,3},{3,2},{4,5},{5,4},{6,7},{7,6},{8,9},{9,8},{10,11... | collective-permute-start | bytes 393224 | tf_op jit(solution)/shard_map/ppermute | solution.py:339
  26.8 0.0 copy-done.2
  26.8 0.0 copy-done.3
  26.8 4.1 %first.1 = (f32[4,512,256]{2,1,0:T(8,128)S(1)}, f32[4,4,64,128]{3,2,1,0:T(8,128)S(1)}) custom-call(s32[10]{0:T(128)S(1)} %get-tuple-element.48.params, bf16[512,1024]{1,0:T(8,128)(2,1)S(1)} %copy-done.2, bf16[2,256,128]{2,1,0:T(8,128)(2,1)S(1)} %add_add_fusion.mine, bf16[2,256,128]{2,1,0:T(8,128)(2,1)S(1)} %collective-permute-done.6.other, ...), custom_call_target="tpu_custom_call" | custom-call | flops 3221225472 | bytes 6291456 | tf_op jit(solution)/shard_map/first/pallas_call | solution.py:318
  30.9 0.0 collective-permute-done.8.there
  30.9 13.3 %collective-permute-done.5.mine = bf16[2,256,128]{2,1,0:T(8,128)(2,1)S(1)} collective-permute-done((bf16[2,256,128]{2,1,0:T(8,128)(2,1)S(1)}, bf16[2,256,128]{2,1,0:T(8,128)(2,1)S(1)}, u32[]{:S(2)}, u32[]{:S(2)}) %collective-permute-start.5) | collective-permute-done | bytes 131104 | tf_op jit(solution)/shard_map/ppermute | solution.py:339
  44.3 2.4 %collective-permute-done.7.other = bf16[2,256,128]{2,1,0:T(8,128)(2,1)S(1)} collective-permute-done((bf16[2,256,128]{2,1,0:T(8,128)(2,1)S(1)}, bf16[2,256,128]{2,1,0:T(8,128)(2,1)S(1)}, u32[]{:S(2)}, u32[]{:S(2)}) %collective-permute-start.7) | collective-permute-done | bytes 131104 | tf_op jit(solution)/shard_map/ppermute | solution.py:339
  46.6 4.1 %second.1 = (f32[4,512,256]{2,1,0:T(8,128)S(1)}, f32[4,4,32,128]{3,2,1,0:T(8,128)S(1)}, bf16[1,4,4,32,128]{4,3,2,1,0:T(8,128)(2,1)S(1)}) custom-call(s32[10]{0:T(128)S(1)} %get-tuple-element.48.params, bf16[512,1024]{1,0:T(8,128)(2,1)S(1)} %copy-done.2, bf16[2,256,128]{2,1,0:T(8,128)(2,1)S(1)} %collective-permute-done.5.mine, ...), custom_call_target="tpu_custom_call" | custom-call | flops 3221225472 | bytes 6291456 | tf_op jit(solution)/shard_map/second/pallas_call | solution.py:318
  50.8 2.7 %collective-permute-start.9 = (bf16[4,4,32,128]{3,2,1,0:T(8,128)(2,1)S(1)}, bf16[4,4,32,128]{3,2,1,0:T(8,128)(2,1)S(1)}, u32[]{:S(2)}, u32[]{:S(2)}) collective-permute-start(bf16[4,4,32,128]{3,2,1,0:T(8,128)(2,1)S(1)} %bitcast.9), channel_id=1, source_target_pairs={{0,2},{1,3},{2,0},{3,1},{4,6},{5,7},{6,4},{7,5},{8,10},{9,11},{10,... | collective-permute-start | bytes 393224 | tf_op jit(solution)/shard_map/ppermute | solution.py:339
  53.4 4.5 %both.3 = (f32[4,4,32,128]{3,2,1,0:T(8,128)S(1)}, bf16[1,4,4,32,128]{4,3,2,1,0:T(8,128)(2,1)S(1)}) custom-call(bf16[512,256]{1,0:T(8,128)(2,1)S(1)} %copy-done.3, bf16[4,256,128]{2,1,0:T(8,128)(2,1)S(1)} %get-tuple-element.57.here, bf16[4,256,128]{2,1,0:T(8,128)(2,1)S(1)} %collective-permute-done.8.there, f32[4,512,256]{2,1,0:T(8,128)S(1)} %get-tuple-element.67.r_here, ...), custom_call_target="tpu_custom_call" | custom-call | flops 6442450944 | bytes 6291456 | tf_op jit(solution)/shard_map/both/pallas_call | solution.py:318
  57.9 0.4 collective-permute-start.10
  58.3 0.0 collective-permute-done.11.there
  58.3 4.3 %both.4 = (f32[4,4,32,128]{3,2,1,0:T(8,128)S(1)}, bf16[1,4,4,32,128]{4,3,2,1,0:T(8,128)(2,1)S(1)}) custom-call(bf16[512,256]{1,0:T(8,128)(2,1)S(1)} %copy-done.3, bf16[4,256,128]{2,1,0:T(8,128)(2,1)S(1)} %get-tuple-element.71.here, bf16[4,256,128]{2,1,0:T(8,128)(2,1)S(1)} %collective-permute-done.11.there, f32[4,512,256]{2,1,0:T(8,128)S(1)} %get-tuple-element.67.r_here, ...), custom_call_target="tpu_custom_call" | custom-call | flops 6442450944 | bytes 6291456 | tf_op jit(solution)/shard_map/both/pallas_call | solution.py:318
  62.6 2.7 %collective-permute-start.12 = (bf16[4,4,32,128]{3,2,1,0:T(8,128)(2,1)S(1)}, bf16[4,4,32,128]{3,2,1,0:T(8,128)(2,1)S(1)}, u32[]{:S(2)}, u32[]{:S(2)}) collective-permute-start(bf16[4,4,32,128]{3,2,1,0:T(8,128)(2,1)S(1)} %bitcast.11), channel_id=1, source_target_pairs={{0,2},{1,3},{2,0},{3,1},{4,6},{5,7},{6,4},{7,5},{8,10},{9,11},{10,... | collective-permute-start | bytes 393224 | tf_op jit(solution)/shard_map/ppermute | solution.py:339
  65.3 0.0 collective-permute-done.13.there
  65.3 4.3 %both.5 = (f32[4,4,32,128]{3,2,1,0:T(8,128)S(1)}, bf16[1,4,4,32,128]{4,3,2,1,0:T(8,128)(2,1)S(1)}) custom-call(bf16[512,256]{1,0:T(8,128)(2,1)S(1)} %copy-done.3, bf16[4,256,128]{2,1,0:T(8,128)(2,1)S(1)} %get-tuple-element.74.here, bf16[4,256,128]{2,1,0:T(8,128)(2,1)S(1)} %collective-permute-done.13.there, f32[4,512,256]{2,1,0:T(8,128)S(1)} %get-tuple-element.67.r_here, ...), custom_call_target="tpu_custom_call" | custom-call | flops 6442450944 | bytes 6291456 | tf_op jit(solution)/shard_map/both/pallas_call | solution.py:318
  69.6 0.4 collective-permute-start.14
  70.0 0.0 collective-permute-done.9
  70.0 0.4 collective-permute-done.10
  70.5 1.7 %collective-permute-done.12 = bf16[4,4,32,128]{3,2,1,0:T(8,128)(2,1)S(1)} collective-permute-done((bf16[4,4,32,128]{3,2,1,0:T(8,128)(2,1)S(1)}, bf16[4,4,32,128]{3,2,1,0:T(8,128)(2,1)S(1)}, u32[]{:S(2)}, u32[]{:S(2)}) %collective-permute-start.12) | collective-permute-done | bytes 131104 | tf_op jit(solution)/shard_map/ppermute | solution.py:339
  72.2 5.5 %collective-permute-done.14 = bf16[4,4,32,128]{3,2,1,0:T(8,128)(2,1)S(1)} collective-permute-done((bf16[4,4,32,128]{3,2,1,0:T(8,128)(2,1)S(1)}, bf16[4,4,32,128]{3,2,1,0:T(8,128)(2,1)S(1)}, u32[]{:S(2)}, u32[]{:S(2)}) %collective-permute-start.14) | collective-permute-done | bytes 131104 | tf_op jit(solution)/shard_map/ppermute | solution.py:339
  77.7 1.0 %pad_maximum_fusion = f32[4,16,32,128]{3,2,1,0:T(8,128)} fusion(f32[4,4,32,128]{3,2,1,0:T(8,128)S(1)} %add_multiply_fusion, f32[4,4,32,128]{3,2,1,0:T(8,128)S(1)} %add_multiply_fusion.1, f32[4,4,32,128]{3,2,1,0:T(8,128)S(1)} %add_multiply_fusion.2, f32[4,4,32,128]{3,2,1,0:T(8,128)S(1)} %add_multiply_fusion.3), kind=kLoop, calls=%fused_computation | loop fusion | flops 786432 | bytes 2097152 | tf_op jit(solution)/shard_map/concatenate | solution.py:414
  (6 shorter events, 0.2 us)
Async XLA Ops:
  0.1 16.4 %copy-start = (f32[2,4,256,128]{3,2,1,0:T(8,128)S(1)}, f32[2,4,256,128]{3,2,1,0:T(8,128)}, u32[]{:S(2)}) copy-start(f32[2,4,256,128]{3,2,1,0:T(8,128)} %constant.24.clone.dop_ref) | copy-start | bytes 3145732
  0.1 16.4 %copy-start.1 = (f32[2,4,192,128]{3,2,1,0:T(8,128)S(1)}, f32[2,4,192,128]{3,2,1,0:T(8,128)}, u32[]{:S(2)}) copy-start(f32[2,4,192,128]{3,2,1,0:T(8,128)} %constant.23.clone.lag_ref) | copy-start | bytes 2359300
  8.4 18.4 %copy-start.2 = (bf16[512,1024]{1,0:T(8,128)(2,1)S(1)}, bf16[512,1024]{1,0:T(8,128)(2,1)}, u32[]{:S(2)}) copy-start(bf16[512,1024]{1,0:T(8,128)(2,1)} %constant.26.clone.rtab) | copy-start | bytes 3145732
  8.4 18.4 %copy-start.3 = (bf16[512,256]{1,0:T(8,128)(2,1)S(1)}, bf16[512,256]{1,0:T(8,128)(2,1)}, u32[]{:S(2)}) copy-start(bf16[512,256]{1,0:T(8,128)(2,1)} %constant.25.clone.stab) | copy-start | bytes 786436
  8.4 1.5 %collective-permute-start = (bf16[2,256,128]{2,1,0:T(8,128)(2,1)S(1)}, bf16[2,256,128]{2,1,0:T(8,128)(2,1)S(1)}, u32[]{:S(2)}, u32[]{:S(2)}) collective-permute-start(bf16[2,256,128]{2,1,0:T(8,128)(2,1)S(1)} %get-tuple-element.42), channel_id=1, source_target_pairs={{0,4},{4,0},{8,12},{12,8},{16,20},{20,16},{24,28},{28,24},{1,5},{5... | collective-permute-start | bytes 393224 | tf_op jit(solution)/shard_map/ppermute | solution.py:339
  10.0 7.4 %collective-permute-start.1 = (bf16[2,256,128]{2,1,0:T(8,128)(2,1)S(1)}, bf16[2,256,128]{2,1,0:T(8,128)(2,1)S(1)}, u32[]{:S(2)}, u32[]{:S(2)}) collective-permute-start(bf16[2,256,128]{2,1,0:T(8,128)(2,1)S(1)} %add.24), channel_id=1, source_target_pairs={{0,8},{4,12},{8,0},{12,4},{16,24},{20,28},{24,16},{28,20},{1,9},{5... | collective-permute-start | bytes 393224 | tf_op jit(solution)/shard_map/ppermute | solution.py:339
  12.9 8.1 %collective-permute-start.2 = (bf16[2,256,128]{2,1,0:T(8,128)(2,1)S(1)}, bf16[2,256,128]{2,1,0:T(8,128)(2,1)S(1)}, u32[]{:S(2)}, u32[]{:S(2)}) collective-permute-start(bf16[2,256,128]{2,1,0:T(8,128)(2,1)S(1)} %add.24), channel_id=1, source_target_pairs={{0,16},{4,20},{8,24},{12,28},{16,0},{20,4},{24,8},{28,12},{1,17},{... | collective-permute-start | bytes 393224 | tf_op jit(solution)/shard_map/ppermute | solution.py:339
  14.4 6.6 %collective-permute-start.3 = (bf16[2,256,128]{2,1,0:T(8,128)(2,1)S(1)}, bf16[2,256,128]{2,1,0:T(8,128)(2,1)S(1)}, u32[]{:S(2)}, u32[]{:S(2)}) collective-permute-start(bf16[2,256,128]{2,1,0:T(8,128)(2,1)S(1)} %add.24), channel_id=1, source_target_pairs={{0,24},{4,28},{8,16},{12,20},{16,8},{20,12},{24,0},{28,4},{1,25},{... | collective-permute-start | bytes 393224 | tf_op jit(solution)/shard_map/ppermute | solution.py:339
  14.4 10.3 %collective-permute-start.4 = (bf16[4,256,128]{2,1,0:T(8,128)(2,1)S(1)}, bf16[4,256,128]{2,1,0:T(8,128)(2,1)S(1)}, u32[]{:S(2)}, u32[]{:S(2)}) collective-permute-start(bf16[4,256,128]{2,1,0:T(8,128)(2,1)S(1)} %get-tuple-element.55.s_ref), channel_id=1, source_target_pairs={{0,1},{1,0},{2,3},{3,2},{4,5},{5,4},{6,7},{7,6},{8,9},{9,8},{10,11... | collective-permute-start | bytes 786440 | tf_op jit(solution)/shard_map/ppermute | solution.py:339
  21.0 4.2 %collective-permute-start.6 = (bf16[2,256,128]{2,1,0:T(8,128)(2,1)S(1)}, bf16[2,256,128]{2,1,0:T(8,128)(2,1)S(1)}, u32[]{:S(2)}, u32[]{:S(2)}) collective-permute-start(bf16[2,256,128]{2,1,0:T(8,128)(2,1)S(1)} %add_add_fusion.mine), channel_id=1, source_target_pairs={{0,4},{4,0},{8,12},{12,8},{16,20},{20,16},{24,28},{28,24},{1,5},{5... | collective-permute-start | bytes 393224 | tf_op jit(solution)/shard_map/ppermute | solution.py:339
  21.1 9.9 %collective-permute-start.8 = (bf16[4,256,128]{2,1,0:T(8,128)(2,1)S(1)}, bf16[4,256,128]{2,1,0:T(8,128)(2,1)S(1)}, u32[]{:S(2)}, u32[]{:S(2)}) collective-permute-start(bf16[4,256,128]{2,1,0:T(8,128)(2,1)S(1)} %get-tuple-element.57.here), channel_id=1, source_target_pairs={{0,1},{1,0},{2,3},{3,2},{4,5},{5,4},{6,7},{7,6},{8,9},{9,8},{10,11... | collective-permute-start | bytes 786440 | tf_op jit(solution)/shard_map/ppermute | solution.py:339
  22.7 35.6 %collective-permute-start.11 = (bf16[4,256,128]{2,1,0:T(8,128)(2,1)S(1)}, bf16[4,256,128]{2,1,0:T(8,128)(2,1)S(1)}, u32[]{:S(2)}, u32[]{:S(2)}) collective-permute-start(bf16[4,256,128]{2,1,0:T(8,128)(2,1)S(1)} %get-tuple-element.71.here), channel_id=1, source_target_pairs={{0,1},{1,0},{2,3},{3,2},{4,5},{5,4},{6,7},{7,6},{8,9},{9,8},{10,11... | collective-permute-start | bytes 786440 | tf_op jit(solution)/shard_map/ppermute | solution.py:339
  23.2 42.1 %collective-permute-start.13 = (bf16[4,256,128]{2,1,0:T(8,128)(2,1)S(1)}, bf16[4,256,128]{2,1,0:T(8,128)(2,1)S(1)}, u32[]{:S(2)}, u32[]{:S(2)}) collective-permute-start(bf16[4,256,128]{2,1,0:T(8,128)(2,1)S(1)} %get-tuple-element.74.here), channel_id=1, source_target_pairs={{0,1},{1,0},{2,3},{3,2},{4,5},{5,4},{6,7},{7,6},{8,9},{9,8},{10,11... | collective-permute-start | bytes 786440 | tf_op jit(solution)/shard_map/ppermute | solution.py:339
  24.7 19.5 %collective-permute-start.5 = (bf16[2,256,128]{2,1,0:T(8,128)(2,1)S(1)}, bf16[2,256,128]{2,1,0:T(8,128)(2,1)S(1)}, u32[]{:S(2)}, u32[]{:S(2)}) collective-permute-start(bf16[2,256,128]{2,1,0:T(8,128)(2,1)S(1)} %add_add_fusion.mine), channel_id=1, source_target_pairs={{0,1},{1,0},{2,3},{3,2},{4,5},{5,4},{6,7},{7,6},{8,9},{9,8},{10,11... | collective-permute-start | bytes 393224 | tf_op jit(solution)/shard_map/ppermute | solution.py:339
  25.2 21.4 %collective-permute-start.7 = (bf16[2,256,128]{2,1,0:T(8,128)(2,1)S(1)}, bf16[2,256,128]{2,1,0:T(8,128)(2,1)S(1)}, u32[]{:S(2)}, u32[]{:S(2)}) collective-permute-start(bf16[2,256,128]{2,1,0:T(8,128)(2,1)S(1)} %collective-permute-done.6.other), channel_id=1, source_target_pairs={{0,1},{1,0},{2,3},{3,2},{4,5},{5,4},{6,7},{7,6},{8,9},{9,8},{10,11... | collective-permute-start | bytes 393224 | tf_op jit(solution)/shard_map/ppermute | solution.py:339
  50.8 19.2 %collective-permute-start.9 = (bf16[4,4,32,128]{3,2,1,0:T(8,128)(2,1)S(1)}, bf16[4,4,32,128]{3,2,1,0:T(8,128)(2,1)S(1)}, u32[]{:S(2)}, u32[]{:S(2)}) collective-permute-start(bf16[4,4,32,128]{3,2,1,0:T(8,128)(2,1)S(1)} %bitcast.9), channel_id=1, source_target_pairs={{0,2},{1,3},{2,0},{3,1},{4,6},{5,7},{6,4},{7,5},{8,10},{9,11},{10,... | collective-permute-start | bytes 393224 | tf_op jit(solution)/shard_map/ppermute | solution.py:339
  57.9 12.5 %collective-permute-start.10 = (bf16[4,4,32,128]{3,2,1,0:T(8,128)(2,1)S(1)}, bf16[4,4,32,128]{3,2,1,0:T(8,128)(2,1)S(1)}, u32[]{:S(2)}, u32[]{:S(2)}) collective-permute-start(bf16[4,4,32,128]{3,2,1,0:T(8,128)(2,1)S(1)} %bitcast.10), channel_id=1, source_target_pairs={{0,2},{1,3},{2,0},{3,1},{4,6},{5,7},{6,4},{7,5},{8,10},{9,11},{10,... | collective-permute-start | bytes 393224 | tf_op jit(solution)/shard_map/ppermute | solution.py:339
  62.6 9.5 %collective-permute-start.12 = (bf16[4,4,32,128]{3,2,1,0:T(8,128)(2,1)S(1)}, bf16[4,4,32,128]{3,2,1,0:T(8,128)(2,1)S(1)}, u32[]{:S(2)}, u32[]{:S(2)}) collective-permute-start(bf16[4,4,32,128]{3,2,1,0:T(8,128)(2,1)S(1)} %bitcast.11), channel_id=1, source_target_pairs={{0,2},{1,3},{2,0},{3,1},{4,6},{5,7},{6,4},{7,5},{8,10},{9,11},{10,... | collective-permute-start | bytes 393224 | tf_op jit(solution)/shard_map/ppermute | solution.py:339
  69.6 8.1 %collective-permute-start.14 = (bf16[4,4,32,128]{3,2,1,0:T(8,128)(2,1)S(1)}, bf16[4,4,32,128]{3,2,1,0:T(8,128)(2,1)S(1)}, u32[]{:S(2)}, u32[]{:S(2)}) collective-permute-start(bf16[4,4,32,128]{3,2,1,0:T(8,128)(2,1)S(1)} %bitcast.12), channel_id=1, source_target_pairs={{0,2},{1,3},{2,0},{3,1},{4,6},{5,7},{6,4},{7,5},{8,10},{9,11},{10,... | collective-permute-start | bytes 393224 | tf_op jit(solution)/shard_map/ppermute | solution.py:339

commit v3 on v2

--- a/solution.py
+++ b/solution.py
@@ -141,37 +141,41 @@
     params[2 * TX] = ids[0]
     params[2 * TX + 1] = ids[1]
 
-    for n in range(chunks):
-        copies[n].wait()
+    def step(n, _):
+        pltpu.make_async_copy(
+            volts.at[:, :, pl.ds(n * wide, wide)],
+            x.at[:, :, pl.ds(LEAD + n * wide, wide)],
+            sems.at[n],
+        ).wait()
         parts = []
         for c in range(2):
-            parts.append(
-                jnp.concatenate(
-                    [x[c, :, l * STRIDE : l * STRIDE + REACH] for l in range(n * rows, (n + 1) * rows)],
-                    axis=0,
-                )
-            )
+            starts = [pl.multiple_of(n * wide + l * STRIDE, STRIDE) for l in range(rows)]
+            parts.append(jnp.concatenate([x[c, :, pl.ds(at, REACH)] for at in starts], axis=0))
         out = dot(jnp.concatenate(parts, axis=1), band[...])
-        span = slice(n * rows * beams, (n + 1) * rows * beams)
+        span = pl.ds(pl.multiple_of(n * rows * beams, rows * beams), rows * beams)
         all_s[span] = out[:, :PAIR]
         all_r[span] = out[:, PAIR:]
+        count = beams // GROUPS
+        here = pl.ds(pl.multiple_of(n * rows, rows), rows)
+        for b in range(beams):
+            picked = all_s[pl.ds(n * rows * beams + b, rows, stride=beams), :]
+            s_refs[b // count][b % count, here] = picked.astype(jnp.bfloat16)
+        return 0
+
+    lax.fori_loop(0, chunks, step, 0)
     core = ids[0] % 2
     for ref, first_tx in ((keep_ref, core * HALF_TX), (send_ref, (1 - core) * HALF_TX)):
         for k in range(HALF_TX):
             beam = small[0, first_tx + k]
             picked = all_r[pl.ds(beam % beams, blocks, stride=beams), :]
             ref[k] = jnp.where(beam // beams == ids[0], picked, 0.0).astype(jnp.bfloat16)
-    count = beams // GROUPS
-    for b in range(beams):
-        picked = all_s[pl.ds(b, blocks, stride=beams), :]
-        s_refs[b // count][b % count] = picked.astype(jnp.bfloat16)
 
 
 def decimate(volts, staps, rtaps, ids, owner, delay, doppler):
     beams, raw = volts.shape[1:]
     blocks = raw // STRIDE
     count = beams // GROUPS
-    chunks = 4
+    chunks = 1
     arrays = (owner, delay, doppler, staps, rtaps, volts)
     shape = lambda n: jax.ShapeDtypeStruct((n, blocks, PAIR), jnp.bfloat16)
     return pl.pallas_call(
@@ -359,7 +363,7 @@
     half = keep + swap(send, "beam", 1)
     half, surv, params = lax.optimization_barrier((half, surv, params))
     got = [swap(half, "beam", flip) for flip in range(2, n_beam, 2)]
-    there = [swap(s, "seg", 1) for s in surv]
+    there = [swap(surv[0], "seg", 1)]
     lags, dops = make_tables(params, n_seg)
     got, lags, dops = lax.optimization_barrier((got, lags, dops))
     half = functools.reduce(jnp.add, got, half)
@@ -385,7 +389,8 @@
         1,
         True,
     )
-    far, far_other, there[1] = lax.optimization_barrier((far, far_other, there[1]))
+    surv, part = lax.optimization_barrier((surv, part))
+    there += [swap(s, "seg", 1) for s in surv[1:]]
     r_there, *sums = call_powers(
         functools.partial(second_kernel, n_seg),
         "second",

time: 78.9 us -> 65.2 us (0.83)
  waiting for transfers between devices: 27.9 us -> 15 us
  Pallas kernels: 30.5 us -> 28.1 us
  starting transfers between devices: 18.9 us -> 20.5 us
    ppermute x15, waiting for transfers between devices: 27.9 us -> 15 us  [swap(): return lax.ppermute(value, axis, [(i, i ^ flip) for i in range(size)])]
    pallas_call x1, Pallas kernels: 8.29 us -> 5.88 us  [decimate(): pl.pallas_call(functools.partial(decimate_kernel, beams), in_specs=[SMEM]...]
    ppermute x15, starting transfers between devices: 18.9 us -> 20.5 us  [swap(): return lax.ppermute(value, axis, [(i, i ^ flip) for i in range(size)])]
  transfers between devices with their start and end apart: 15 -> 15, of which waited for: 7 -> 6; matrix products, arithmetic and copies ran while one was open for 0% -> 0% of each run, Pallas kernels for 28% -> 34%
where the time goes in v3:
time: 65.2 us; the launch traced here: 65 us
  Pallas kernels  28.1 us (43%)
  starting transfers between devices  20.5 us (31%)
  waiting for transfers between devices  15 us (23%)
  other arithmetic  1.31 us (2%)
    pallas_call x5, Pallas kernels, call_powers(): pl.pallas_call(kernel, in_specs=[SMEM if a.ndim == 1 else VMEM for a in a...  21.3 us
    ppermute x15, starting transfers between devices, swap(): return lax.ppermute(value, axis, [(i, i ^ flip) for i in range(size)])  20.5 us
    ppermute x15, waiting for transfers between devices, swap(): return lax.ppermute(value, axis, [(i, i ^ flip) for i in range(size)])  15 us
    pallas_call x1, Pallas kernels, decimate(): pl.pallas_call(functools.partial(decimate_kernel, beams), in_specs=[SMEM]...  5.88 us
  transfers between devices with their start and end apart: 15, of which 6 were waited for; matrix products, arithmetic and copies ran while one was open for 0% of the time, Pallas kernels for 34%

profile of v3, /device:TPU:0, one launch (start us, length us, event | category | flops | bytes accessed | tf_op | source)
XLA Modules:
  0.0 65.0 jit_solution(4990119065379393104)
XLA Ops:
  0.0 0.1 pad_add_fusion.ids
  0.1 0.0 copy-start
  0.1 0.0 copy-start.1
  0.1 5.9 %decimate.1 = (bf16[4,256,128]{2,1,0:T(8,128)(2,1)S(1)}, bf16[4,256,128]{2,1,0:T(8,128)(2,1)S(1)}, bf16[4,256,128]{2,1,0:T(8,128)(2,1)S(1)}, bf16[4,256,128]{2,1...) custom-call(s32[2]{0:T(128)S(1)} %pad_add_fusion.ids, ...), custom_call_target="tpu_custom_call" | custom-call | tf_op jit(solution)/shard_map/decimate/pallas_call | solution.py:181
  6.0 0.0 copy-start.2
  6.0 0.0 copy-start.3
  6.0 0.5 collective-permute-start
  6.5 1.0 %collective-permute-done = bf16[2,256,128]{2,1,0:T(8,128)(2,1)S(1)} collective-permute-done((bf16[2,256,128]{2,1,0:T(8,128)(2,1)S(1)}, bf16[2,256,128]{2,1,0:T(8,128)(2,1)S(1)}, u32[]{:S(2)}, u32[]{:S(2)}) %collective-permute-start) | collective-permute-done | bytes 131104 | tf_op jit(solution)/shard_map/ppermute | solution.py:343
  7.5 2.9 %collective-permute-start.1 = (bf16[2,256,128]{2,1,0:T(8,128)(2,1)S(1)}, bf16[2,256,128]{2,1,0:T(8,128)(2,1)S(1)}, u32[]{:S(2)}, u32[]{:S(2)}) collective-permute-start(bf16[2,256,128]{2,1,0:T(8,128)(2,1)S(1)} %add.24), channel_id=1, source_target_pairs={{0,8},{4,12},{8,0},{12,4},{16,24},{20,28},{24,16},{28,20},{1,9},{5... | collective-permute-start | bytes 393224 | tf_op jit(solution)/shard_map/ppermute | solution.py:343
  10.5 1.5 %collective-permute-start.2 = (bf16[2,256,128]{2,1,0:T(8,128)(2,1)S(1)}, bf16[2,256,128]{2,1,0:T(8,128)(2,1)S(1)}, u32[]{:S(2)}, u32[]{:S(2)}) collective-permute-start(bf16[2,256,128]{2,1,0:T(8,128)(2,1)S(1)} %add.24), channel_id=1, source_target_pairs={{0,16},{4,20},{8,24},{12,28},{16,0},{20,4},{24,8},{28,12},{1,17},{... | collective-permute-start | bytes 393224 | tf_op jit(solution)/shard_map/ppermute | solution.py:343
  12.0 0.0 collective-permute-start.3
  12.0 2.0 %collective-permute-start.4 = (bf16[4,256,128]{2,1,0:T(8,128)(2,1)S(1)}, bf16[4,256,128]{2,1,0:T(8,128)(2,1)S(1)}, u32[]{:S(2)}, u32[]{:S(2)}) collective-permute-start(bf16[4,256,128]{2,1,0:T(8,128)(2,1)S(1)} %get-tuple-element.56.s_ref), channel_id=1, source_target_pairs={{0,1},{1,0},{2,3},{3,2},{4,5},{5,4},{6,7},{7,6},{8,9},{9,8},{10,11... | collective-permute-start | bytes 786440 | tf_op jit(solution)/shard_map/ppermute | solution.py:343
  14.0 0.0 copy-done
  14.0 0.0 copy-done.1
  14.0 0.9 %tables.1 = (bf16[4,128,512]{2,1,0:T(8,128)(2,1)S(1)}, bf16[4,512,256]{2,1,0:T(8,128)(2,1)S(1)}) custom-call(s32[10]{0:T(128)S(1)} %get-tuple-element.49.params, f32[2,4,192,128]{3,2,1,0:T(8,128)S(1)} %copy-done.1, f32[2,4,256,128]{3,2,1,0:T(8,128)S(1)} %copy-done), custom_call_target="tpu_custom_call" | custom-call | tf_op jit(solution)/shard_map/tables/pallas_call | solution.py:220
  15.0 0.0 collective-permute-done.1
  15.0 3.6 %collective-permute-done.2 = bf16[2,256,128]{2,1,0:T(8,128)(2,1)S(1)} collective-permute-done((bf16[2,256,128]{2,1,0:T(8,128)(2,1)S(1)}, bf16[2,256,128]{2,1,0:T(8,128)(2,1)S(1)}, u32[]{:S(2)}, u32[]{:S(2)}) %collective-permute-start.2) | collective-permute-done | bytes 131104 | tf_op jit(solution)/shard_map/ppermute | solution.py:343
  18.5 0.0 collective-permute-done.3
  18.6 0.1 collective-permute-start.6
  18.7 1.1 %collective-permute-done.4.s_ref = bf16[4,256,128]{2,1,0:T(8,128)(2,1)S(1)} collective-permute-done((bf16[4,256,128]{2,1,0:T(8,128)(2,1)S(1)}, bf16[4,256,128]{2,1,0:T(8,128)(2,1)S(1)}, u32[]{:S(2)}, u32[]{:S(2)}) %collective-permute-start.4) | collective-permute-done | bytes 262176 | tf_op jit(solution)/shard_map/ppermute | solution.py:343
  19.8 1.7 %collective-permute-start.5 = (bf16[2,256,128]{2,1,0:T(8,128)(2,1)S(1)}, bf16[2,256,128]{2,1,0:T(8,128)(2,1)S(1)}, u32[]{:S(2)}, u32[]{:S(2)}) collective-permute-start(bf16[2,256,128]{2,1,0:T(8,128)(2,1)S(1)} %add_add_fusion.mine), channel_id=1, source_target_pairs={{0,1},{1,0},{2,3},{3,2},{4,5},{5,4},{6,7},{7,6},{8,9},{9,8},{10,11... | collective-permute-start | bytes 393224 | tf_op jit(solution)/shard_map/ppermute | solution.py:343
  21.6 0.0 collective-permute-done.6.other
  21.6 0.3 collective-permute-start.7
  21.8 0.0 copy-done.2
  21.8 0.0 copy-done.3
  21.8 4.1 %first.1 = (f32[4,512,256]{2,1,0:T(8,128)S(1)}, f32[4,4,64,128]{3,2,1,0:T(8,128)S(1)}) custom-call(s32[10]{0:T(128)S(1)} %get-tuple-element.49.params, bf16[512,1024]{1,0:T(8,128)(2,1)S(1)} %copy-done.2, bf16[2,256,128]{2,1,0:T(8,128)(2,1)S(1)} %add_add_fusion.mine, bf16[2,256,128]{2,1,0:T(8,128)(2,1)S(1)} %collective-permute-done.6.other, ...), custom_call_target="tpu_custom_call" | custom-call | flops 3221225472 | bytes 6291456 | tf_op jit(solution)/shard_map/first/pallas_call | solution.py:322
  26.0 1.8 %collective-permute-start.9 = (bf16[4,256,128]{2,1,0:T(8,128)(2,1)S(1)}, bf16[4,256,128]{2,1,0:T(8,128)(2,1)S(1)}, u32[]{:S(2)}, u32[]{:S(2)}) collective-permute-start(bf16[4,256,128]{2,1,0:T(8,128)(2,1)S(1)} %get-tuple-element.68.here), channel_id=1, source_target_pairs={{0,1},{1,0},{2,3},{3,2},{4,5},{5,4},{6,7},{7,6},{8,9},{9,8},{10,11... | collective-permute-start | bytes 786440 | tf_op jit(solution)/shard_map/ppermute | solution.py:343
  27.8 0.3 collective-permute-start.11
  28.1 1.7 %collective-permute-start.13 = (bf16[4,256,128]{2,1,0:T(8,128)(2,1)S(1)}, bf16[4,256,128]{2,1,0:T(8,128)(2,1)S(1)}, u32[]{:S(2)}, u32[]{:S(2)}) collective-permute-start(bf16[4,256,128]{2,1,0:T(8,128)(2,1)S(1)} %get-tuple-element.76.here), channel_id=1, source_target_pairs={{0,1},{1,0},{2,3},{3,2},{4,5},{5,4},{6,7},{7,6},{8,9},{9,8},{10,11... | collective-permute-start | bytes 786440 | tf_op jit(solution)/shard_map/ppermute | solution.py:343
  29.8 0.0 collective-permute-done.5.mine
  29.8 0.0 collective-permute-done.7.other
  29.8 4.1 %second.1 = (f32[4,512,256]{2,1,0:T(8,128)S(1)}, f32[4,4,32,128]{3,2,1,0:T(8,128)S(1)}, bf16[1,4,4,32,128]{4,3,2,1,0:T(8,128)(2,1)S(1)}) custom-call(s32[10]{0:T(128)S(1)} %get-tuple-element.49.params, bf16[512,1024]{1,0:T(8,128)(2,1)S(1)} %copy-done.2, bf16[2,256,128]{2,1,0:T(8,128)(2,1)S(1)} %collective-permute-done.5.mine, ...), custom_call_target="tpu_custom_call" | custom-call | flops 3221225472 | bytes 6291456 | tf_op jit(solution)/shard_map/second/pallas_call | solution.py:322
  34.0 2.7 %collective-permute-start.8 = (bf16[4,4,32,128]{3,2,1,0:T(8,128)(2,1)S(1)}, bf16[4,4,32,128]{3,2,1,0:T(8,128)(2,1)S(1)}, u32[]{:S(2)}, u32[]{:S(2)}) collective-permute-start(bf16[4,4,32,128]{3,2,1,0:T(8,128)(2,1)S(1)} %bitcast.9), channel_id=1, source_target_pairs={{0,2},{1,3},{2,0},{3,1},{4,6},{5,7},{6,4},{7,5},{8,10},{9,11},{10,... | collective-permute-start | bytes 393224 | tf_op jit(solution)/shard_map/ppermute | solution.py:343
  36.6 0.0 collective-permute-done.9.there
  36.6 4.5 %both.3 = (f32[4,4,32,128]{3,2,1,0:T(8,128)S(1)}, bf16[1,4,4,32,128]{4,3,2,1,0:T(8,128)(2,1)S(1)}) custom-call(bf16[512,256]{1,0:T(8,128)(2,1)S(1)} %copy-done.3, bf16[4,256,128]{2,1,0:T(8,128)(2,1)S(1)} %get-tuple-element.68.here, bf16[4,256,128]{2,1,0:T(8,128)(2,1)S(1)} %collective-permute-done.9.there, f32[4,512,256]{2,1,0:T(8,128)S(1)} %get-tuple-element.69.r_here, ...), custom_call_target="tpu_custom_call" | custom-call | flops 6442450944 | bytes 6291456 | tf_op jit(solution)/shard_map/both/pallas_call | solution.py:322
  41.1 1.8 %collective-permute-start.10 = (bf16[4,4,32,128]{3,2,1,0:T(8,128)(2,1)S(1)}, bf16[4,4,32,128]{3,2,1,0:T(8,128)(2,1)S(1)}, u32[]{:S(2)}, u32[]{:S(2)}) collective-permute-start(bf16[4,4,32,128]{3,2,1,0:T(8,128)(2,1)S(1)} %bitcast.10), channel_id=1, source_target_pairs={{0,2},{1,3},{2,0},{3,1},{4,6},{5,7},{6,4},{7,5},{8,10},{9,11},{10,... | collective-permute-start | bytes 393224 | tf_op jit(solution)/shard_map/ppermute | solution.py:343
  42.9 2.2 %collective-permute-done.11.there = bf16[4,256,128]{2,1,0:T(8,128)(2,1)S(1)} collective-permute-done((bf16[4,256,128]{2,1,0:T(8,128)(2,1)S(1)}, bf16[4,256,128]{2,1,0:T(8,128)(2,1)S(1)}, u32[]{:S(2)}, u32[]{:S(2)}) %collective-permute-start.11) | collective-permute-done | bytes 262176 | tf_op jit(solution)/shard_map/ppermute | solution.py:343
  45.1 4.3 %both.4 = (f32[4,4,32,128]{3,2,1,0:T(8,128)S(1)}, bf16[1,4,4,32,128]{4,3,2,1,0:T(8,128)(2,1)S(1)}) custom-call(bf16[512,256]{1,0:T(8,128)(2,1)S(1)} %copy-done.3, bf16[4,256,128]{2,1,0:T(8,128)(2,1)S(1)} %get-tuple-element.73.here, bf16[4,256,128]{2,1,0:T(8,128)(2,1)S(1)} %collective-permute-done.11.there, f32[4,512,256]{2,1,0:T(8,128)S(1)} %get-tuple-element.69.r_here, ...), custom_call_target="tpu_custom_call" | custom-call | flops 6442450944 | bytes 6291456 | tf_op jit(solution)/shard_map/both/pallas_call | solution.py:322
  49.4 1.9 %collective-permute-start.12 = (bf16[4,4,32,128]{3,2,1,0:T(8,128)(2,1)S(1)}, bf16[4,4,32,128]{3,2,1,0:T(8,128)(2,1)S(1)}, u32[]{:S(2)}, u32[]{:S(2)}) collective-permute-start(bf16[4,4,32,128]{3,2,1,0:T(8,128)(2,1)S(1)} %bitcast.11), channel_id=1, source_target_pairs={{0,2},{1,3},{2,0},{3,1},{4,6},{5,7},{6,4},{7,5},{8,10},{9,11},{10,... | collective-permute-start | bytes 393224 | tf_op jit(solution)/shard_map/ppermute | solution.py:343
  51.3 0.0 collective-permute-done.13.there
  51.3 4.3 %both.5 = (f32[4,4,32,128]{3,2,1,0:T(8,128)S(1)}, bf16[1,4,4,32,128]{4,3,2,1,0:T(8,128)(2,1)S(1)}) custom-call(bf16[512,256]{1,0:T(8,128)(2,1)S(1)} %copy-done.3, bf16[4,256,128]{2,1,0:T(8,128)(2,1)S(1)} %get-tuple-element.76.here, bf16[4,256,128]{2,1,0:T(8,128)(2,1)S(1)} %collective-permute-done.13.there, f32[4,512,256]{2,1,0:T(8,128)S(1)} %get-tuple-element.69.r_here, ...), custom_call_target="tpu_custom_call" | custom-call | flops 6442450944 | bytes 6291456 | tf_op jit(solution)/shard_map/both/pallas_call | solution.py:322
  55.6 1.1 %collective-permute-start.14 = (bf16[4,4,32,128]{3,2,1,0:T(8,128)(2,1)S(1)}, bf16[4,4,32,128]{3,2,1,0:T(8,128)(2,1)S(1)}, u32[]{:S(2)}, u32[]{:S(2)}) collective-permute-start(bf16[4,4,32,128]{3,2,1,0:T(8,128)(2,1)S(1)} %bitcast.12), channel_id=1, source_target_pairs={{0,2},{1,3},{2,0},{3,1},{4,6},{5,7},{6,4},{7,5},{8,10},{9,11},{10,... | collective-permute-start | bytes 393224 | tf_op jit(solution)/shard_map/ppermute | solution.py:343
  56.7 0.0 collective-permute-done.8
  56.8 0.0 collective-permute-done.10
  56.8 3.0 %collective-permute-done.12 = bf16[4,4,32,128]{3,2,1,0:T(8,128)(2,1)S(1)} collective-permute-done((bf16[4,4,32,128]{3,2,1,0:T(8,128)(2,1)S(1)}, bf16[4,4,32,128]{3,2,1,0:T(8,128)(2,1)S(1)}, u32[]{:S(2)}, u32[]{:S(2)}) %collective-permute-start.12) | collective-permute-done | bytes 131104 | tf_op jit(solution)/shard_map/ppermute | solution.py:343
  59.9 4.1 %collective-permute-done.14 = bf16[4,4,32,128]{3,2,1,0:T(8,128)(2,1)S(1)} collective-permute-done((bf16[4,4,32,128]{3,2,1,0:T(8,128)(2,1)S(1)}, bf16[4,4,32,128]{3,2,1,0:T(8,128)(2,1)S(1)}, u32[]{:S(2)}, u32[]{:S(2)}) %collective-permute-start.14) | collective-permute-done | bytes 131104 | tf_op jit(solution)/shard_map/ppermute | solution.py:343
  64.0 1.0 %pad_maximum_fusion = f32[4,16,32,128]{3,2,1,0:T(8,128)} fusion(f32[4,4,32,128]{3,2,1,0:T(8,128)S(1)} %add_multiply_fusion, f32[4,4,32,128]{3,2,1,0:T(8,128)S(1)} %add_multiply_fusion.1, f32[4,4,32,128]{3,2,1,0:T(8,128)S(1)} %add_multiply_fusion.2, f32[4,4,32,128]{3,2,1,0:T(8,128)S(1)} %add_multiply_fusion.3), kind=kLoop, calls=%fused_computation | loop fusion | flops 786432 | bytes 2097152 | tf_op jit(solution)/shard_map/concatenate | solution.py:419
  (6 shorter events, 0.2 us)
Async XLA Ops:
  0.1 14.0 %copy-start = (f32[2,4,256,128]{3,2,1,0:T(8,128)S(1)}, f32[2,4,256,128]{3,2,1,0:T(8,128)}, u32[]{:S(2)}) copy-start(f32[2,4,256,128]{3,2,1,0:T(8,128)} %constant.24.clone.dop_ref) | copy-start | bytes 3145732
  0.1 14.0 %copy-start.1 = (f32[2,4,192,128]{3,2,1,0:T(8,128)S(1)}, f32[2,4,192,128]{3,2,1,0:T(8,128)}, u32[]{:S(2)}) copy-start(f32[2,4,192,128]{3,2,1,0:T(8,128)} %constant.23.clone.lag_ref) | copy-start | bytes 2359300
  6.0 15.9 %copy-start.2 = (bf16[512,1024]{1,0:T(8,128)(2,1)S(1)}, bf16[512,1024]{1,0:T(8,128)(2,1)}, u32[]{:S(2)}) copy-start(bf16[512,1024]{1,0:T(8,128)(2,1)} %constant.26.clone.rtab) | copy-start | bytes 3145732
  6.0 15.9 %copy-start.3 = (bf16[512,256]{1,0:T(8,128)(2,1)S(1)}, bf16[512,256]{1,0:T(8,128)(2,1)}, u32[]{:S(2)}) copy-start(bf16[512,256]{1,0:T(8,128)(2,1)} %constant.25.clone.stab) | copy-start | bytes 786436
  6.0 1.5 %collective-permute-start = (bf16[2,256,128]{2,1,0:T(8,128)(2,1)S(1)}, bf16[2,256,128]{2,1,0:T(8,128)(2,1)S(1)}, u32[]{:S(2)}, u32[]{:S(2)}) collective-permute-start(bf16[2,256,128]{2,1,0:T(8,128)(2,1)S(1)} %get-tuple-element.43), channel_id=1, source_target_pairs={{0,4},{4,0},{8,12},{12,8},{16,20},{20,16},{24,28},{28,24},{1,5},{5... | collective-permute-start | bytes 393224 | tf_op jit(solution)/shard_map/ppermute | solution.py:343
  7.5 7.4 %collective-permute-start.1 = (bf16[2,256,128]{2,1,0:T(8,128)(2,1)S(1)}, bf16[2,256,128]{2,1,0:T(8,128)(2,1)S(1)}, u32[]{:S(2)}, u32[]{:S(2)}) collective-permute-start(bf16[2,256,128]{2,1,0:T(8,128)(2,1)S(1)} %add.24), channel_id=1, source_target_pairs={{0,8},{4,12},{8,0},{12,4},{16,24},{20,28},{24,16},{28,20},{1,9},{5... | collective-permute-start | bytes 393224 | tf_op jit(solution)/shard_map/ppermute | solution.py:343
  10.5 8.1 %collective-permute-start.2 = (bf16[2,256,128]{2,1,0:T(8,128)(2,1)S(1)}, bf16[2,256,128]{2,1,0:T(8,128)(2,1)S(1)}, u32[]{:S(2)}, u32[]{:S(2)}) collective-permute-start(bf16[2,256,128]{2,1,0:T(8,128)(2,1)S(1)} %add.24), channel_id=1, source_target_pairs={{0,16},{4,20},{8,24},{12,28},{16,0},{20,4},{24,8},{28,12},{1,17},{... | collective-permute-start | bytes 393224 | tf_op jit(solution)/shard_map/ppermute | solution.py:343
  12.0 6.6 %collective-permute-start.3 = (bf16[2,256,128]{2,1,0:T(8,128)(2,1)S(1)}, bf16[2,256,128]{2,1,0:T(8,128)(2,1)S(1)}, u32[]{:S(2)}, u32[]{:S(2)}) collective-permute-start(bf16[2,256,128]{2,1,0:T(8,128)(2,1)S(1)} %add.24), channel_id=1, source_target_pairs={{0,24},{4,28},{8,16},{12,20},{16,8},{20,12},{24,0},{28,4},{1,25},{... | collective-permute-start | bytes 393224 | tf_op jit(solution)/shard_map/ppermute | solution.py:343
  12.0 7.8 %collective-permute-start.4 = (bf16[4,256,128]{2,1,0:T(8,128)(2,1)S(1)}, bf16[4,256,128]{2,1,0:T(8,128)(2,1)S(1)}, u32[]{:S(2)}, u32[]{:S(2)}) collective-permute-start(bf16[4,256,128]{2,1,0:T(8,128)(2,1)S(1)} %get-tuple-element.56.s_ref), channel_id=1, source_target_pairs={{0,1},{1,0},{2,3},{3,2},{4,5},{5,4},{6,7},{7,6},{8,9},{9,8},{10,11... | collective-permute-start | bytes 786440 | tf_op jit(solution)/shard_map/ppermute | solution.py:343
  18.6 3.0 %collective-permute-start.6 = (bf16[2,256,128]{2,1,0:T(8,128)(2,1)S(1)}, bf16[2,256,128]{2,1,0:T(8,128)(2,1)S(1)}, u32[]{:S(2)}, u32[]{:S(2)}) collective-permute-start(bf16[2,256,128]{2,1,0:T(8,128)(2,1)S(1)} %add_add_fusion.mine), channel_id=1, source_target_pairs={{0,4},{4,0},{8,12},{12,8},{16,20},{20,16},{24,28},{28,24},{1,5},{5... | collective-permute-start | bytes 393224 | tf_op jit(solution)/shard_map/ppermute | solution.py:343
  19.8 10.0 %collective-permute-start.5 = (bf16[2,256,128]{2,1,0:T(8,128)(2,1)S(1)}, bf16[2,256,128]{2,1,0:T(8,128)(2,1)S(1)}, u32[]{:S(2)}, u32[]{:S(2)}) collective-permute-start(bf16[2,256,128]{2,1,0:T(8,128)(2,1)S(1)} %add_add_fusion.mine), channel_id=1, source_target_pairs={{0,1},{1,0},{2,3},{3,2},{4,5},{5,4},{6,7},{7,6},{8,9},{9,8},{10,11... | collective-permute-start | bytes 393224 | tf_op jit(solution)/shard_map/ppermute | solution.py:343
  21.6 8.3 %collective-permute-start.7 = (bf16[2,256,128]{2,1,0:T(8,128)(2,1)S(1)}, bf16[2,256,128]{2,1,0:T(8,128)(2,1)S(1)}, u32[]{:S(2)}, u32[]{:S(2)}) collective-permute-start(bf16[2,256,128]{2,1,0:T(8,128)(2,1)S(1)} %collective-permute-done.6.other), channel_id=1, source_target_pairs={{0,1},{1,0},{2,3},{3,2},{4,5},{5,4},{6,7},{7,6},{8,9},{9,8},{10,11... | collective-permute-start | bytes 393224 | tf_op jit(solution)/shard_map/ppermute | solution.py:343
  26.0 10.6 %collective-permute-start.9 = (bf16[4,256,128]{2,1,0:T(8,128)(2,1)S(1)}, bf16[4,256,128]{2,1,0:T(8,128)(2,1)S(1)}, u32[]{:S(2)}, u32[]{:S(2)}) collective-permute-start(bf16[4,256,128]{2,1,0:T(8,128)(2,1)S(1)} %get-tuple-element.68.here), channel_id=1, source_target_pairs={{0,1},{1,0},{2,3},{3,2},{4,5},{5,4},{6,7},{7,6},{8,9},{9,8},{10,11... | collective-permute-start | bytes 786440 | tf_op jit(solution)/shard_map/ppermute | solution.py:343
  27.8 17.3 %collective-permute-start.11 = (bf16[4,256,128]{2,1,0:T(8,128)(2,1)S(1)}, bf16[4,256,128]{2,1,0:T(8,128)(2,1)S(1)}, u32[]{:S(2)}, u32[]{:S(2)}) collective-permute-start(bf16[4,256,128]{2,1,0:T(8,128)(2,1)S(1)} %get-tuple-element.73.here), channel_id=1, source_target_pairs={{0,1},{1,0},{2,3},{3,2},{4,5},{5,4},{6,7},{7,6},{8,9},{9,8},{10,11... | collective-permute-start | bytes 786440 | tf_op jit(solution)/shard_map/ppermute | solution.py:343
  28.1 23.3 %collective-permute-start.13 = (bf16[4,256,128]{2,1,0:T(8,128)(2,1)S(1)}, bf16[4,256,128]{2,1,0:T(8,128)(2,1)S(1)}, u32[]{:S(2)}, u32[]{:S(2)}) collective-permute-start(bf16[4,256,128]{2,1,0:T(8,128)(2,1)S(1)} %get-tuple-element.76.here), channel_id=1, source_target_pairs={{0,1},{1,0},{2,3},{3,2},{4,5},{5,4},{6,7},{7,6},{8,9},{9,8},{10,11... | collective-permute-start | bytes 786440 | tf_op jit(solution)/shard_map/ppermute | solution.py:343
  34.0 22.8 %collective-permute-start.8 = (bf16[4,4,32,128]{3,2,1,0:T(8,128)(2,1)S(1)}, bf16[4,4,32,128]{3,2,1,0:T(8,128)(2,1)S(1)}, u32[]{:S(2)}, u32[]{:S(2)}) collective-permute-start(bf16[4,4,32,128]{3,2,1,0:T(8,128)(2,1)S(1)} %bitcast.9), channel_id=1, source_target_pairs={{0,2},{1,3},{2,0},{3,1},{4,6},{5,7},{6,4},{7,5},{8,10},{9,11},{10,... | collective-permute-start | bytes 393224 | tf_op jit(solution)/shard_map/ppermute | solution.py:343
  41.1 15.7 %collective-permute-start.10 = (bf16[4,4,32,128]{3,2,1,0:T(8,128)(2,1)S(1)}, bf16[4,4,32,128]{3,2,1,0:T(8,128)(2,1)S(1)}, u32[]{:S(2)}, u32[]{:S(2)}) collective-permute-start(bf16[4,4,32,128]{3,2,1,0:T(8,128)(2,1)S(1)} %bitcast.10), channel_id=1, source_target_pairs={{0,2},{1,3},{2,0},{3,1},{4,6},{5,7},{6,4},{7,5},{8,10},{9,11},{10,... | collective-permute-start | bytes 393224 | tf_op jit(solution)/shard_map/ppermute | solution.py:343
  49.4 10.5 %collective-permute-start.12 = (bf16[4,4,32,128]{3,2,1,0:T(8,128)(2,1)S(1)}, bf16[4,4,32,128]{3,2,1,0:T(8,128)(2,1)S(1)}, u32[]{:S(2)}, u32[]{:S(2)}) collective-permute-start(bf16[4,4,32,128]{3,2,1,0:T(8,128)(2,1)S(1)} %bitcast.11), channel_id=1, source_target_pairs={{0,2},{1,3},{2,0},{3,1},{4,6},{5,7},{6,4},{7,5},{8,10},{9,11},{10,... | collective-permute-start | bytes 393224 | tf_op jit(solution)/shard_map/ppermute | solution.py:343
  55.6 8.3 %collective-permute-start.14 = (bf16[4,4,32,128]{3,2,1,0:T(8,128)(2,1)S(1)}, bf16[4,4,32,128]{3,2,1,0:T(8,128)(2,1)S(1)}, u32[]{:S(2)}, u32[]{:S(2)}) collective-permute-start(bf16[4,4,32,128]{3,2,1,0:T(8,128)(2,1)S(1)} %bitcast.12), channel_id=1, source_target_pairs={{0,2},{1,3},{2,0},{3,1},{4,6},{5,7},{6,4},{7,5},{8,10},{9,11},{10,... | collective-permute-start | bytes 393224 | tf_op jit(solution)/shard_map/ppermute | solution.py:343

commit v4 on v3

--- a/solution.py
+++ b/solution.py
@@ -22,10 +22,9 @@
 LEAD = 128
 REACH = LEAD + STRIDE
 PAIR = 2 * BLOCK_LEN
-GROUPS = 4
+GROUPS = (4, 4)
 LANES = 128
 LANE_BLOCKS = 2 * FFT // LANES
-HALF_DELAYS = DELAYS // 2
 VMEM_LIMIT = 24 * 1024 * 1024
 
 SMEM = pl.BlockSpec(memory_space=pltpu.SMEM)
@@ -90,8 +89,7 @@
 
 
 def decimate_kernel(beams, ids, owner, delay, doppler, staps, rtaps, volts, *refs):
-    s_refs, refs = refs[:GROUPS], refs[GROUPS:]
-    keep_ref, send_ref, params, x, taps, small, band, all_s, all_r, sems, small_sems = refs
+    here_ref, give_ref, keep_ref, send_ref, params, x, taps, small, band, all_s, all_r, sems, small_sems = refs
     chunks = sems.shape[0]
     raw = volts.shape[2]
     wide = raw // chunks
@@ -155,11 +153,13 @@
         span = pl.ds(pl.multiple_of(n * rows * beams, rows * beams), rows * beams)
         all_s[span] = out[:, :PAIR]
         all_r[span] = out[:, PAIR:]
-        count = beams // GROUPS
         here = pl.ds(pl.multiple_of(n * rows, rows), rows)
-        for b in range(beams):
-            picked = all_s[pl.ds(n * rows * beams + b, rows, stride=beams), :]
-            s_refs[b // count][b % count, here] = picked.astype(jnp.bfloat16)
+        part = ids[1] % 2
+        half = beams // 2
+        for s_ref, at in ((here_ref, part * half), (give_ref, (1 - part) * half)):
+            for b in range(half):
+                picked = all_s[pl.ds(n * rows * beams + at + b, rows, stride=beams), :]
+                s_ref[b, here] = picked.astype(jnp.bfloat16)
         return 0
 
     lax.fori_loop(0, chunks, step, 0)
@@ -174,15 +174,14 @@
 def decimate(volts, staps, rtaps, ids, owner, delay, doppler):
     beams, raw = volts.shape[1:]
     blocks = raw // STRIDE
-    count = beams // GROUPS
     chunks = 1
     arrays = (owner, delay, doppler, staps, rtaps, volts)
     shape = lambda n: jax.ShapeDtypeStruct((n, blocks, PAIR), jnp.bfloat16)
     return pl.pallas_call(
         functools.partial(decimate_kernel, beams),
         in_specs=[SMEM] + [HBM] * 6,
-        out_specs=[VMEM] * (GROUPS + 2) + [SMEM],
-        out_shape=[shape(count)] * GROUPS
+        out_specs=[VMEM] * 4 + [SMEM],
+        out_shape=[shape(beams // 2)] * 2
         + [shape(HALF_TX)] * 2
         + [jax.ShapeDtypeStruct((2 * TX + 2,), jnp.int32)],
         scratch_shapes=[
@@ -205,9 +204,9 @@
     for k in range(TX):
         base = (params[k] + DELAYS - 1) % BLOCK_LEN
         for part in range(2):
-            for n in range(chunks // 2):
-                chunk = params[2 * TX + 1] ^ (2 * n)
-                at = part * HALF_DELAYS + n * each
+            for n in range(chunks):
+                chunk = params[2 * TX + 1] ^ n
+                at = part * DELAYS + n * each
                 for q in range(LANE_BLOCKS):
                     picked = lag_ref[part, q, pl.ds(base + chunk * each, each), :]
                     lags[k, at : at + each, q * LANES : (q + 1) * LANES] = picked.astype(jnp.bfloat16)
@@ -222,7 +221,7 @@
         in_specs=[SMEM, VMEM, VMEM],
         out_specs=[VMEM, VMEM],
         out_shape=[
-            jax.ShapeDtypeStruct((TX, DELAYS, 2 * FFT), jnp.bfloat16),
+            jax.ShapeDtypeStruct((TX, 2 * DELAYS, 2 * FFT), jnp.bfloat16),
             jax.ShapeDtypeStruct((TX, 2 * BLOCKS, 2 * DOPPLER), jnp.bfloat16),
         ],
         compiler_params=pltpu.CompilerParams(vmem_limit_bytes=VMEM_LIMIT),
@@ -248,91 +247,128 @@
         out_ref[k] = nt_dot(table_ref[...], jnp.concatenate([window, window], axis=1))
 
 
-def sum_powers(table_ref, segments, lag_ref, dop_ref, spec, prods, corrs, emit):
-    count = segments[0][0].shape[0]
-    rows = count * HALF_DELAYS
-    for n, (s_ref, _) in enumerate(segments):
-        s = s_ref[...].reshape(count * BLOCKS, PAIR)
-        spec[n] = nt_dot(table_ref[...], jnp.concatenate([s, s], axis=1))
+def surv_spectrum(table_ref, s):
+    return nt_dot(table_ref[...], jnp.concatenate([s, s], axis=1))
+
+
+def surv_spectra_kernel(table_ref, s_ref, out_ref):
+    for b in range(s_ref.shape[0]):
+        out_ref[b] = surv_spectrum(table_ref, s_ref[b])
+
+
+def surv_spectra(table, surv, name):
+    return pl.pallas_call(
+        surv_spectra_kernel,
+        in_specs=[VMEM] * 2,
+        out_specs=VMEM,
+        out_shape=jax.ShapeDtypeStruct((surv.shape[0], 2 * FFT, BLOCKS), jnp.float32),
+        compiler_params=pltpu.CompilerParams(vmem_limit_bytes=VMEM_LIMIT),
+        name=name,
+    )(table, surv)
+
+
+def sum_powers(segments, lag_ref, dop_ref, prods, corrs, emit):
+    count = len(segments[0][0])
+    rows = count * DELAYS
     for k in range(TX):
         corr = corrs.at[k % 2]
-        for n, (_, r_ref) in enumerate(segments):
+        for n, (beams, r_ref) in enumerate(segments):
             r_re, r_im = r_ref[k, :FFT], r_ref[k, FFT:]
             prod = prods.at[n]
-            for b in range(count):
+            for b, (s_ref, at) in enumerate(beams):
                 cols = slice(b * BLOCKS, (b + 1) * BLOCKS)
-                s_re, s_im = spec[n, :FFT, cols], spec[n, FFT:, cols]
+                s_re, s_im = s_ref[at, :FFT], s_ref[at, FFT:]
                 prod[:FFT, cols] = (s_re * r_re + s_im * r_im).astype(jnp.bfloat16)
                 prod[FFT:, cols] = (s_im * r_re - s_re * r_im).astype(jnp.bfloat16)
             out = dot(lag_ref[k], prod[...]).astype(jnp.bfloat16)
             for b in range(count):
                 cols = slice(b * BLOCKS, (b + 1) * BLOCKS)
-                at = n * rows + b * HALF_DELAYS
-                corr[at : at + HALF_DELAYS, :BLOCKS] = out[:HALF_DELAYS, cols]
-                corr[at : at + HALF_DELAYS, BLOCKS:] = out[HALF_DELAYS:, cols]
+                at = n * rows + b * DELAYS
+                corr[at : at + DELAYS, :BLOCKS] = out[:DELAYS, cols]
+                corr[at : at + DELAYS, BLOCKS:] = out[DELAYS:, cols]
         x = dot(corr[...], dop_ref[k])
         x_re, x_im = x[:, :DOPPLER], x[:, DOPPLER:]
         power = (x_re * x_re + x_im * x_im) * (1.0 / (4 * BLOCKS))
         power = functools.reduce(
             jnp.add, [power[n * rows : (n + 1) * rows] for n in range(len(segments))]
         )
-        emit(k, power.reshape(count, HALF_DELAYS, DOPPLER))
-
-
-def emit_halves(chunks, own_ref, send_ref):
-    each = DELAYS // chunks
+        emit(k, power.reshape(count, DELAYS, DOPPLER))
+
+
+def emit_chunks(own_ref, send_refs):
+    each = own_ref.shape[2]
 
     def emit(k, power):
         own_ref[k] = power[:, :each]
-        for n in range(1, chunks // 2):
-            send_ref[n - 1, k] = power[:, n * each : (n + 1) * each].astype(jnp.bfloat16)
+        for n, ref in enumerate(send_refs):
+            ref[k] = power[:, (n + 1) * each : (n + 2) * each].astype(jnp.bfloat16)
 
     return emit
 
 
-def first_kernel(
-    params, rtab, mine, other, stab, s_ref, lags, dops, r_ref, part_ref, padded, spec, prods, corrs
-):
+def beams_of(ref, first, count):
+    return [(ref, first + b) for b in range(count)]
+
+
+def own_part_kernel(count, params, rtab, mine, other, spec, lags, dops, r_ref, part_ref, padded, prods, corrs):
     write_ref_spectra(params, rtab, mine, other, r_ref, padded)
 
     def emit(k, power):
         part_ref[k] = power
 
-    sum_powers(stab, [(s_ref, r_ref)], lags, dops, spec, prods, corrs, emit)
-
-
-def second_kernel(
-    chunks, params, rtab, mine, other, stab, s_ref, lags, dops, part_ref, r_ref, own_ref, send_ref, padded, spec, prods, corrs
+    sum_powers([(beams_of(spec, 0, count), r_ref)], lags, dops, prods, corrs, emit)
+
+
+def far_part_kernel(
+    count, params, rtab, mine, other, stab, s_ref, part_ref, lags, dops, r_ref, far_spec, own_ref, *refs
 ):
+    send_refs, (padded, prods, corrs) = refs[:-3], refs[-3:]
     write_ref_spectra(params, rtab, mine, other, r_ref, padded)
-    store = emit_halves(chunks, own_ref, send_ref)
+    surv_spectra_kernel(stab, s_ref, far_spec)
+    store = emit_chunks(own_ref, send_refs)
     emit = lambda k, power: store(k, power + part_ref[k])
-    sum_powers(stab, [(s_ref, r_ref)], lags, dops, spec, prods, corrs, emit)
-
-
-def both_kernel(
-    chunks, stab, here, there, r_here, r_there, lags, dops, own_ref, send_ref, spec, prods, corrs
-):
-    emit = emit_halves(chunks, own_ref, send_ref)
-    sum_powers(stab, [(here, r_here), (there, r_there)], lags, dops, spec, prods, corrs, emit)
-
-
-def call_powers(kernel, name, args, out_shape, count, segments, spectra):
-    padded = [pltpu.VMEM((BLOCKS + 2 * PAD, PAIR), jnp.float32)]
+    sum_powers([(beams_of(far_spec, 0, count), r_ref)], lags, dops, prods, corrs, emit)
+
+
+def both_kernel(first, count, spec, far_spec, r_here, r_there, lags, dops, own_ref, *refs):
+    send_refs, (prods, corrs) = refs[:-2], refs[-2:]
+    emit = emit_chunks(own_ref, send_refs)
+    segments = [(beams_of(s, first, count), r) for s, r in ((spec, r_here), (far_spec, r_there))]
+    sum_powers(segments, lags, dops, prods, corrs, emit)
+
+
+def assemble_kernel(n_seg, sizes, params, *refs):
+    out_ref = refs[-1]
+    groups = [refs[g * n_seg : (g + 1) * n_seg] for g in range(len(sizes))]
+    half = out_ref.shape[1] // 2
+    part = params[2 * TX + 1] % 2
+
+    def total(refs, k):
+        return functools.reduce(jnp.add, [r[k].astype(jnp.float32) for r in refs]) * (1.0 / n_seg)
+
+    for k in range(TX):
+        first = 0
+        for size, group in zip(sizes, groups, strict=True):
+            out_ref[k, pl.ds(part * half + first, size)] = total(group[::2], k)
+            out_ref[k, pl.ds((1 - part) * half + first, size)] = total(group[1::2], k)
+            first += size
+
+
+def call_powers(kernel, name, args, out_shape, count, segments, ref_spectra):
+    padded = pltpu.VMEM((BLOCKS + 2 * PAD, PAIR), jnp.float32)
+    work = [
+        pltpu.VMEM((segments, 2 * FFT, count * BLOCKS), jnp.bfloat16),
+        pltpu.VMEM((2, segments * count * DELAYS, 2 * BLOCKS), jnp.bfloat16),
+    ]
     return pl.pallas_call(
         kernel,
         in_specs=[SMEM if a.ndim == 1 else VMEM for a in args],
         out_specs=[VMEM] * len(out_shape),
         out_shape=out_shape,
-        scratch_shapes=(padded if spectra else [])
-        + [
-            pltpu.VMEM((segments, 2 * FFT, count * BLOCKS), jnp.float32),
-            pltpu.VMEM((segments, 2 * FFT, count * BLOCKS), jnp.bfloat16),
-            pltpu.VMEM((2, segments * count * HALF_DELAYS, 2 * BLOCKS), jnp.bfloat16),
-        ],
+        scratch_shapes=[padded] * ref_spectra + work,
         compiler_params=pltpu.CompilerParams(vmem_limit_bytes=VMEM_LIMIT),
         cost_estimate=pl.CostEstimate(
-            flops=segments * count * TX * 4 * 768 * 65536, bytes_accessed=6 << 20, transcendentals=0
+            flops=segments * count * TX * 2 * 768 * 65536, bytes_accessed=6 << 20, transcendentals=0
         ),
         name=name,
     )(*args)
@@ -347,7 +383,6 @@
     beams_here = voltages.shape[1]
     n_beam = lax.axis_size("beam")
     n_seg = lax.axis_size("seg")
-    segments_all = n_seg * voltages.shape[2]
     ids = jnp.stack([lax.axis_index("beam"), lax.axis_index("seg")]).astype(jnp.int32)
     volts = voltages.reshape(2, beams_here, voltages.shape[3])
     out = decimate(
@@ -359,64 +394,74 @@
         delay_start,
         doppler_start,
     )
-    surv, (keep, send, params) = out[:GROUPS], out[GROUPS:]
+    here, give, keep, send, params = out
+    stab, rtab = jnp.asarray(surv_fourier()), jnp.asarray(ref_fourier())
+    there = swap(give, "seg", 1)
     half = keep + swap(send, "beam", 1)
-    half, surv, params = lax.optimization_barrier((half, surv, params))
+    half, here, params = lax.optimization_barrier((half, here, params))
     got = [swap(half, "beam", flip) for flip in range(2, n_beam, 2)]
-    there = [swap(surv[0], "seg", 1)]
     lags, dops = make_tables(params, n_seg)
-    got, lags, dops = lax.optimization_barrier((got, lags, dops))
+    spec = surv_spectra(stab, here, "own_spectra")
+    got, lags, dops, spec = lax.optimization_barrier((got, lags, dops, spec))
     half = functools.reduce(jnp.add, got, half)
     other = swap(half, "beam", 1)
-    leaving, there[0] = lax.optimization_barrier((half, there[0]))
-    far = swap(leaving, "seg", 1)
-    far_other = swap(other, "seg", 1)
-    stab, rtab = jnp.asarray(surv_fourier()), jnp.asarray(ref_fourier())
-    count = beams_here // GROUPS
+    far = swap(half, "seg", 1)
+    leaving, there = lax.optimization_barrier((other, there))
+    far_other = swap(leaving, "seg", 1)
+
     each = DELAYS // n_seg
     r_shape = jax.ShapeDtypeStruct((TX, 2 * FFT, BLOCKS), jnp.float32)
-    part_shape = jax.ShapeDtypeStruct((TX, count, HALF_DELAYS, DOPPLER), jnp.float32)
-    halves = [
-        jax.ShapeDtypeStruct((TX, count, each, DOPPLER), jnp.float32),
-        jax.ShapeDtypeStruct((n_seg // 2 - 1, TX, count, each, DOPPLER), jnp.bfloat16),
-    ]
+    chunks = lambda n: [jax.ShapeDtypeStruct((TX, n, each, DOPPLER), jnp.float32)] + [
+        jax.ShapeDtypeStruct((TX, n, each, DOPPLER), jnp.bfloat16)
+    ] * (n_seg - 1)
+    sizes = [n * beams_here // 16 for n in GROUPS]
+    count = sizes[0]
     r_here, part = call_powers(
-        first_kernel,
-        "first",
-        (params, rtab, half, other, stab, surv[0], lags, dops),
-        [r_shape, part_shape],
+        functools.partial(own_part_kernel, count),
+        "own_part",
+        (params, rtab, half, other, spec, lags, dops),
+        [r_shape, jax.ShapeDtypeStruct((TX, count, DELAYS, DOPPLER), jnp.float32)],
         count,
         1,
         True,
     )
-    surv, part = lax.optimization_barrier((surv, part))
-    there += [swap(s, "seg", 1) for s in surv[1:]]
-    r_there, *sums = call_powers(
-        functools.partial(second_kernel, n_seg),
-        "second",
-        (params, rtab, far, far_other, stab, there[0], lags, dops, part),
-        [r_shape] + halves,
-        count,
-        1,
-        True,
-    )
-    maps = []
-    for g in range(GROUPS):
-        if g > 0:
-            sums = call_powers(
-                functools.partial(both_kernel, n_seg),
+    behind = []
+    collected = []
+    first = 0
+    for g, count in enumerate(sizes):
+        if g == 0:
+            r_there, far_spec, own, *sends = call_powers(
+                functools.partial(far_part_kernel, count),
+                "far_part",
+                (params, rtab, far, far_other, stab, there, part, lags, dops),
+                [r_shape, jax.ShapeDtypeStruct(spec.shape, spec.dtype)] + chunks(count),
+                count,
+                1,
+                True,
+            )
+        else:
+            own, *sends = call_powers(
+                functools.partial(both_kernel, first, count),
                 "both",
-                (stab, surv[g], there[g], r_here, r_there, lags, dops),
-                halves,
+                (spec, far_spec, r_here, r_there, lags, dops),
+                chunks(count),
                 count,
                 2,
                 False,
             )
-        total, outgoing = sums
-        for n in range(1, n_seg // 2):
-            total = total + swap(outgoing[n - 1], "seg", 2 * n).astype(jnp.float32)
-        maps.append(total / segments_all)
-    return jnp.concatenate(maps, axis=1)
+        sends[0], *behind = lax.optimization_barrier((sends[0], *behind))
+        arrived = [swap(s, "seg", n + 1) for n, s in enumerate(sends)]
+        collected += [own] + arrived
+        behind = arrived[1:]
+        first += count
+    return pl.pallas_call(
+        functools.partial(assemble_kernel, n_seg, sizes),
+        in_specs=[SMEM] + [VMEM] * len(collected),
+        out_specs=VMEM,
+        out_shape=jax.ShapeDtypeStruct((TX, beams_here, each, DOPPLER), jnp.float32),
+        compiler_params=pltpu.CompilerParams(vmem_limit_bytes=VMEM_LIMIT),
+        name="assemble",
+    )(params, *collected)
 
 
 def solution(mesh):

time: 65.2 us -> 62.1 us (0.952)
  Pallas kernels: 28.1 us -> 26.1 us
  starting transfers between devices: 20.5 us -> 22 us
  waiting for transfers between devices: 15 us -> 13.6 us
  other arithmetic: 1.31 us -> 0.15 us
    pallas_call x5 -> x3, Pallas kernels: 21.3 us -> 16.5 us  [call_powers(): pl.pallas_call(kernel, in_specs=[SMEM if a.ndim == 1 else VMEM for a in a...]
    pallas_call x0 -> x2, Pallas kernels: none -> 2.37 us  [the longest x1 1.63 us: shards(): pl.pallas_call(functools.partial(assemble_kernel, n_seg, sizes), in_specs...]
    ppermute x15 -> x14, starting transfers between devices: 20.5 us -> 22 us  [swap(): return lax.ppermute(value, axis, [(i, i ^ flip) for i in range(size)])]
    ppermute x15 -> x14, waiting for transfers between devices: 15 us -> 13.6 us  [swap(): return lax.ppermute(value, axis, [(i, i ^ flip) for i in range(size)])]
    concatenate x1 -> x0, other arithmetic: 1.04 us -> none  [shards(): return jnp.concatenate(maps, axis=1)]
  transfers between devices with their start and end apart: 15 -> 14, of which waited for: 6 -> 7; matrix products, arithmetic and copies ran while one was open for 0% -> 0% of each run, Pallas kernels for 34% -> 20%
where the time goes in v4:
time: 62.1 us; the launch traced here: 62 us
  Pallas kernels  26.1 us (42%)
  starting transfers between devices  22 us (35%)
  waiting for transfers between devices  13.6 us (22%)
    ppermute x14, starting transfers between devices, swap(): return lax.ppermute(value, axis, [(i, i ^ flip) for i in range(size)])  22 us
    pallas_call x3, Pallas kernels, call_powers(): pl.pallas_call(kernel, in_specs=[SMEM if a.ndim == 1 else VMEM for a in a...  16.5 us
    ppermute x14, waiting for transfers between devices, swap(): return lax.ppermute(value, axis, [(i, i ^ flip) for i in range(size)])  13.6 us
    pallas_call x1, Pallas kernels, decimate(): pl.pallas_call(functools.partial(decimate_kernel, beams), in_specs=[SMEM]...  6.26 us
    pallas_call x1, Pallas kernels, shards(): pl.pallas_call(functools.partial(assemble_kernel, n_seg, sizes), in_specs...  1.63 us
  transfers between devices with their start and end apart: 14, of which 7 were waited for; matrix products, arithmetic and copies ran while one was open for 0% of the time, Pallas kernels for 20%

profile of v4, /device:TPU:0, one launch (start us, length us, event | category | flops | bytes accessed | tf_op | source)
XLA Modules:
  0.0 62.0 jit_solution(16406880478470436574)
XLA Ops:
  0.0 0.0 copy-start.3
  0.0 0.1 pad_add_fusion.ids
  0.1 0.0 copy-start
  0.1 0.0 copy-start.2
  0.1 6.3 %decimate.1 = (bf16[8,256,128]{2,1,0:T(8,128)(2,1)S(1)}, bf16[8,256,128]{2,1,0:T(8,128)(2,1)S(1)}, bf16[2,256,128]{2,1,0:T(8,128)(2,1)S(1)}, bf16[2,256,128]{2,1,0:T(8,128)(2,1)S(1)}, s32[10]{0:T(128)S(1)}) custom-call(s32[2]{0:T(128)S(1)} %pad_add_fusion.ids, s32[4]{0:T(128)} %owner.1, s32[4]{0:T(128)} %delay.1, s32[4]{0:T(128)} %doppler.1, ...), custom_call_target="tpu_custom_call" | custom-call | tf_op jit(solution)/shard_map/decimate/pallas_call | solution.py:180
  6.3 0.0 copy-start.1
  6.4 0.5 collective-permute-start
  6.9 2.7 %collective-permute-start.6 = (bf16[8,256,128]{2,1,0:T(8,128)(2,1)S(1)}, bf16[8,256,128]{2,1,0:T(8,128)(2,1)S(1)}, u32[]{:S(2)}, u32[]{:S(2)}) collective-permute-start(bf16[8,256,128]{2,1,0:T(8,128)(2,1)S(1)} %get-tuple-element.48), channel_id=1, source_target_pairs={{0,1},{1,0},{2,3},{3,2},{4,5},{5,4},{6,7},{7,6},{8,9},{9,8},{10,11... | collective-permute-start | bytes 1572872 | tf_op jit(solution)/shard_map/ppermute | solution.py:379
  9.5 0.0 collective-permute-done
  9.6 2.5 %collective-permute-start.3 = (bf16[2,256,128]{2,1,0:T(8,128)(2,1)S(1)}, bf16[2,256,128]{2,1,0:T(8,128)(2,1)S(1)}, u32[]{:S(2)}, u32[]{:S(2)}) collective-permute-start(bf16[2,256,128]{2,1,0:T(8,128)(2,1)S(1)} %add.12), channel_id=1, source_target_pairs={{0,24},{4,28},{8,16},{12,20},{16,8},{20,12},{24,0},{28,4},{1,25},{... | collective-permute-start | bytes 393224 | tf_op jit(solution)/shard_map/ppermute | solution.py:379
  12.1 0.5 collective-permute-start.2
  12.6 0.5 collective-permute-start.1
  13.1 0.0 copy-done.3
  13.1 0.7 %own_spectra.1.spec = f32[8,512,256]{2,1,0:T(8,128)S(1)} custom-call(bf16[512,256]{1,0:T(8,128)(2,1)S(1)} %copy-done.3, bf16[8,256,128]{2,1,0:T(8,128)(2,1)S(1)} %get-tuple-element.44.s_ref), custom_call_target="tpu_custom_call" | custom-call | tf_op jit(solution)/shard_map/own_spectra/pallas_call | solution.py:260
  13.9 0.0 copy-done
  13.9 0.0 copy-done.2
  13.9 1.0 %tables.1 = (bf16[4,256,512]{2,1,0:T(8,128)(2,1)S(1)}, bf16[4,512,256]{2,1,0:T(8,128)(2,1)S(1)}) custom-call(s32[10]{0:T(128)S(1)} %get-tuple-element.40.params, f32[2,4,192,128]{3,2,1,0:T(8,128)S(1)} %copy-done.2, f32[2,4,256,128]{3,2,1,0:T(8,128)S(1)} %copy-done), custom_call_target="tpu_custom_call" | custom-call | tf_op jit(solution)/shard_map/tables/pallas_call | solution.py:219
  14.9 1.5 %collective-permute-done.3 = bf16[2,256,128]{2,1,0:T(8,128)(2,1)S(1)} collective-permute-done((bf16[2,256,128]{2,1,0:T(8,128)(2,1)S(1)}, bf16[2,256,128]{2,1,0:T(8,128)(2,1)S(1)}, u32[]{:S(2)}, u32[]{:S(2)}) %collective-permute-start.3) | collective-permute-done | bytes 131104 | tf_op jit(solution)/shard_map/ppermute | solution.py:379
  16.4 2.5 %collective-permute-done.2 = bf16[2,256,128]{2,1,0:T(8,128)(2,1)S(1)} collective-permute-done((bf16[2,256,128]{2,1,0:T(8,128)(2,1)S(1)}, bf16[2,256,128]{2,1,0:T(8,128)(2,1)S(1)}, u32[]{:S(2)}, u32[]{:S(2)}) %collective-permute-start.2) | collective-permute-done | bytes 131104 | tf_op jit(solution)/shard_map/ppermute | solution.py:379
  18.9 0.1 collective-permute-done.1
  19.1 0.1 collective-permute-start.5
  19.1 1.3 %collective-permute-start.4 = (bf16[2,256,128]{2,1,0:T(8,128)(2,1)S(1)}, bf16[2,256,128]{2,1,0:T(8,128)(2,1)S(1)}, u32[]{:S(2)}, u32[]{:S(2)}) collective-permute-start(bf16[2,256,128]{2,1,0:T(8,128)(2,1)S(1)} %add_add_fusion.mine), channel_id=1, source_target_pairs={{0,1},{1,0},{2,3},{3,2},{4,5},{5,4},{6,7},{7,6},{8,9},{9,8},{10,11... | collective-permute-start | bytes 393224 | tf_op jit(solution)/shard_map/ppermute | solution.py:379
  20.4 0.0 collective-permute-done.5.other
  20.5 1.6 %collective-permute-done.6.s_ref = bf16[8,256,128]{2,1,0:T(8,128)(2,1)S(1)} collective-permute-done((bf16[8,256,128]{2,1,0:T(8,128)(2,1)S(1)}, bf16[8,256,128]{2,1,0:T(8,128)(2,1)S(1)}, u32[]{:S(2)}, u32[]{:S(2)}) %collective-permute-start.6) | collective-permute-done | bytes 524320 | tf_op jit(solution)/shard_map/ppermute | solution.py:379
  22.1 2.0 %collective-permute-start.7 = (bf16[2,256,128]{2,1,0:T(8,128)(2,1)S(1)}, bf16[2,256,128]{2,1,0:T(8,128)(2,1)S(1)}, u32[]{:S(2)}, u32[]{:S(2)}) collective-permute-start(bf16[2,256,128]{2,1,0:T(8,128)(2,1)S(1)} %collective-permute-done.5.other), channel_id=1, source_target_pairs={{0,1},{1,0},{2,3},{3,2},{4,5},{5,4},{6,7},{7,6},{8,9},{9,8},{10,11... | collective-permute-start | bytes 393224 | tf_op jit(solution)/shard_map/ppermute | solution.py:379
  24.1 0.0 copy-done.1
  24.1 4.8 %own_part.1 = (f32[4,512,256]{2,1,0:T(8,128)S(1)}, f32[4,4,128,128]{3,2,1,0:T(8,128)S(1)}) custom-call(s32[10]{0:T(128)S(1)} %get-tuple-element.40.params, bf16[512,1024]{1,0:T(8,128)(2,1)S(1)} %copy-done.1, bf16[2,256,128]{2,1,0:T(8,128)(2,1)S(1)} %add_add_fusion.mine, bf16[2,256,128]{2,1,0:T(8,128)(2,1)S(1)} %collective-permute-done.5.other, ...), custom_call_target="tpu_custom_call" | custom-call | flops 1610612736 | bytes 6291456 | tf_op jit(solution)/shard_map/own_part/pallas_call | solution.py:363
  28.9 0.0 collective-permute-done.4.mine
  28.9 0.0 collective-permute-done.7.other
  28.9 5.7 %far_part.1 = (f32[4,512,256]{2,1,0:T(8,128)S(1)}, f32[8,512,256]{2,1,0:T(8,128)S(1)}, f32[4,4,32,128]{3,2,1,0:T(8,128)S(1)}, bf16[4,4,32,128]{3,2,1,0:T(8,128)(...) custom-call(s32[10]{0:T(128)S(1)} %get-tuple-element.40.params, ...), custom_call_target="tpu_custom_call" | custom-call | flops 1610612736 | bytes 6291456 | tf_op jit(solution)/shard_map/far_part/pallas_call | solution.py:363
  34.7 0.6 collective-permute-start.8
  35.2 2.6 %collective-permute-start.9 = (bf16[4,4,32,128]{3,2,1,0:T(8,128)(2,1)S(1)}, bf16[4,4,32,128]{3,2,1,0:T(8,128)(2,1)S(1)}, u32[]{:S(2)}, u32[]{:S(2)}) collective-permute-start(bf16[4,4,32,128]{3,2,1,0:T(8,128)(2,1)S(1)} %get-tuple-element.57), channel_id=1, source_target_pairs={{0,2},{1,3},{2,0},{3,1},{4,6},{5,7},{6,4},{7,5},{8,10},{9,11},{10,... | collective-permute-start | bytes 393224 | tf_op jit(solution)/shard_map/ppermute | solution.py:379
  37.8 1.3 %collective-permute-start.10 = (bf16[4,4,32,128]{3,2,1,0:T(8,128)(2,1)S(1)}, bf16[4,4,32,128]{3,2,1,0:T(8,128)(2,1)S(1)}, u32[]{:S(2)}, u32[]{:S(2)}) collective-permute-start(bf16[4,4,32,128]{3,2,1,0:T(8,128)(2,1)S(1)} %get-tuple-element.58), channel_id=1, source_target_pairs={{0,3},{1,2},{2,1},{3,0},{4,7},{5,6},{6,5},{7,4},{8,11},{9,10},{10,... | collective-permute-start | bytes 393224 | tf_op jit(solution)/shard_map/ppermute | solution.py:379
  39.1 5.9 %both.1 = (f32[4,4,32,128]{3,2,1,0:T(8,128)S(1)}, bf16[4,4,32,128]{3,2,1,0:T(8,128)(2,1)S(1)}, bf16[4,4,32,128]{3,2,1,0:T(8,128)(2,1)S(1)}, bf16[4,4,32,128]{3,2,1,0:T(8,128)(2,1)S(1)}) custom-call(f32[8,512,256]{2,1,0:T(8,128)S(1)} %own_spectra.1.spec, f32[8,512,256]{2,1,0:T(8,128)S(1)} %get-tuple-element.59.far_spec, ...), custom_call_target="tpu_custom_call" | custom-call | flops 3221225472 | bytes 6291456 | tf_op jit(solution)/shard_map/both/pallas_call | solution.py:363
  45.0 1.7 %collective-permute-start.12 = (bf16[4,4,32,128]{3,2,1,0:T(8,128)(2,1)S(1)}, bf16[4,4,32,128]{3,2,1,0:T(8,128)(2,1)S(1)}, u32[]{:S(2)}, u32[]{:S(2)}) collective-permute-start(bf16[4,4,32,128]{3,2,1,0:T(8,128)(2,1)S(1)} %get-tuple-element.65), channel_id=1, source_target_pairs={{0,2},{1,3},{2,0},{3,1},{4,6},{5,7},{6,4},{7,5},{8,10},{9,11},{10,... | collective-permute-start | bytes 393224 | tf_op jit(solution)/shard_map/ppermute | solution.py:379
  46.8 0.9 %collective-permute-start.13 = (bf16[4,4,32,128]{3,2,1,0:T(8,128)(2,1)S(1)}, bf16[4,4,32,128]{3,2,1,0:T(8,128)(2,1)S(1)}, u32[]{:S(2)}, u32[]{:S(2)}) collective-permute-start(bf16[4,4,32,128]{3,2,1,0:T(8,128)(2,1)S(1)} %get-tuple-element.66), channel_id=1, source_target_pairs={{0,3},{1,2},{2,1},{3,0},{4,7},{5,6},{6,5},{7,4},{8,11},{9,10},{10,... | collective-permute-start | bytes 393224 | tf_op jit(solution)/shard_map/ppermute | solution.py:379
  47.7 4.4 %collective-permute-done.9.refs_2_ = bf16[4,4,32,128]{3,2,1,0:T(8,128)(2,1)S(1)} collective-permute-done((bf16[4,4,32,128]{3,2,1,0:T(8,128)(2,1)S(1)}, bf16[4,4,32,128]{3,2,1,0:T(8,128)(2,1)S(1)}, u32[]{:S(2)}, u32[]{:S(2)}) %collective-permute-start.9) | collective-permute-done | bytes 131104 | tf_op jit(solution)/shard_map/ppermute | solution.py:379
  52.1 0.0 collective-permute-done.10.refs_3_
  52.1 4.8 %collective-permute-start.11 = (bf16[4,4,32,128]{3,2,1,0:T(8,128)(2,1)S(1)}, bf16[4,4,32,128]{3,2,1,0:T(8,128)(2,1)S(1)}, u32[]{:S(2)}, u32[]{:S(2)}) collective-permute-start(bf16[4,4,32,128]{3,2,1,0:T(8,128)(2,1)S(1)} %get-tuple-element.64), channel_id=1, source_target_pairs={{0,1},{1,0},{2,3},{3,2},{4,5},{5,4},{6,7},{7,6},{8,9},{9,8},{10,11... | collective-permute-start | bytes 393224 | tf_op jit(solution)/shard_map/ppermute | solution.py:379
  56.9 0.0 collective-permute-done.8.refs_1_
  56.9 2.2 %collective-permute-done.12.refs_6_ = bf16[4,4,32,128]{3,2,1,0:T(8,128)(2,1)S(1)} collective-permute-done((bf16[4,4,32,128]{3,2,1,0:T(8,128)(2,1)S(1)}, bf16[4,4,32,128]{3,2,1,0:T(8,128)(2,1)S(1)}, u32[]{:S(2)}, u32[]{:S(2)}) %collective-permute-start.12) | collective-permute-done | bytes 131104 | tf_op jit(solution)/shard_map/ppermute | solution.py:379
  59.1 0.0 collective-permute-done.13.refs_7_
  59.1 1.2 %collective-permute-done.11.refs_5_ = bf16[4,4,32,128]{3,2,1,0:T(8,128)(2,1)S(1)} collective-permute-done((bf16[4,4,32,128]{3,2,1,0:T(8,128)(2,1)S(1)}, bf16[4,4,32,128]{3,2,1,0:T(8,128)(2,1)S(1)}, u32[]{:S(2)}, u32[]{:S(2)}) %collective-permute-start.11) | collective-permute-done | bytes 131104 | tf_op jit(solution)/shard_map/ppermute | solution.py:379
  60.4 1.6 %assemble.1 = f32[4,16,32,128]{3,2,1,0:T(8,128)} custom-call(s32[10]{0:T(128)S(1)} %get-tuple-element.40.params, f32[4,4,32,128]{3,2,1,0:T(8,128)S(1)} %get-tuple-element.55.refs_0_, bf16[4,4,32,128]{3,2,1,0:T(8,128)(2,1)S(1)} %collective-permute-done.8.refs_1_, bf16[4,4,32,128]{3,2,1,0:T(8,128)(2,1)S(1)} %collective-permute-done.9.refs_2_, ...), custom_call_target="tpu_custom_call" | custom-call | tf_op jit(solution)/shard_map/assemble/pallas_call | solution.py:457
  (2 shorter events, 0.1 us)
Async XLA Ops:
  0.0 13.1 %copy-start.3 = (bf16[512,256]{1,0:T(8,128)(2,1)S(1)}, bf16[512,256]{1,0:T(8,128)(2,1)}, u32[]{:S(2)}) copy-start(bf16[512,256]{1,0:T(8,128)(2,1)} %constant.17.clone.table_ref.stab) | copy-start | bytes 786436
  0.1 13.8 %copy-start = (f32[2,4,256,128]{3,2,1,0:T(8,128)S(1)}, f32[2,4,256,128]{3,2,1,0:T(8,128)}, u32[]{:S(2)}) copy-start(f32[2,4,256,128]{3,2,1,0:T(8,128)} %constant.20.clone.dop_ref) | copy-start | bytes 3145732
  0.1 13.8 %copy-start.2 = (f32[2,4,192,128]{3,2,1,0:T(8,128)S(1)}, f32[2,4,192,128]{3,2,1,0:T(8,128)}, u32[]{:S(2)}) copy-start(f32[2,4,192,128]{3,2,1,0:T(8,128)} %constant.19.clone.lag_ref) | copy-start | bytes 2359300
  6.3 17.7 %copy-start.1 = (bf16[512,1024]{1,0:T(8,128)(2,1)S(1)}, bf16[512,1024]{1,0:T(8,128)(2,1)}, u32[]{:S(2)}) copy-start(bf16[512,1024]{1,0:T(8,128)(2,1)} %constant.18.clone.rtab) | copy-start | bytes 3145732
  6.4 3.2 %collective-permute-start = (bf16[2,256,128]{2,1,0:T(8,128)(2,1)S(1)}, bf16[2,256,128]{2,1,0:T(8,128)(2,1)S(1)}, u32[]{:S(2)}, u32[]{:S(2)}) collective-permute-start(bf16[2,256,128]{2,1,0:T(8,128)(2,1)S(1)} %get-tuple-element.37), channel_id=1, source_target_pairs={{0,4},{4,0},{8,12},{12,8},{16,20},{20,16},{24,28},{28,24},{1,5},{5... | collective-permute-start | bytes 393224 | tf_op jit(solution)/shard_map/ppermute | solution.py:379
  6.9 15.2 %collective-permute-start.6 = (bf16[8,256,128]{2,1,0:T(8,128)(2,1)S(1)}, bf16[8,256,128]{2,1,0:T(8,128)(2,1)S(1)}, u32[]{:S(2)}, u32[]{:S(2)}) collective-permute-start(bf16[8,256,128]{2,1,0:T(8,128)(2,1)S(1)} %get-tuple-element.48), channel_id=1, source_target_pairs={{0,1},{1,0},{2,3},{3,2},{4,5},{5,4},{6,7},{7,6},{8,9},{9,8},{10,11... | collective-permute-start | bytes 1572872 | tf_op jit(solution)/shard_map/ppermute | solution.py:379
  9.6 6.8 %collective-permute-start.3 = (bf16[2,256,128]{2,1,0:T(8,128)(2,1)S(1)}, bf16[2,256,128]{2,1,0:T(8,128)(2,1)S(1)}, u32[]{:S(2)}, u32[]{:S(2)}) collective-permute-start(bf16[2,256,128]{2,1,0:T(8,128)(2,1)S(1)} %add.12), channel_id=1, source_target_pairs={{0,24},{4,28},{8,16},{12,20},{16,8},{20,12},{24,0},{28,4},{1,25},{... | collective-permute-start | bytes 393224 | tf_op jit(solution)/shard_map/ppermute | solution.py:379
  12.1 6.8 %collective-permute-start.2 = (bf16[2,256,128]{2,1,0:T(8,128)(2,1)S(1)}, bf16[2,256,128]{2,1,0:T(8,128)(2,1)S(1)}, u32[]{:S(2)}, u32[]{:S(2)}) collective-permute-start(bf16[2,256,128]{2,1,0:T(8,128)(2,1)S(1)} %add.12), channel_id=1, source_target_pairs={{0,16},{4,20},{8,24},{12,28},{16,0},{20,4},{24,8},{28,12},{1,17},{... | collective-permute-start | bytes 393224 | tf_op jit(solution)/shard_map/ppermute | solution.py:379
  12.6 6.4 %collective-permute-start.1 = (bf16[2,256,128]{2,1,0:T(8,128)(2,1)S(1)}, bf16[2,256,128]{2,1,0:T(8,128)(2,1)S(1)}, u32[]{:S(2)}, u32[]{:S(2)}) collective-permute-start(bf16[2,256,128]{2,1,0:T(8,128)(2,1)S(1)} %add.12), channel_id=1, source_target_pairs={{0,8},{4,12},{8,0},{12,4},{16,24},{20,28},{24,16},{28,20},{1,9},{5... | collective-permute-start | bytes 393224 | tf_op jit(solution)/shard_map/ppermute | solution.py:379
  19.1 1.4 %collective-permute-start.5 = (bf16[2,256,128]{2,1,0:T(8,128)(2,1)S(1)}, bf16[2,256,128]{2,1,0:T(8,128)(2,1)S(1)}, u32[]{:S(2)}, u32[]{:S(2)}) collective-permute-start(bf16[2,256,128]{2,1,0:T(8,128)(2,1)S(1)} %add_add_fusion.mine), channel_id=1, source_target_pairs={{0,4},{4,0},{8,12},{12,8},{16,20},{20,16},{24,28},{28,24},{1,5},{5... | collective-permute-start | bytes 393224 | tf_op jit(solution)/shard_map/ppermute | solution.py:379
  19.1 9.8 %collective-permute-start.4 = (bf16[2,256,128]{2,1,0:T(8,128)(2,1)S(1)}, bf16[2,256,128]{2,1,0:T(8,128)(2,1)S(1)}, u32[]{:S(2)}, u32[]{:S(2)}) collective-permute-start(bf16[2,256,128]{2,1,0:T(8,128)(2,1)S(1)} %add_add_fusion.mine), channel_id=1, source_target_pairs={{0,1},{1,0},{2,3},{3,2},{4,5},{5,4},{6,7},{7,6},{8,9},{9,8},{10,11... | collective-permute-start | bytes 393224 | tf_op jit(solution)/shard_map/ppermute | solution.py:379
  22.1 6.9 %collective-permute-start.7 = (bf16[2,256,128]{2,1,0:T(8,128)(2,1)S(1)}, bf16[2,256,128]{2,1,0:T(8,128)(2,1)S(1)}, u32[]{:S(2)}, u32[]{:S(2)}) collective-permute-start(bf16[2,256,128]{2,1,0:T(8,128)(2,1)S(1)} %collective-permute-done.5.other), channel_id=1, source_target_pairs={{0,1},{1,0},{2,3},{3,2},{4,5},{5,4},{6,7},{7,6},{8,9},{9,8},{10,11... | collective-permute-start | bytes 393224 | tf_op jit(solution)/shard_map/ppermute | solution.py:379
  34.7 22.2 %collective-permute-start.8 = (bf16[4,4,32,128]{3,2,1,0:T(8,128)(2,1)S(1)}, bf16[4,4,32,128]{3,2,1,0:T(8,128)(2,1)S(1)}, u32[]{:S(2)}, u32[]{:S(2)}) collective-permute-start(bf16[4,4,32,128]{3,2,1,0:T(8,128)(2,1)S(1)} %get-tuple-element.56), channel_id=1, source_target_pairs={{0,1},{1,0},{2,3},{3,2},{4,5},{5,4},{6,7},{7,6},{8,9},{9,8},{10,11... | collective-permute-start | bytes 393224 | tf_op jit(solution)/shard_map/ppermute | solution.py:379
  35.2 16.9 %collective-permute-start.9 = (bf16[4,4,32,128]{3,2,1,0:T(8,128)(2,1)S(1)}, bf16[4,4,32,128]{3,2,1,0:T(8,128)(2,1)S(1)}, u32[]{:S(2)}, u32[]{:S(2)}) collective-permute-start(bf16[4,4,32,128]{3,2,1,0:T(8,128)(2,1)S(1)} %get-tuple-element.57), channel_id=1, source_target_pairs={{0,2},{1,3},{2,0},{3,1},{4,6},{5,7},{6,4},{7,5},{8,10},{9,11},{10,... | collective-permute-start | bytes 393224 | tf_op jit(solution)/shard_map/ppermute | solution.py:379
  37.8 14.3 %collective-permute-start.10 = (bf16[4,4,32,128]{3,2,1,0:T(8,128)(2,1)S(1)}, bf16[4,4,32,128]{3,2,1,0:T(8,128)(2,1)S(1)}, u32[]{:S(2)}, u32[]{:S(2)}) collective-permute-start(bf16[4,4,32,128]{3,2,1,0:T(8,128)(2,1)S(1)} %get-tuple-element.58), channel_id=1, source_target_pairs={{0,3},{1,2},{2,1},{3,0},{4,7},{5,6},{6,5},{7,4},{8,11},{9,10},{10,... | collective-permute-start | bytes 393224 | tf_op jit(solution)/shard_map/ppermute | solution.py:379
  45.0 14.1 %collective-permute-start.12 = (bf16[4,4,32,128]{3,2,1,0:T(8,128)(2,1)S(1)}, bf16[4,4,32,128]{3,2,1,0:T(8,128)(2,1)S(1)}, u32[]{:S(2)}, u32[]{:S(2)}) collective-permute-start(bf16[4,4,32,128]{3,2,1,0:T(8,128)(2,1)S(1)} %get-tuple-element.65), channel_id=1, source_target_pairs={{0,2},{1,3},{2,0},{3,1},{4,6},{5,7},{6,4},{7,5},{8,10},{9,11},{10,... | collective-permute-start | bytes 393224 | tf_op jit(solution)/shard_map/ppermute | solution.py:379
  46.8 12.4 %collective-permute-start.13 = (bf16[4,4,32,128]{3,2,1,0:T(8,128)(2,1)S(1)}, bf16[4,4,32,128]{3,2,1,0:T(8,128)(2,1)S(1)}, u32[]{:S(2)}, u32[]{:S(2)}) collective-permute-start(bf16[4,4,32,128]{3,2,1,0:T(8,128)(2,1)S(1)} %get-tuple-element.66), channel_id=1, source_target_pairs={{0,3},{1,2},{2,1},{3,0},{4,7},{5,6},{6,5},{7,4},{8,11},{9,10},{10,... | collective-permute-start | bytes 393224 | tf_op jit(solution)/shard_map/ppermute | solution.py:379
  52.1 8.2 %collective-permute-start.11 = (bf16[4,4,32,128]{3,2,1,0:T(8,128)(2,1)S(1)}, bf16[4,4,32,128]{3,2,1,0:T(8,128)(2,1)S(1)}, u32[]{:S(2)}, u32[]{:S(2)}) collective-permute-start(bf16[4,4,32,128]{3,2,1,0:T(8,128)(2,1)S(1)} %get-tuple-element.64), channel_id=1, source_target_pairs={{0,1},{1,0},{2,3},{3,2},{4,5},{5,4},{6,7},{7,6},{8,9},{9,8},{10,11... | collective-permute-start | bytes 393224 | tf_op jit(solution)/shard_map/ppermute | solution.py:379

commit v5 on v4

--- a/solution.py
+++ b/solution.py
@@ -22,10 +22,13 @@
 LEAD = 128
 REACH = LEAD + STRIDE
 PAIR = 2 * BLOCK_LEN
-GROUPS = (4, 4)
+TOGETHER = 4
 LANES = 128
 LANE_BLOCKS = 2 * FFT // LANES
 VMEM_LIMIT = 24 * 1024 * 1024
+OWN_FLOPS = 1_600_000_000
+FAR_FLOPS = 1_600_000_000
+BOTH_FLOPS = 3_200_000_000
 
 SMEM = pl.BlockSpec(memory_space=pltpu.SMEM)
 VMEM = pl.BlockSpec(memory_space=pltpu.VMEM)
@@ -232,15 +235,17 @@
 PAD = 8
 
 
-def write_ref_spectra(params, table_ref, mine_ref, other_ref, out_ref, padded):
+def first_tx(params, group):
     core = params[2 * TX] % 2
+    return (core if group == 0 else 1 - core) * HALF_TX
+
+
+def write_ref_spectra(params, first, table_ref, ref, out_ref, padded):
     padded[:PAD] = jnp.zeros((PAD, PAIR), jnp.float32)
     padded[PAD + BLOCKS :] = jnp.zeros((PAD, PAIR), jnp.float32)
-    for k in range(TX):
-        here = core == k // HALF_TX
-        ref = jnp.where(here, mine_ref[k % HALF_TX], other_ref[k % HALF_TX])
-        padded[PAD : PAD + BLOCKS] = ref.astype(jnp.float32)
-        start = PAD - 1 - (params[k] + DELAYS - 1) // BLOCK_LEN
+    for k in range(HALF_TX):
+        padded[PAD : PAD + BLOCKS] = ref[k].astype(jnp.float32)
+        start = PAD - 1 - (params[first + k] + DELAYS - 1) // BLOCK_LEN
         window = jnp.concatenate(
             [padded[pl.ds(start + e, BLOCKS), :].astype(jnp.bfloat16) for e in range(4)], axis=1
         )
@@ -267,109 +272,117 @@
     )(table, surv)
 
 
-def sum_powers(segments, lag_ref, dop_ref, prods, corrs, emit):
-    count = len(segments[0][0])
+def sum_powers(segments, first, lag_ref, dop_ref, prods, corrs, emit):
+    count = segments[0][0].shape[0]
     rows = count * DELAYS
-    for k in range(TX):
-        corr = corrs.at[k % 2]
-        for n, (beams, r_ref) in enumerate(segments):
+    for k in range(HALF_TX):
+        corr = corrs.at[k]
+        for n, (s_ref, r_ref) in enumerate(segments):
             r_re, r_im = r_ref[k, :FFT], r_ref[k, FFT:]
             prod = prods.at[n]
-            for b, (s_ref, at) in enumerate(beams):
+            for b in range(count):
                 cols = slice(b * BLOCKS, (b + 1) * BLOCKS)
-                s_re, s_im = s_ref[at, :FFT], s_ref[at, FFT:]
+                s_re, s_im = s_ref[b, :FFT], s_ref[b, FFT:]
                 prod[:FFT, cols] = (s_re * r_re + s_im * r_im).astype(jnp.bfloat16)
                 prod[FFT:, cols] = (s_im * r_re - s_re * r_im).astype(jnp.bfloat16)
-            out = dot(lag_ref[k], prod[...]).astype(jnp.bfloat16)
+            out = dot(lag_ref[first + k], prod[...]).astype(jnp.bfloat16)
             for b in range(count):
                 cols = slice(b * BLOCKS, (b + 1) * BLOCKS)
                 at = n * rows + b * DELAYS
                 corr[at : at + DELAYS, :BLOCKS] = out[:DELAYS, cols]
                 corr[at : at + DELAYS, BLOCKS:] = out[DELAYS:, cols]
-        x = dot(corr[...], dop_ref[k])
-        x_re, x_im = x[:, :DOPPLER], x[:, DOPPLER:]
-        power = (x_re * x_re + x_im * x_im) * (1.0 / (4 * BLOCKS))
-        power = functools.reduce(
-            jnp.add, [power[n * rows : (n + 1) * rows] for n in range(len(segments))]
-        )
-        emit(k, power.reshape(count, DELAYS, DOPPLER))
+        for b in range(0, count, TOGETHER):
+            power = 0.0
+            for n in range(len(segments)):
+                at = n * rows + b * DELAYS
+                x = dot(corr[at : at + TOGETHER * DELAYS], dop_ref[first + k])
+                x_re, x_im = x[:, :DOPPLER], x[:, DOPPLER:]
+                power = power + (x_re * x_re + x_im * x_im) * (1.0 / (4 * BLOCKS))
+            emit(k, slice(b, b + TOGETHER), power.reshape(TOGETHER, DELAYS, DOPPLER))
 
 
 def emit_chunks(own_ref, send_refs):
     each = own_ref.shape[2]
 
-    def emit(k, power):
-        own_ref[k] = power[:, :each]
+    def emit(k, at, power):
+        own_ref[k, at] = power[:, :each]
         for n, ref in enumerate(send_refs):
-            ref[k] = power[:, (n + 1) * each : (n + 2) * each].astype(jnp.bfloat16)
+            ref[k, at] = power[:, (n + 1) * each : (n + 2) * each].astype(jnp.bfloat16)
 
     return emit
 
 
-def beams_of(ref, first, count):
-    return [(ref, first + b) for b in range(count)]
-
-
-def own_part_kernel(count, params, rtab, mine, other, spec, lags, dops, r_ref, part_ref, padded, prods, corrs):
-    write_ref_spectra(params, rtab, mine, other, r_ref, padded)
-
-    def emit(k, power):
-        part_ref[k] = power
-
-    sum_powers([(beams_of(spec, 0, count), r_ref)], lags, dops, prods, corrs, emit)
-
-
-def far_part_kernel(
-    count, params, rtab, mine, other, stab, s_ref, part_ref, lags, dops, r_ref, far_spec, own_ref, *refs
+def own_part_kernel(params, rtab, mine, spec, lags, dops, part_ref, padded, r_here, prods, corrs):
+    first = first_tx(params, 0)
+    write_ref_spectra(params, first, rtab, mine, r_here, padded)
+
+    def emit(k, at, power):
+        part_ref[k, at] = power
+
+    sum_powers([(spec, r_here)], first, lags, dops, prods, corrs, emit)
+
+
+def far_part_kernel(params, rtab, far, stab, there, part_ref, lags, dops, far_spec, own_ref, *refs):
+    send_refs, (padded, r_there, prods, corrs) = refs[:-4], refs[-4:]
+    first = first_tx(params, 0)
+    write_ref_spectra(params, first, rtab, far, r_there, padded)
+    surv_spectra_kernel(stab, there, far_spec)
+    store = emit_chunks(own_ref, send_refs)
+    emit = lambda k, at, power: store(k, at, power + part_ref[k, at])
+    sum_powers([(far_spec, r_there)], first, lags, dops, prods, corrs, emit)
+
+
+def both_kernel(
+    params, rtab, mine, far, spec, far_spec, near_ref, lags, dops, own_ref, near_all, *refs
 ):
-    send_refs, (padded, prods, corrs) = refs[:-3], refs[-3:]
-    write_ref_spectra(params, rtab, mine, other, r_ref, padded)
-    surv_spectra_kernel(stab, s_ref, far_spec)
-    store = emit_chunks(own_ref, send_refs)
-    emit = lambda k, power: store(k, power + part_ref[k])
-    sum_powers([(beams_of(far_spec, 0, count), r_ref)], lags, dops, prods, corrs, emit)
-
-
-def both_kernel(first, count, spec, far_spec, r_here, r_there, lags, dops, own_ref, *refs):
-    send_refs, (prods, corrs) = refs[:-2], refs[-2:]
-    emit = emit_chunks(own_ref, send_refs)
-    segments = [(beams_of(s, first, count), r) for s, r in ((spec, r_here), (far_spec, r_there))]
-    sum_powers(segments, lags, dops, prods, corrs, emit)
-
-
-def assemble_kernel(n_seg, sizes, params, *refs):
-    out_ref = refs[-1]
-    groups = [refs[g * n_seg : (g + 1) * n_seg] for g in range(len(sizes))]
+    send_refs, (padded, r_here, r_there, prods, corrs) = refs[:-5], refs[-5:]
+    first = first_tx(params, 1)
+    write_ref_spectra(params, first, rtab, mine, r_here, padded)
+    write_ref_spectra(params, first, rtab, far, r_there, padded)
+    near_all[:HALF_TX] = near_ref[...]
+    emit = emit_chunks(own_ref, (near_all.at[HALF_TX:], *send_refs))
+    sum_powers([(spec, r_here), (far_spec, r_there)], first, lags, dops, prods, corrs, emit)
+
+
+def assemble_kernel(n_seg, params, near_ref, *refs):
+    groups, (out_ref, mean, sems) = refs[:-3], refs[-3:]
     half = out_ref.shape[1] // 2
     part = params[2 * TX + 1] % 2
 
-    def total(refs, k):
-        return functools.reduce(jnp.add, [r[k].astype(jnp.float32) for r in refs]) * (1.0 / n_seg)
-
-    for k in range(TX):
-        first = 0
-        for size, group in zip(sizes, groups, strict=True):
-            out_ref[k, pl.ds(part * half + first, size)] = total(group[::2], k)
-            out_ref[k, pl.ds((1 - part) * half + first, size)] = total(group[1::2], k)
-            first += size
-
-
-def call_powers(kernel, name, args, out_shape, count, segments, ref_spectra):
-    padded = pltpu.VMEM((BLOCKS + 2 * PAD, PAIR), jnp.float32)
-    work = [
-        pltpu.VMEM((segments, 2 * FFT, count * BLOCKS), jnp.bfloat16),
-        pltpu.VMEM((2, segments * count * DELAYS, 2 * BLOCKS), jnp.bfloat16),
-    ]
+    def total(values):
+        return functools.reduce(jnp.add, [v.astype(jnp.float32) for v in values]) * (1.0 / n_seg)
+
+    copies = []
+    for g in range(2):
+        own, *arrived = groups[g * (n_seg - 1) : (g + 1) * (n_seg - 1)]
+        for k in range(HALF_TX):
+            at = g * HALF_TX + k
+            mean[at, pl.ds(part * half, half)] = total([r[k] for r in (own, *arrived[0::2])])
+            theirs = total([near_ref[at]] + [r[k] for r in arrived[1::2]])
+            mean[at, pl.ds((1 - part) * half, half)] = theirs
+            copy = pltpu.make_async_copy(
+                mean.at[at], out_ref.at[first_tx(params, g) + k], sems.at[at]
+            )
+            copy.start()
+            copies.append(copy)
+    for copy in copies:
+        copy.wait()
+
+
+def call_powers(kernel, name, args, out_shape, count, segments, flops):
     return pl.pallas_call(
         kernel,
         in_specs=[SMEM if a.ndim == 1 else VMEM for a in args],
         out_specs=[VMEM] * len(out_shape),
         out_shape=out_shape,
-        scratch_shapes=[padded] * ref_spectra + work,
-        compiler_params=pltpu.CompilerParams(vmem_limit_bytes=VMEM_LIMIT),
-        cost_estimate=pl.CostEstimate(
-            flops=segments * count * TX * 2 * 768 * 65536, bytes_accessed=6 << 20, transcendentals=0
-        ),
+        scratch_shapes=[pltpu.VMEM((BLOCKS + 2 * PAD, PAIR), jnp.float32)]
+        + [pltpu.VMEM((HALF_TX, 2 * FFT, BLOCKS), jnp.float32)] * segments
+        + [
+            pltpu.VMEM((segments, 2 * FFT, count * BLOCKS), jnp.bfloat16),
+            pltpu.VMEM((HALF_TX, segments * count * DELAYS, 2 * BLOCKS), jnp.bfloat16),
+        ],
+        compiler_params=pltpu.CompilerParams(vmem_limit_bytes=VMEM_LIMIT * count // 8),
+        cost_estimate=pl.CostEstimate(flops=flops, bytes_accessed=1 << 20, transcendentals=0),
         name=name,
     )(*args)
 
@@ -406,62 +419,54 @@
     half = functools.reduce(jnp.add, got, half)
     other = swap(half, "beam", 1)
     far = swap(half, "seg", 1)
-    leaving, there = lax.optimization_barrier((other, there))
-    far_other = swap(leaving, "seg", 1)
-
+    far_other = swap(other, "seg", 1)
+    spec, there = lax.optimization_barrier((spec, there))
+    count = beams_here // 2
     each = DELAYS // n_seg
-    r_shape = jax.ShapeDtypeStruct((TX, 2 * FFT, BLOCKS), jnp.float32)
-    chunks = lambda n: [jax.ShapeDtypeStruct((TX, n, each, DOPPLER), jnp.float32)] + [
-        jax.ShapeDtypeStruct((TX, n, each, DOPPLER), jnp.bfloat16)
-    ] * (n_seg - 1)
-    sizes = [n * beams_here // 16 for n in GROUPS]
-    count = sizes[0]
-    r_here, part = call_powers(
-        functools.partial(own_part_kernel, count),
+    kept = lambda n: jax.ShapeDtypeStruct((HALF_TX, count, n, DOPPLER), jnp.float32)
+    sent = lambda n: jax.ShapeDtypeStruct((n, count, each, DOPPLER), jnp.bfloat16)
+    (part,) = call_powers(
+        own_part_kernel,
         "own_part",
-        (params, rtab, half, other, spec, lags, dops),
-        [r_shape, jax.ShapeDtypeStruct((TX, count, DELAYS, DOPPLER), jnp.float32)],
+        (params, rtab, half, spec, lags, dops),
+        [kept(DELAYS)],
         count,
         1,
-        True,
-    )
-    behind = []
-    collected = []
-    first = 0
-    for g, count in enumerate(sizes):
-        if g == 0:
-            r_there, far_spec, own, *sends = call_powers(
-                functools.partial(far_part_kernel, count),
-                "far_part",
-                (params, rtab, far, far_other, stab, there, part, lags, dops),
-                [r_shape, jax.ShapeDtypeStruct(spec.shape, spec.dtype)] + chunks(count),
-                count,
-                1,
-                True,
-            )
-        else:
-            own, *sends = call_powers(
-                functools.partial(both_kernel, first, count),
-                "both",
-                (spec, far_spec, r_here, r_there, lags, dops),
-                chunks(count),
-                count,
-                2,
-                False,
-            )
-        sends[0], *behind = lax.optimization_barrier((sends[0], *behind))
-        arrived = [swap(s, "seg", n + 1) for n, s in enumerate(sends)]
-        collected += [own] + arrived
-        behind = arrived[1:]
-        first += count
+        OWN_FLOPS,
+    )
+    far_spec, own, near, *long_way = call_powers(
+        far_part_kernel,
+        "far_part",
+        (params, rtab, far, stab, there, part, lags, dops),
+        [jax.ShapeDtypeStruct(spec.shape, spec.dtype), kept(each)] + [sent(HALF_TX)] * (n_seg - 1),
+        count,
+        1,
+        FAR_FLOPS,
+    )
+    arrived = [swap(s, "seg", n) for n, s in enumerate(long_way, 2)]
+    collected = [own] + arrived
+    own, near, *long_way = call_powers(
+        both_kernel,
+        "both",
+        (params, rtab, other, far_other, spec, far_spec, near, lags, dops),
+        [kept(each), sent(TX)] + [sent(HALF_TX)] * (n_seg - 2),
+        count,
+        2,
+        BOTH_FLOPS,
+    )
+    near = swap(near, "seg", 1)
+    long_way[-1], *arrived = lax.optimization_barrier((long_way[-1], *arrived))
+    collected += [own] + [swap(s, "seg", n) for n, s in enumerate(long_way, 2)]
+    out = (TX, beams_here, each, DOPPLER)
     return pl.pallas_call(
-        functools.partial(assemble_kernel, n_seg, sizes),
-        in_specs=[SMEM] + [VMEM] * len(collected),
-        out_specs=VMEM,
-        out_shape=jax.ShapeDtypeStruct((TX, beams_here, each, DOPPLER), jnp.float32),
+        functools.partial(assemble_kernel, n_seg),
+        in_specs=[SMEM] + [VMEM] * (1 + len(collected)),
+        out_specs=pl.BlockSpec(memory_space=pl.ANY),
+        out_shape=jax.ShapeDtypeStruct(out, jnp.float32),
+        scratch_shapes=[pltpu.VMEM(out, jnp.float32), pltpu.SemaphoreType.DMA((TX,))],
         compiler_params=pltpu.CompilerParams(vmem_limit_bytes=VMEM_LIMIT),
         name="assemble",
-    )(params, *collected)
+    )(params, near, *collected)
 
 
 def solution(mesh):

time: 62.1 us -> 60.3 us (0.971)
  starting transfers between devices: 22 us -> 18.7 us
  waiting for transfers between devices: 13.6 us -> 14.4 us
    ppermute x14 -> x13, starting transfers between devices: 22 us -> 18.7 us  [swap(): return lax.ppermute(value, axis, [(i, i ^ flip) for i in range(size)])]
    ppermute x14 -> x13, waiting for transfers between devices: 13.6 us -> 14.4 us  [swap(): return lax.ppermute(value, axis, [(i, i ^ flip) for i in range(size)])]
  transfers between devices with their start and end apart: 14 -> 13, of which waited for: 7 -> 6; matrix products, arithmetic and copies ran while one was open for 0% -> 0% of each run, Pallas kernels for 20% -> 31%
where the time goes in v5:
time: 60.3 us; the launch traced here: 60.1 us
  Pallas kernels  26.6 us (44%)
  starting transfers between devices  18.7 us (31%)
  waiting for transfers between devices  14.4 us (24%)
    ppermute x13, starting transfers between devices, swap(): return lax.ppermute(value, axis, [(i, i ^ flip) for i in range(size)])  18.7 us
    pallas_call x3, Pallas kernels, call_powers(): pl.pallas_call(kernel, in_specs=[SMEM if a.ndim == 1 else VMEM for a in a...  17.1 us
    ppermute x13, waiting for transfers between devices, swap(): return lax.ppermute(value, axis, [(i, i ^ flip) for i in range(size)])  14.4 us
    pallas_call x1, Pallas kernels, decimate(): pl.pallas_call(functools.partial(decimate_kernel, beams), in_specs=[SMEM]...  6.26 us
    pallas_call x1, Pallas kernels, shards(): pl.pallas_call(functools.partial(assemble_kernel, n_seg), in_specs=[SMEM]...  1.57 us
  transfers between devices with their start and end apart: 13, of which 6 were waited for; matrix products, arithmetic and copies ran while one was open for 0% of the time, Pallas kernels for 31%

profile of v5, /device:TPU:0, one launch (start us, length us, event | category | flops | bytes accessed | tf_op | source)
XLA Modules:
  0.0 60.1 jit_solution(14107504122966822954)
XLA Ops:
  0.0 0.0 copy-start.3
  0.0 0.1 pad_add_fusion.ids
  0.1 0.0 copy-start.1
  0.1 0.0 copy-start.2
  0.1 6.3 %decimate.1 = (bf16[8,256,128]{2,1,0:T(8,128)(2,1)S(1)}, bf16[8,256,128]{2,1,0:T(8,128)(2,1)S(1)}, bf16[2,256,128]{2,1,0:T(8,128)(2,1)S(1)}, bf16[2,256,128]{2,1,0:T(8,128)(2,1)S(1)}, s32[10]{0:T(128)S(1)}) custom-call(s32[2]{0:T(128)S(1)} %pad_add_fusion.ids, s32[4]{0:T(128)} %owner.1, s32[4]{0:T(128)} %delay.1, s32[4]{0:T(128)} %doppler.1, ...), custom_call_target="tpu_custom_call" | custom-call | tf_op jit(solution)/shard_map/decimate/pallas_call | solution.py:183
  6.4 0.0 copy-start
  6.4 0.5 collective-permute-start
  6.9 2.7 %collective-permute-start.6 = (bf16[8,256,128]{2,1,0:T(8,128)(2,1)S(1)}, bf16[8,256,128]{2,1,0:T(8,128)(2,1)S(1)}, u32[]{:S(2)}, u32[]{:S(2)}) collective-permute-start(bf16[8,256,128]{2,1,0:T(8,128)(2,1)S(1)} %get-tuple-element.46), channel_id=1, source_target_pairs={{0,1},{1,0},{2,3},{3,2},{4,5},{5,4},{6,7},{7,6},{8,9},{9,8},{10,11... | collective-permute-start | bytes 1572872 | tf_op jit(solution)/shard_map/ppermute | solution.py:392
  9.6 0.0 collective-permute-done
  9.6 1.5 %collective-permute-start.1 = (bf16[2,256,128]{2,1,0:T(8,128)(2,1)S(1)}, bf16[2,256,128]{2,1,0:T(8,128)(2,1)S(1)}, u32[]{:S(2)}, u32[]{:S(2)}) collective-permute-start(bf16[2,256,128]{2,1,0:T(8,128)(2,1)S(1)} %add.12), channel_id=1, source_target_pairs={{0,8},{4,12},{8,0},{12,4},{16,24},{20,28},{24,16},{28,20},{1,9},{5... | collective-permute-start | bytes 393224 | tf_op jit(solution)/shard_map/ppermute | solution.py:392
  11.1 1.5 %collective-permute-start.2 = (bf16[2,256,128]{2,1,0:T(8,128)(2,1)S(1)}, bf16[2,256,128]{2,1,0:T(8,128)(2,1)S(1)}, u32[]{:S(2)}, u32[]{:S(2)}) collective-permute-start(bf16[2,256,128]{2,1,0:T(8,128)(2,1)S(1)} %add.12), channel_id=1, source_target_pairs={{0,16},{4,20},{8,24},{12,28},{16,0},{20,4},{24,8},{28,12},{1,17},{... | collective-permute-start | bytes 393224 | tf_op jit(solution)/shard_map/ppermute | solution.py:392
  12.7 0.5 collective-permute-start.3
  13.2 0.0 copy-done.3
  13.2 0.7 %own_spectra.1.spec = f32[8,512,256]{2,1,0:T(8,128)S(1)} custom-call(bf16[512,256]{1,0:T(8,128)(2,1)S(1)} %copy-done.3, bf16[8,256,128]{2,1,0:T(8,128)(2,1)S(1)} %get-tuple-element.41.s_ref), custom_call_target="tpu_custom_call" | custom-call | tf_op jit(solution)/shard_map/own_spectra/pallas_call | solution.py:265
  13.9 0.0 copy-done.1
  13.9 0.0 copy-done.2
  13.9 1.0 %tables.1 = (bf16[4,256,512]{2,1,0:T(8,128)(2,1)S(1)}, bf16[4,512,256]{2,1,0:T(8,128)(2,1)S(1)}) custom-call(s32[10]{0:T(128)S(1)} %get-tuple-element.37.params, f32[2,4,192,128]{3,2,1,0:T(8,128)S(1)} %copy-done.2, f32[2,4,256,128]{3,2,1,0:T(8,128)S(1)} %copy-done.1), custom_call_target="tpu_custom_call" | custom-call | tf_op jit(solution)/shard_map/tables/pallas_call | solution.py:222
  14.9 0.7 %collective-permute-done.1 = bf16[2,256,128]{2,1,0:T(8,128)(2,1)S(1)} collective-permute-done((bf16[2,256,128]{2,1,0:T(8,128)(2,1)S(1)}, bf16[2,256,128]{2,1,0:T(8,128)(2,1)S(1)}, u32[]{:S(2)}, u32[]{:S(2)}) %collective-permute-start.1) | collective-permute-done | bytes 131104 | tf_op jit(solution)/shard_map/ppermute | solution.py:392
  15.6 3.7 %collective-permute-done.2 = bf16[2,256,128]{2,1,0:T(8,128)(2,1)S(1)} collective-permute-done((bf16[2,256,128]{2,1,0:T(8,128)(2,1)S(1)}, bf16[2,256,128]{2,1,0:T(8,128)(2,1)S(1)}, u32[]{:S(2)}, u32[]{:S(2)}) %collective-permute-start.2) | collective-permute-done | bytes 131104 | tf_op jit(solution)/shard_map/ppermute | solution.py:392
  19.2 0.0 collective-permute-done.3
  19.3 0.1 collective-permute-start.4
  19.4 1.3 %collective-permute-start.7 = (bf16[2,256,128]{2,1,0:T(8,128)(2,1)S(1)}, bf16[2,256,128]{2,1,0:T(8,128)(2,1)S(1)}, u32[]{:S(2)}, u32[]{:S(2)}) collective-permute-start(bf16[2,256,128]{2,1,0:T(8,128)(2,1)S(1)} %add_add_fusion.mine), channel_id=1, source_target_pairs={{0,1},{1,0},{2,3},{3,2},{4,5},{5,4},{6,7},{7,6},{8,9},{9,8},{10,11... | collective-permute-start | bytes 393224 | tf_op jit(solution)/shard_map/ppermute | solution.py:392
  20.7 0.0 collective-permute-done.4.mine
  20.7 1.2 %collective-permute-start.5 = (bf16[2,256,128]{2,1,0:T(8,128)(2,1)S(1)}, bf16[2,256,128]{2,1,0:T(8,128)(2,1)S(1)}, u32[]{:S(2)}, u32[]{:S(2)}) collective-permute-start(bf16[2,256,128]{2,1,0:T(8,128)(2,1)S(1)} %collective-permute-done.4.mine), channel_id=1, source_target_pairs={{0,1},{1,0},{2,3},{3,2},{4,5},{5,4},{6,7},{7,6},{8,9},{9,8},{10,11... | collective-permute-start | bytes 393224 | tf_op jit(solution)/shard_map/ppermute | solution.py:392
  21.9 0.1 collective-permute-done.6.there
  22.1 0.0 copy-done
  22.1 4.1 %own_part.1.part_ref = f32[2,8,128,128]{3,2,1,0:T(8,128)S(1)} custom-call(s32[10]{0:T(128)S(1)} %get-tuple-element.37.params, bf16[512,1024]{1,0:T(8,128)(2,1)S(1)} %copy-done, bf16[2,256,128]{2,1,0:T(8,128)(2,1)S(1)} %add_add_fusion.mine, f32[8,512,256]{2,1,0:T(8,128)S(1)} %own_spectra.1.spec, bf16[4,256,512]{2,1,0:T(8,128)(2,1)S(1)} %get-tuple-element.49.lags, ...), custom_call_target="tpu_custom_call" | custom-call | flops 1600000000 | bytes 1048576 | tf_op jit(solution)/shard_map/own_part/pallas_call | solution.py:373
  26.2 0.0 collective-permute-done.7.far
  26.2 5.0 %far_part.1 = (f32[8,512,256]{2,1,0:T(8,128)S(1)}, f32[2,8,32,128]{3,2,1,0:T(8,128)S(1)}, bf16[2,8,32,128]{3,2,1,0:T(8,128)(2,1)S(1)}, bf16[2,8,32,128]{3,2,1,0:T(8,128)(2,1)S(1)}, bf16[2,8,32,128]{3,2,1,0:T(8,128)(2,1)S(1)}) custom-call(s32[10]{0:T(128)S(1)} %get-tuple-element.37.params, bf16[512,1024]{1,0:T(8,128)(2,1)S(1)} %copy-done, ...), custom_call_target="tpu_custom_call" | custom-call | flops 1600000000 | bytes 1048576 | tf_op jit(solution)/shard_map/far_part/pallas_call | solution.py:373
  31.2 3.9 %collective-permute-start.10 = (bf16[2,8,32,128]{3,2,1,0:T(8,128)(2,1)S(1)}, bf16[2,8,32,128]{3,2,1,0:T(8,128)(2,1)S(1)}, u32[]{:S(2)}, u32[]{:S(2)}) collective-permute-start(bf16[2,8,32,128]{3,2,1,0:T(8,128)(2,1)S(1)} %get-tuple-element.56), channel_id=1, source_target_pairs={{0,3},{1,2},{2,1},{3,0},{4,7},{5,6},{6,5},{7,4},{8,11},{9,10},{10,... | collective-permute-start | bytes 393224 | tf_op jit(solution)/shard_map/ppermute | solution.py:392
  35.0 0.0 collective-permute-start.9
  35.0 0.0 collective-permute-done.5.far
  35.0 8.0 %both.1 = (f32[2,8,32,128]{3,2,1,0:T(8,128)S(1)}, bf16[4,8,32,128]{3,2,1,0:T(8,128)(2,1)S(1)}, bf16[2,8,32,128]{3,2,1,0:T(8,128)(2,1)S(1)}, bf16[2,8,32,128]{3,2,1,0:T(8,128)(2,1)S(1)}) custom-call(s32[10]{0:T(128)S(1)} %get-tuple-element.37.params, bf16[512,1024]{1,0:T(8,128)(2,1)S(1)} %copy-done, bf16[2,256,128]{2,1,0:T(8,128)(2,1)S(1)} %collective-permute-done.4.mine, ...), custom_call_target="tpu_custom_call" | custom-call | flops 3200000000 | bytes 1048576 | tf_op jit(solution)/shard_map/both/pallas_call | solution.py:373
  43.1 0.7 %collective-permute-start.8 = (bf16[4,8,32,128]{3,2,1,0:T(8,128)(2,1)S(1)}, bf16[4,8,32,128]{3,2,1,0:T(8,128)(2,1)S(1)}, u32[]{:S(2)}, u32[]{:S(2)}) collective-permute-start(bf16[4,8,32,128]{3,2,1,0:T(8,128)(2,1)S(1)} %get-tuple-element.53), channel_id=1, source_target_pairs={{0,1},{1,0},{2,3},{3,2},{4,5},{5,4},{6,7},{7,6},{8,9},{9,8},{10,11... | collective-permute-start | bytes 786440 | tf_op jit(solution)/shard_map/ppermute | solution.py:392
  43.8 2.4 %collective-permute-start.11 = (bf16[2,8,32,128]{3,2,1,0:T(8,128)(2,1)S(1)}, bf16[2,8,32,128]{3,2,1,0:T(8,128)(2,1)S(1)}, u32[]{:S(2)}, u32[]{:S(2)}) collective-permute-start(bf16[2,8,32,128]{3,2,1,0:T(8,128)(2,1)S(1)} %get-tuple-element.58), channel_id=1, source_target_pairs={{0,2},{1,3},{2,0},{3,1},{4,6},{5,7},{6,4},{7,5},{8,10},{9,11},{10,... | collective-permute-start | bytes 393224 | tf_op jit(solution)/shard_map/ppermute | solution.py:392
  46.1 0.0 collective-permute-done.10.refs_2_
  46.1 0.0 collective-permute-done.9.refs_1_
  46.1 2.3 %collective-permute-start.12 = (bf16[2,8,32,128]{3,2,1,0:T(8,128)(2,1)S(1)}, bf16[2,8,32,128]{3,2,1,0:T(8,128)(2,1)S(1)}, u32[]{:S(2)}, u32[]{:S(2)}) collective-permute-start(bf16[2,8,32,128]{3,2,1,0:T(8,128)(2,1)S(1)} %get-tuple-element.60), channel_id=1, source_target_pairs={{0,3},{1,2},{2,1},{3,0},{4,7},{5,6},{6,5},{7,4},{8,11},{9,10},{10,... | collective-permute-start | bytes 393224 | tf_op jit(solution)/shard_map/ppermute | solution.py:392
  48.5 4.6 %collective-permute-done.11.refs_4_ = bf16[2,8,32,128]{3,2,1,0:T(8,128)(2,1)S(1)} collective-permute-done((bf16[2,8,32,128]{3,2,1,0:T(8,128)(2,1)S(1)}, bf16[2,8,32,128]{3,2,1,0:T(8,128)(2,1)S(1)}, u32[]{:S(2)}, u32[]{:S(2)}) %collective-permute-start.11) | collective-permute-done | bytes 131104 | tf_op jit(solution)/shard_map/ppermute | solution.py:392
  53.1 2.0 %collective-permute-done.8.near_ref = bf16[4,8,32,128]{3,2,1,0:T(8,128)(2,1)S(1)} collective-permute-done((bf16[4,8,32,128]{3,2,1,0:T(8,128)(2,1)S(1)}, bf16[4,8,32,128]{3,2,1,0:T(8,128)(2,1)S(1)}, u32[]{:S(2)}, u32[]{:S(2)}) %collective-permute-start.8) | collective-permute-done | bytes 262176 | tf_op jit(solution)/shard_map/ppermute | solution.py:392
  55.1 3.3 %collective-permute-done.12.refs_5_ = bf16[2,8,32,128]{3,2,1,0:T(8,128)(2,1)S(1)} collective-permute-done((bf16[2,8,32,128]{3,2,1,0:T(8,128)(2,1)S(1)}, bf16[2,8,32,128]{3,2,1,0:T(8,128)(2,1)S(1)}, u32[]{:S(2)}, u32[]{:S(2)}) %collective-permute-start.12) | collective-permute-done | bytes 131104 | tf_op jit(solution)/shard_map/ppermute | solution.py:392
  58.4 1.6 %assemble.1 = f32[4,16,32,128]{3,2,1,0:T(8,128)} custom-call(s32[10]{0:T(128)S(1)} %get-tuple-element.37.params, bf16[4,8,32,128]{3,2,1,0:T(8,128)(2,1)S(1)} %collective-permute-done.8.near_ref, f32[2,8,32,128]{3,2,1,0:T(8,128)S(1)} %get-tuple-element.54.refs_0_, bf16[2,8,32,128]{3,2,1,0:T(8,128)(2,1)S(1)} %collective-permute-done.9.refs_1_, ...), custom_call_target="tpu_custom_call" | custom-call | tf_op jit(solution)/shard_map/assemble/pallas_call | solution.py:461
  (2 shorter events, 0.1 us)
Async XLA Ops:
  0.0 13.2 %copy-start.3 = (bf16[512,256]{1,0:T(8,128)(2,1)S(1)}, bf16[512,256]{1,0:T(8,128)(2,1)}, u32[]{:S(2)}) copy-start(bf16[512,256]{1,0:T(8,128)(2,1)} %constant.17.clone.table_ref.stab) | copy-start | bytes 786436
  0.1 13.8 %copy-start.1 = (f32[2,4,256,128]{3,2,1,0:T(8,128)S(1)}, f32[2,4,256,128]{3,2,1,0:T(8,128)}, u32[]{:S(2)}) copy-start(f32[2,4,256,128]{3,2,1,0:T(8,128)} %constant.20.clone.dop_ref) | copy-start | bytes 3145732
  0.1 13.8 %copy-start.2 = (f32[2,4,192,128]{3,2,1,0:T(8,128)S(1)}, f32[2,4,192,128]{3,2,1,0:T(8,128)}, u32[]{:S(2)}) copy-start(f32[2,4,192,128]{3,2,1,0:T(8,128)} %constant.19.clone.lag_ref) | copy-start | bytes 2359300
  6.4 15.7 %copy-start = (bf16[512,1024]{1,0:T(8,128)(2,1)S(1)}, bf16[512,1024]{1,0:T(8,128)(2,1)}, u32[]{:S(2)}) copy-start(bf16[512,1024]{1,0:T(8,128)(2,1)} %constant.18.clone.rtab) | copy-start | bytes 3145732
  6.4 3.2 %collective-permute-start = (bf16[2,256,128]{2,1,0:T(8,128)(2,1)S(1)}, bf16[2,256,128]{2,1,0:T(8,128)(2,1)S(1)}, u32[]{:S(2)}, u32[]{:S(2)}) collective-permute-start(bf16[2,256,128]{2,1,0:T(8,128)(2,1)S(1)} %get-tuple-element.34), channel_id=1, source_target_pairs={{0,4},{4,0},{8,12},{12,8},{16,20},{20,16},{24,28},{28,24},{1,5},{5... | collective-permute-start | bytes 393224 | tf_op jit(solution)/shard_map/ppermute | solution.py:392
  6.9 15.2 %collective-permute-start.6 = (bf16[8,256,128]{2,1,0:T(8,128)(2,1)S(1)}, bf16[8,256,128]{2,1,0:T(8,128)(2,1)S(1)}, u32[]{:S(2)}, u32[]{:S(2)}) collective-permute-start(bf16[8,256,128]{2,1,0:T(8,128)(2,1)S(1)} %get-tuple-element.46), channel_id=1, source_target_pairs={{0,1},{1,0},{2,3},{3,2},{4,5},{5,4},{6,7},{7,6},{8,9},{9,8},{10,11... | collective-permute-start | bytes 1572872 | tf_op jit(solution)/shard_map/ppermute | solution.py:392
  9.6 6.0 %collective-permute-start.1 = (bf16[2,256,128]{2,1,0:T(8,128)(2,1)S(1)}, bf16[2,256,128]{2,1,0:T(8,128)(2,1)S(1)}, u32[]{:S(2)}, u32[]{:S(2)}) collective-permute-start(bf16[2,256,128]{2,1,0:T(8,128)(2,1)S(1)} %add.12), channel_id=1, source_target_pairs={{0,8},{4,12},{8,0},{12,4},{16,24},{20,28},{24,16},{28,20},{1,9},{5... | collective-permute-start | bytes 393224 | tf_op jit(solution)/shard_map/ppermute | solution.py:392
  11.1 8.1 %collective-permute-start.2 = (bf16[2,256,128]{2,1,0:T(8,128)(2,1)S(1)}, bf16[2,256,128]{2,1,0:T(8,128)(2,1)S(1)}, u32[]{:S(2)}, u32[]{:S(2)}) collective-permute-start(bf16[2,256,128]{2,1,0:T(8,128)(2,1)S(1)} %add.12), channel_id=1, source_target_pairs={{0,16},{4,20},{8,24},{12,28},{16,0},{20,4},{24,8},{28,12},{1,17},{... | collective-permute-start | bytes 393224 | tf_op jit(solution)/shard_map/ppermute | solution.py:392
  12.7 6.6 %collective-permute-start.3 = (bf16[2,256,128]{2,1,0:T(8,128)(2,1)S(1)}, bf16[2,256,128]{2,1,0:T(8,128)(2,1)S(1)}, u32[]{:S(2)}, u32[]{:S(2)}) collective-permute-start(bf16[2,256,128]{2,1,0:T(8,128)(2,1)S(1)} %add.12), channel_id=1, source_target_pairs={{0,24},{4,28},{8,16},{12,20},{16,8},{20,12},{24,0},{28,4},{1,25},{... | collective-permute-start | bytes 393224 | tf_op jit(solution)/shard_map/ppermute | solution.py:392
  19.3 1.4 %collective-permute-start.4 = (bf16[2,256,128]{2,1,0:T(8,128)(2,1)S(1)}, bf16[2,256,128]{2,1,0:T(8,128)(2,1)S(1)}, u32[]{:S(2)}, u32[]{:S(2)}) collective-permute-start(bf16[2,256,128]{2,1,0:T(8,128)(2,1)S(1)} %add_add_fusion.mine), channel_id=1, source_target_pairs={{0,4},{4,0},{8,12},{12,8},{16,20},{20,16},{24,28},{28,24},{1,5},{5... | collective-permute-start | bytes 393224 | tf_op jit(solution)/shard_map/ppermute | solution.py:392
  19.4 6.8 %collective-permute-start.7 = (bf16[2,256,128]{2,1,0:T(8,128)(2,1)S(1)}, bf16[2,256,128]{2,1,0:T(8,128)(2,1)S(1)}, u32[]{:S(2)}, u32[]{:S(2)}) collective-permute-start(bf16[2,256,128]{2,1,0:T(8,128)(2,1)S(1)} %add_add_fusion.mine), channel_id=1, source_target_pairs={{0,1},{1,0},{2,3},{3,2},{4,5},{5,4},{6,7},{7,6},{8,9},{9,8},{10,11... | collective-permute-start | bytes 393224 | tf_op jit(solution)/shard_map/ppermute | solution.py:392
  20.7 14.4 %collective-permute-start.5 = (bf16[2,256,128]{2,1,0:T(8,128)(2,1)S(1)}, bf16[2,256,128]{2,1,0:T(8,128)(2,1)S(1)}, u32[]{:S(2)}, u32[]{:S(2)}) collective-permute-start(bf16[2,256,128]{2,1,0:T(8,128)(2,1)S(1)} %collective-permute-done.4.mine), channel_id=1, source_target_pairs={{0,1},{1,0},{2,3},{3,2},{4,5},{5,4},{6,7},{7,6},{8,9},{9,8},{10,11... | collective-permute-start | bytes 393224 | tf_op jit(solution)/shard_map/ppermute | solution.py:392
  31.2 15.0 %collective-permute-start.10 = (bf16[2,8,32,128]{3,2,1,0:T(8,128)(2,1)S(1)}, bf16[2,8,32,128]{3,2,1,0:T(8,128)(2,1)S(1)}, u32[]{:S(2)}, u32[]{:S(2)}) collective-permute-start(bf16[2,8,32,128]{3,2,1,0:T(8,128)(2,1)S(1)} %get-tuple-element.56), channel_id=1, source_target_pairs={{0,3},{1,2},{2,1},{3,0},{4,7},{5,6},{6,5},{7,4},{8,11},{9,10},{10,... | collective-permute-start | bytes 393224 | tf_op jit(solution)/shard_map/ppermute | solution.py:392
  35.0 11.1 %collective-permute-start.9 = (bf16[2,8,32,128]{3,2,1,0:T(8,128)(2,1)S(1)}, bf16[2,8,32,128]{3,2,1,0:T(8,128)(2,1)S(1)}, u32[]{:S(2)}, u32[]{:S(2)}) collective-permute-start(bf16[2,8,32,128]{3,2,1,0:T(8,128)(2,1)S(1)} %get-tuple-element.55), channel_id=1, source_target_pairs={{0,2},{1,3},{2,0},{3,1},{4,6},{5,7},{6,4},{7,5},{8,10},{9,11},{10,... | collective-permute-start | bytes 393224 | tf_op jit(solution)/shard_map/ppermute | solution.py:392
  43.1 12.0 %collective-permute-start.8 = (bf16[4,8,32,128]{3,2,1,0:T(8,128)(2,1)S(1)}, bf16[4,8,32,128]{3,2,1,0:T(8,128)(2,1)S(1)}, u32[]{:S(2)}, u32[]{:S(2)}) collective-permute-start(bf16[4,8,32,128]{3,2,1,0:T(8,128)(2,1)S(1)} %get-tuple-element.53), channel_id=1, source_target_pairs={{0,1},{1,0},{2,3},{3,2},{4,5},{5,4},{6,7},{7,6},{8,9},{9,8},{10,11... | collective-permute-start | bytes 786440 | tf_op jit(solution)/shard_map/ppermute | solution.py:392
  43.8 9.3 %collective-permute-start.11 = (bf16[2,8,32,128]{3,2,1,0:T(8,128)(2,1)S(1)}, bf16[2,8,32,128]{3,2,1,0:T(8,128)(2,1)S(1)}, u32[]{:S(2)}, u32[]{:S(2)}) collective-permute-start(bf16[2,8,32,128]{3,2,1,0:T(8,128)(2,1)S(1)} %get-tuple-element.58), channel_id=1, source_target_pairs={{0,2},{1,3},{2,0},{3,1},{4,6},{5,7},{6,4},{7,5},{8,10},{9,11},{10,... | collective-permute-start | bytes 393224 | tf_op jit(solution)/shard_map/ppermute | solution.py:392
  46.1 12.2 %collective-permute-start.12 = (bf16[2,8,32,128]{3,2,1,0:T(8,128)(2,1)S(1)}, bf16[2,8,32,128]{3,2,1,0:T(8,128)(2,1)S(1)}, u32[]{:S(2)}, u32[]{:S(2)}) collective-permute-start(bf16[2,8,32,128]{3,2,1,0:T(8,128)(2,1)S(1)} %get-tuple-element.60), channel_id=1, source_target_pairs={{0,3},{1,2},{2,1},{3,0},{4,7},{5,6},{6,5},{7,4},{8,11},{9,10},{10,... | collective-permute-start | bytes 393224 | tf_op jit(solution)/shard_map/ppermute | solution.py:392

commit v6 on v5

--- a/solution.py
+++ b/solution.py
@@ -420,7 +420,6 @@
     other = swap(half, "beam", 1)
     far = swap(half, "seg", 1)
     far_other = swap(other, "seg", 1)
-    spec, there = lax.optimization_barrier((spec, there))
     count = beams_here // 2
     each = DELAYS // n_seg
     kept = lambda n: jax.ShapeDtypeStruct((HALF_TX, count, n, DOPPLER), jnp.float32)
@@ -434,6 +433,7 @@
         1,
         OWN_FLOPS,
     )
+    part, there = lax.optimization_barrier((part, there))
     far_spec, own, near, *long_way = call_powers(
         far_part_kernel,
         "far_part",
@@ -455,7 +455,7 @@
         BOTH_FLOPS,
     )
     near = swap(near, "seg", 1)
-    long_way[-1], *arrived = lax.optimization_barrier((long_way[-1], *arrived))
+    long_way[0], *arrived = lax.optimization_barrier((long_way[0], *arrived))
     collected += [own] + [swap(s, "seg", n) for n, s in enumerate(long_way, 2)]
     out = (TX, beams_here, each, DOPPLER)
     return pl.pallas_call(

time: 60.3 us -> 58.6 us (0.972)
  starting transfers between devices: 18.7 us -> 16.7 us
    ppermute x13, starting transfers between devices: 18.7 us -> 16.7 us  [swap(): return lax.ppermute(value, axis, [(i, i ^ flip) for i in range(size)])]
  transfers between devices with their start and end apart: 13 -> 13, of which waited for: 6 -> 4; matrix products, arithmetic and copies ran while one was open for 0% -> 0% of each run, Pallas kernels for 31% -> 32%
where the time goes in v6:
time: 58.6 us; the launch traced here: 58.5 us
  Pallas kernels  26.6 us (45%)
  starting transfers between devices  16.7 us (28%)
  waiting for transfers between devices  14.7 us (25%)
    pallas_call x3, Pallas kernels, call_powers(): pl.pallas_call(kernel, in_specs=[SMEM if a.ndim == 1 else VMEM for a in a...  17.1 us
    ppermute x13, starting transfers between devices, swap(): return lax.ppermute(value, axis, [(i, i ^ flip) for i in range(size)])  16.7 us
    ppermute x13, waiting for transfers between devices, swap(): return lax.ppermute(value, axis, [(i, i ^ flip) for i in range(size)])  14.7 us
    pallas_call x1, Pallas kernels, decimate(): pl.pallas_call(functools.partial(decimate_kernel, beams), in_specs=[SMEM]...  6.26 us
    pallas_call x1, Pallas kernels, shards(): pl.pallas_call(functools.partial(assemble_kernel, n_seg), in_specs=[SMEM]...  1.57 us
  transfers between devices with their start and end apart: 13, of which 4 were waited for; matrix products, arithmetic and copies ran while one was open for 0% of the time, Pallas kernels for 32%

profile of v6, /device:TPU:0, one launch (start us, length us, event | category | flops | bytes accessed | tf_op | source)
XLA Modules:
  0.0 58.5 jit_solution(4489827938981506562)
XLA Ops:
  0.0 0.0 copy-start.3
  0.0 0.1 pad_add_fusion.ids
  0.1 0.0 copy-start.1
  0.1 0.0 copy-start.2
  0.1 6.3 %decimate.1 = (bf16[8,256,128]{2,1,0:T(8,128)(2,1)S(1)}, bf16[8,256,128]{2,1,0:T(8,128)(2,1)S(1)}, bf16[2,256,128]{2,1,0:T(8,128)(2,1)S(1)}, bf16[2,256,128]{2,1,0:T(8,128)(2,1)S(1)}, s32[10]{0:T(128)S(1)}) custom-call(s32[2]{0:T(128)S(1)} %pad_add_fusion.ids, s32[4]{0:T(128)} %owner.1, s32[4]{0:T(128)} %delay.1, s32[4]{0:T(128)} %doppler.1, ...), custom_call_target="tpu_custom_call" | custom-call | tf_op jit(solution)/shard_map/decimate/pallas_call | solution.py:183
  6.4 0.0 copy-start
  6.4 0.5 collective-permute-start
  6.9 2.7 %collective-permute-start.7 = (bf16[8,256,128]{2,1,0:T(8,128)(2,1)S(1)}, bf16[8,256,128]{2,1,0:T(8,128)(2,1)S(1)}, u32[]{:S(2)}, u32[]{:S(2)}) collective-permute-start(bf16[8,256,128]{2,1,0:T(8,128)(2,1)S(1)} %get-tuple-element.48), channel_id=1, source_target_pairs={{0,1},{1,0},{2,3},{3,2},{4,5},{5,4},{6,7},{7,6},{8,9},{9,8},{10,11... | collective-permute-start | bytes 1572872 | tf_op jit(solution)/shard_map/ppermute | solution.py:392
  9.6 0.0 collective-permute-done
  9.6 1.5 %collective-permute-start.1 = (bf16[2,256,128]{2,1,0:T(8,128)(2,1)S(1)}, bf16[2,256,128]{2,1,0:T(8,128)(2,1)S(1)}, u32[]{:S(2)}, u32[]{:S(2)}) collective-permute-start(bf16[2,256,128]{2,1,0:T(8,128)(2,1)S(1)} %add.12), channel_id=1, source_target_pairs={{0,8},{4,12},{8,0},{12,4},{16,24},{20,28},{24,16},{28,20},{1,9},{5... | collective-permute-start | bytes 393224 | tf_op jit(solution)/shard_map/ppermute | solution.py:392
  11.1 1.5 %collective-permute-start.2 = (bf16[2,256,128]{2,1,0:T(8,128)(2,1)S(1)}, bf16[2,256,128]{2,1,0:T(8,128)(2,1)S(1)}, u32[]{:S(2)}, u32[]{:S(2)}) collective-permute-start(bf16[2,256,128]{2,1,0:T(8,128)(2,1)S(1)} %add.12), channel_id=1, source_target_pairs={{0,16},{4,20},{8,24},{12,28},{16,0},{20,4},{24,8},{28,12},{1,17},{... | collective-permute-start | bytes 393224 | tf_op jit(solution)/shard_map/ppermute | solution.py:392
  12.7 0.5 collective-permute-start.3
  13.2 0.0 copy-done.3
  13.2 0.7 %own_spectra.1.spec = f32[8,512,256]{2,1,0:T(8,128)S(1)} custom-call(bf16[512,256]{1,0:T(8,128)(2,1)S(1)} %copy-done.3, bf16[8,256,128]{2,1,0:T(8,128)(2,1)S(1)} %get-tuple-element.41.s_ref), custom_call_target="tpu_custom_call" | custom-call | tf_op jit(solution)/shard_map/own_spectra/pallas_call | solution.py:265
  13.9 0.0 copy-done.1
  13.9 0.0 copy-done.2
  13.9 1.0 %tables.1 = (bf16[4,256,512]{2,1,0:T(8,128)(2,1)S(1)}, bf16[4,512,256]{2,1,0:T(8,128)(2,1)S(1)}) custom-call(s32[10]{0:T(128)S(1)} %get-tuple-element.37.params, f32[2,4,192,128]{3,2,1,0:T(8,128)S(1)} %copy-done.2, f32[2,4,256,128]{3,2,1,0:T(8,128)S(1)} %copy-done.1), custom_call_target="tpu_custom_call" | custom-call | tf_op jit(solution)/shard_map/tables/pallas_call | solution.py:222
  14.9 0.7 %collective-permute-done.1 = bf16[2,256,128]{2,1,0:T(8,128)(2,1)S(1)} collective-permute-done((bf16[2,256,128]{2,1,0:T(8,128)(2,1)S(1)}, bf16[2,256,128]{2,1,0:T(8,128)(2,1)S(1)}, u32[]{:S(2)}, u32[]{:S(2)}) %collective-permute-start.1) | collective-permute-done | bytes 131104 | tf_op jit(solution)/shard_map/ppermute | solution.py:392
  15.6 3.7 %collective-permute-done.2 = bf16[2,256,128]{2,1,0:T(8,128)(2,1)S(1)} collective-permute-done((bf16[2,256,128]{2,1,0:T(8,128)(2,1)S(1)}, bf16[2,256,128]{2,1,0:T(8,128)(2,1)S(1)}, u32[]{:S(2)}, u32[]{:S(2)}) %collective-permute-start.2) | collective-permute-done | bytes 131104 | tf_op jit(solution)/shard_map/ppermute | solution.py:392
  19.2 0.0 collective-permute-done.3
  19.3 1.3 %collective-permute-start.6 = (bf16[2,256,128]{2,1,0:T(8,128)(2,1)S(1)}, bf16[2,256,128]{2,1,0:T(8,128)(2,1)S(1)}, u32[]{:S(2)}, u32[]{:S(2)}) collective-permute-start(bf16[2,256,128]{2,1,0:T(8,128)(2,1)S(1)} %add_add_fusion.mine), channel_id=1, source_target_pairs={{0,1},{1,0},{2,3},{3,2},{4,5},{5,4},{6,7},{7,6},{8,9},{9,8},{10,11... | collective-permute-start | bytes 393224 | tf_op jit(solution)/shard_map/ppermute | solution.py:392
  20.6 0.0 collective-permute-start.4
  20.6 0.0 copy-done
  20.6 4.1 %own_part.1.part_ref = f32[2,8,128,128]{3,2,1,0:T(8,128)S(1)} custom-call(s32[10]{0:T(128)S(1)} %get-tuple-element.37.params, bf16[512,1024]{1,0:T(8,128)(2,1)S(1)} %copy-done, bf16[2,256,128]{2,1,0:T(8,128)(2,1)S(1)} %add_add_fusion.mine, f32[8,512,256]{2,1,0:T(8,128)S(1)} %own_spectra.1.spec, bf16[4,256,512]{2,1,0:T(8,128)(2,1)S(1)} %get-tuple-element.46.lags, ...), custom_call_target="tpu_custom_call" | custom-call | flops 1600000000 | bytes 1048576 | tf_op jit(solution)/shard_map/own_part/pallas_call | solution.py:373
  24.7 0.0 collective-permute-done.4.mine
  24.7 0.8 %collective-permute-start.5 = (bf16[2,256,128]{2,1,0:T(8,128)(2,1)S(1)}, bf16[2,256,128]{2,1,0:T(8,128)(2,1)S(1)}, u32[]{:S(2)}, u32[]{:S(2)}) collective-permute-start(bf16[2,256,128]{2,1,0:T(8,128)(2,1)S(1)} %collective-permute-done.4.mine), channel_id=1, source_target_pairs={{0,1},{1,0},{2,3},{3,2},{4,5},{5,4},{6,7},{7,6},{8,9},{9,8},{10,11... | collective-permute-start | bytes 393224 | tf_op jit(solution)/shard_map/ppermute | solution.py:392
  25.6 0.0 collective-permute-done.7.there
  25.6 0.0 collective-permute-done.6.far
  25.6 5.0 %far_part.1 = (f32[8,512,256]{2,1,0:T(8,128)S(1)}, f32[2,8,32,128]{3,2,1,0:T(8,128)S(1)}, bf16[2,8,32,128]{3,2,1,0:T(8,128)(2,1)S(1)}, bf16[2,8,32,128]{3,2,1,0:T(8,128)(2,1)S(1)}, bf16[2,8,32,128]{3,2,1,0:T(8,128)(2,1)S(1)}) custom-call(s32[10]{0:T(128)S(1)} %get-tuple-element.37.params, bf16[512,1024]{1,0:T(8,128)(2,1)S(1)} %copy-done, ...), custom_call_target="tpu_custom_call" | custom-call | flops 1600000000 | bytes 1048576 | tf_op jit(solution)/shard_map/far_part/pallas_call | solution.py:373
  30.5 3.4 %collective-permute-start.10 = (bf16[2,8,32,128]{3,2,1,0:T(8,128)(2,1)S(1)}, bf16[2,8,32,128]{3,2,1,0:T(8,128)(2,1)S(1)}, u32[]{:S(2)}, u32[]{:S(2)}) collective-permute-start(bf16[2,8,32,128]{3,2,1,0:T(8,128)(2,1)S(1)} %get-tuple-element.56), channel_id=1, source_target_pairs={{0,3},{1,2},{2,1},{3,0},{4,7},{5,6},{6,5},{7,4},{8,11},{9,10},{10,... | collective-permute-start | bytes 393224 | tf_op jit(solution)/shard_map/ppermute | solution.py:392
  33.9 0.0 collective-permute-start.9
  33.9 0.0 collective-permute-done.5.far
  33.9 8.0 %both.1 = (f32[2,8,32,128]{3,2,1,0:T(8,128)S(1)}, bf16[4,8,32,128]{3,2,1,0:T(8,128)(2,1)S(1)}, bf16[2,8,32,128]{3,2,1,0:T(8,128)(2,1)S(1)}, bf16[2,8,32,128]{3,2,1,0:T(8,128)(2,1)S(1)}) custom-call(s32[10]{0:T(128)S(1)} %get-tuple-element.37.params, bf16[512,1024]{1,0:T(8,128)(2,1)S(1)} %copy-done, bf16[2,256,128]{2,1,0:T(8,128)(2,1)S(1)} %collective-permute-done.4.mine, ...), custom_call_target="tpu_custom_call" | custom-call | flops 3200000000 | bytes 1048576 | tf_op jit(solution)/shard_map/both/pallas_call | solution.py:373
  41.9 1.2 %collective-permute-start.8 = (bf16[4,8,32,128]{3,2,1,0:T(8,128)(2,1)S(1)}, bf16[4,8,32,128]{3,2,1,0:T(8,128)(2,1)S(1)}, u32[]{:S(2)}, u32[]{:S(2)}) collective-permute-start(bf16[4,8,32,128]{3,2,1,0:T(8,128)(2,1)S(1)} %get-tuple-element.53), channel_id=1, source_target_pairs={{0,1},{1,0},{2,3},{3,2},{4,5},{5,4},{6,7},{7,6},{8,9},{9,8},{10,11... | collective-permute-start | bytes 786440 | tf_op jit(solution)/shard_map/ppermute | solution.py:392
  43.1 3.3 %collective-permute-start.12 = (bf16[2,8,32,128]{3,2,1,0:T(8,128)(2,1)S(1)}, bf16[2,8,32,128]{3,2,1,0:T(8,128)(2,1)S(1)}, u32[]{:S(2)}, u32[]{:S(2)}) collective-permute-start(bf16[2,8,32,128]{3,2,1,0:T(8,128)(2,1)S(1)} %get-tuple-element.60), channel_id=1, source_target_pairs={{0,3},{1,2},{2,1},{3,0},{4,7},{5,6},{6,5},{7,4},{8,11},{9,10},{10,... | collective-permute-start | bytes 393224 | tf_op jit(solution)/shard_map/ppermute | solution.py:392
  46.4 0.0 collective-permute-done.10.refs_2_
  46.4 0.0 collective-permute-done.9.refs_1_
  46.4 0.0 collective-permute-start.11
  46.4 10.0 %collective-permute-done.12.refs_5_ = bf16[2,8,32,128]{3,2,1,0:T(8,128)(2,1)S(1)} collective-permute-done((bf16[2,8,32,128]{3,2,1,0:T(8,128)(2,1)S(1)}, bf16[2,8,32,128]{3,2,1,0:T(8,128)(2,1)S(1)}, u32[]{:S(2)}, u32[]{:S(2)}) %collective-permute-start.12) | collective-permute-done | bytes 131104 | tf_op jit(solution)/shard_map/ppermute | solution.py:392
  56.4 0.4 collective-permute-done.8.near_ref
  56.7 0.0 collective-permute-done.11.refs_4_
  56.7 1.6 %assemble.1 = f32[4,16,32,128]{3,2,1,0:T(8,128)} custom-call(s32[10]{0:T(128)S(1)} %get-tuple-element.37.params, bf16[4,8,32,128]{3,2,1,0:T(8,128)(2,1)S(1)} %collective-permute-done.8.near_ref, f32[2,8,32,128]{3,2,1,0:T(8,128)S(1)} %get-tuple-element.54.refs_0_, bf16[2,8,32,128]{3,2,1,0:T(8,128)(2,1)S(1)} %collective-permute-done.9.refs_1_, ...), custom_call_target="tpu_custom_call" | custom-call | tf_op jit(solution)/shard_map/assemble/pallas_call | solution.py:461
  (2 shorter events, 0.1 us)
Async XLA Ops:
  0.0 13.2 %copy-start.3 = (bf16[512,256]{1,0:T(8,128)(2,1)S(1)}, bf16[512,256]{1,0:T(8,128)(2,1)}, u32[]{:S(2)}) copy-start(bf16[512,256]{1,0:T(8,128)(2,1)} %constant.17.clone.table_ref.stab) | copy-start | bytes 786436
  0.1 13.8 %copy-start.1 = (f32[2,4,256,128]{3,2,1,0:T(8,128)S(1)}, f32[2,4,256,128]{3,2,1,0:T(8,128)}, u32[]{:S(2)}) copy-start(f32[2,4,256,128]{3,2,1,0:T(8,128)} %constant.20.clone.dop_ref) | copy-start | bytes 3145732
  0.1 13.8 %copy-start.2 = (f32[2,4,192,128]{3,2,1,0:T(8,128)S(1)}, f32[2,4,192,128]{3,2,1,0:T(8,128)}, u32[]{:S(2)}) copy-start(f32[2,4,192,128]{3,2,1,0:T(8,128)} %constant.19.clone.lag_ref) | copy-start | bytes 2359300
  6.4 14.2 %copy-start = (bf16[512,1024]{1,0:T(8,128)(2,1)S(1)}, bf16[512,1024]{1,0:T(8,128)(2,1)}, u32[]{:S(2)}) copy-start(bf16[512,1024]{1,0:T(8,128)(2,1)} %constant.18.clone.rtab) | copy-start | bytes 3145732
  6.4 3.2 %collective-permute-start = (bf16[2,256,128]{2,1,0:T(8,128)(2,1)S(1)}, bf16[2,256,128]{2,1,0:T(8,128)(2,1)S(1)}, u32[]{:S(2)}, u32[]{:S(2)}) collective-permute-start(bf16[2,256,128]{2,1,0:T(8,128)(2,1)S(1)} %get-tuple-element.34), channel_id=1, source_target_pairs={{0,4},{4,0},{8,12},{12,8},{16,20},{20,16},{24,28},{28,24},{1,5},{5... | collective-permute-start | bytes 393224 | tf_op jit(solution)/shard_map/ppermute | solution.py:392
  6.9 18.7 %collective-permute-start.7 = (bf16[8,256,128]{2,1,0:T(8,128)(2,1)S(1)}, bf16[8,256,128]{2,1,0:T(8,128)(2,1)S(1)}, u32[]{:S(2)}, u32[]{:S(2)}) collective-permute-start(bf16[8,256,128]{2,1,0:T(8,128)(2,1)S(1)} %get-tuple-element.48), channel_id=1, source_target_pairs={{0,1},{1,0},{2,3},{3,2},{4,5},{5,4},{6,7},{7,6},{8,9},{9,8},{10,11... | collective-permute-start | bytes 1572872 | tf_op jit(solution)/shard_map/ppermute | solution.py:392
  9.6 6.0 %collective-permute-start.1 = (bf16[2,256,128]{2,1,0:T(8,128)(2,1)S(1)}, bf16[2,256,128]{2,1,0:T(8,128)(2,1)S(1)}, u32[]{:S(2)}, u32[]{:S(2)}) collective-permute-start(bf16[2,256,128]{2,1,0:T(8,128)(2,1)S(1)} %add.12), channel_id=1, source_target_pairs={{0,8},{4,12},{8,0},{12,4},{16,24},{20,28},{24,16},{28,20},{1,9},{5... | collective-permute-start | bytes 393224 | tf_op jit(solution)/shard_map/ppermute | solution.py:392
  11.1 8.1 %collective-permute-start.2 = (bf16[2,256,128]{2,1,0:T(8,128)(2,1)S(1)}, bf16[2,256,128]{2,1,0:T(8,128)(2,1)S(1)}, u32[]{:S(2)}, u32[]{:S(2)}) collective-permute-start(bf16[2,256,128]{2,1,0:T(8,128)(2,1)S(1)} %add.12), channel_id=1, source_target_pairs={{0,16},{4,20},{8,24},{12,28},{16,0},{20,4},{24,8},{28,12},{1,17},{... | collective-permute-start | bytes 393224 | tf_op jit(solution)/shard_map/ppermute | solution.py:392
  12.7 6.6 %collective-permute-start.3 = (bf16[2,256,128]{2,1,0:T(8,128)(2,1)S(1)}, bf16[2,256,128]{2,1,0:T(8,128)(2,1)S(1)}, u32[]{:S(2)}, u32[]{:S(2)}) collective-permute-start(bf16[2,256,128]{2,1,0:T(8,128)(2,1)S(1)} %add.12), channel_id=1, source_target_pairs={{0,24},{4,28},{8,16},{12,20},{16,8},{20,12},{24,0},{28,4},{1,25},{... | collective-permute-start | bytes 393224 | tf_op jit(solution)/shard_map/ppermute | solution.py:392
  19.3 6.3 %collective-permute-start.6 = (bf16[2,256,128]{2,1,0:T(8,128)(2,1)S(1)}, bf16[2,256,128]{2,1,0:T(8,128)(2,1)S(1)}, u32[]{:S(2)}, u32[]{:S(2)}) collective-permute-start(bf16[2,256,128]{2,1,0:T(8,128)(2,1)S(1)} %add_add_fusion.mine), channel_id=1, source_target_pairs={{0,1},{1,0},{2,3},{3,2},{4,5},{5,4},{6,7},{7,6},{8,9},{9,8},{10,11... | collective-permute-start | bytes 393224 | tf_op jit(solution)/shard_map/ppermute | solution.py:392
  20.6 4.1 %collective-permute-start.4 = (bf16[2,256,128]{2,1,0:T(8,128)(2,1)S(1)}, bf16[2,256,128]{2,1,0:T(8,128)(2,1)S(1)}, u32[]{:S(2)}, u32[]{:S(2)}) collective-permute-start(bf16[2,256,128]{2,1,0:T(8,128)(2,1)S(1)} %add_add_fusion.mine), channel_id=1, source_target_pairs={{0,4},{4,0},{8,12},{12,8},{16,20},{20,16},{24,28},{28,24},{1,5},{5... | collective-permute-start | bytes 393224 | tf_op jit(solution)/shard_map/ppermute | solution.py:392
  24.7 9.2 %collective-permute-start.5 = (bf16[2,256,128]{2,1,0:T(8,128)(2,1)S(1)}, bf16[2,256,128]{2,1,0:T(8,128)(2,1)S(1)}, u32[]{:S(2)}, u32[]{:S(2)}) collective-permute-start(bf16[2,256,128]{2,1,0:T(8,128)(2,1)S(1)} %collective-permute-done.4.mine), channel_id=1, source_target_pairs={{0,1},{1,0},{2,3},{3,2},{4,5},{5,4},{6,7},{7,6},{8,9},{9,8},{10,11... | collective-permute-start | bytes 393224 | tf_op jit(solution)/shard_map/ppermute | solution.py:392
  30.5 15.8 %collective-permute-start.10 = (bf16[2,8,32,128]{3,2,1,0:T(8,128)(2,1)S(1)}, bf16[2,8,32,128]{3,2,1,0:T(8,128)(2,1)S(1)}, u32[]{:S(2)}, u32[]{:S(2)}) collective-permute-start(bf16[2,8,32,128]{3,2,1,0:T(8,128)(2,1)S(1)} %get-tuple-element.56), channel_id=1, source_target_pairs={{0,3},{1,2},{2,1},{3,0},{4,7},{5,6},{6,5},{7,4},{8,11},{9,10},{10,... | collective-permute-start | bytes 393224 | tf_op jit(solution)/shard_map/ppermute | solution.py:392
  33.9 12.5 %collective-permute-start.9 = (bf16[2,8,32,128]{3,2,1,0:T(8,128)(2,1)S(1)}, bf16[2,8,32,128]{3,2,1,0:T(8,128)(2,1)S(1)}, u32[]{:S(2)}, u32[]{:S(2)}) collective-permute-start(bf16[2,8,32,128]{3,2,1,0:T(8,128)(2,1)S(1)} %get-tuple-element.55), channel_id=1, source_target_pairs={{0,2},{1,3},{2,0},{3,1},{4,6},{5,7},{6,4},{7,5},{8,10},{9,11},{10,... | collective-permute-start | bytes 393224 | tf_op jit(solution)/shard_map/ppermute | solution.py:392
  41.9 14.8 %collective-permute-start.8 = (bf16[4,8,32,128]{3,2,1,0:T(8,128)(2,1)S(1)}, bf16[4,8,32,128]{3,2,1,0:T(8,128)(2,1)S(1)}, u32[]{:S(2)}, u32[]{:S(2)}) collective-permute-start(bf16[4,8,32,128]{3,2,1,0:T(8,128)(2,1)S(1)} %get-tuple-element.53), channel_id=1, source_target_pairs={{0,1},{1,0},{2,3},{3,2},{4,5},{5,4},{6,7},{7,6},{8,9},{9,8},{10,11... | collective-permute-start | bytes 786440 | tf_op jit(solution)/shard_map/ppermute | solution.py:392
  43.1 13.3 %collective-permute-start.12 = (bf16[2,8,32,128]{3,2,1,0:T(8,128)(2,1)S(1)}, bf16[2,8,32,128]{3,2,1,0:T(8,128)(2,1)S(1)}, u32[]{:S(2)}, u32[]{:S(2)}) collective-permute-start(bf16[2,8,32,128]{3,2,1,0:T(8,128)(2,1)S(1)} %get-tuple-element.60), channel_id=1, source_target_pairs={{0,3},{1,2},{2,1},{3,0},{4,7},{5,6},{6,5},{7,4},{8,11},{9,10},{10,... | collective-permute-start | bytes 393224 | tf_op jit(solution)/shard_map/ppermute | solution.py:392
  46.4 10.4 %collective-permute-start.11 = (bf16[2,8,32,128]{3,2,1,0:T(8,128)(2,1)S(1)}, bf16[2,8,32,128]{3,2,1,0:T(8,128)(2,1)S(1)}, u32[]{:S(2)}, u32[]{:S(2)}) collective-permute-start(bf16[2,8,32,128]{3,2,1,0:T(8,128)(2,1)S(1)} %get-tuple-element.59), channel_id=1, source_target_pairs={{0,2},{1,3},{2,0},{3,1},{4,6},{5,7},{6,4},{7,5},{8,10},{9,11},{10,... | collective-permute-start | bytes 393224 | tf_op jit(solution)/shard_map/ppermute | solution.py:392

commit v7 on v6

--- a/solution.py
+++ b/solution.py
@@ -192,8 +192,8 @@
             pltpu.VMEM((2, 1, TAPS), jnp.bfloat16),
             pltpu.SMEM((3, TX), jnp.int32),
             pltpu.VMEM((2 * REACH, 2 * PAIR), jnp.bfloat16),
-            pltpu.VMEM((blocks * beams, PAIR), jnp.float32),
-            pltpu.VMEM((blocks * beams, PAIR), jnp.float32),
+            pltpu.VMEM((blocks * beams + beams, PAIR), jnp.float32),
+            pltpu.VMEM((blocks * beams + beams, PAIR), jnp.float32),
             pltpu.SemaphoreType.DMA((chunks,)),
             pltpu.SemaphoreType.DMA((5,)),
         ],

time: 58.6 us -> 58.6 us (level)
  no operation moved by 1% of the time
where the time goes in v7:
time: 58.6 us; the launch traced here: 58.5 us
  Pallas kernels  26.6 us (45%)
  starting transfers between devices  16.7 us (28%)
  waiting for transfers between devices  14.7 us (25%)
    pallas_call x3, Pallas kernels, call_powers(): pl.pallas_call(kernel, in_specs=[SMEM if a.ndim == 1 else VMEM for a in a...  17.1 us
    ppermute x13, starting transfers between devices, swap(): return lax.ppermute(value, axis, [(i, i ^ flip) for i in range(size)])  16.7 us
    ppermute x13, waiting for transfers between devices, swap(): return lax.ppermute(value, axis, [(i, i ^ flip) for i in range(size)])  14.7 us
    pallas_call x1, Pallas kernels, decimate(): pl.pallas_call(functools.partial(decimate_kernel, beams), in_specs=[SMEM]...  6.26 us
    pallas_call x1, Pallas kernels, shards(): pl.pallas_call(functools.partial(assemble_kernel, n_seg), in_specs=[SMEM]...  1.57 us
  transfers between devices with their start and end apart: 13, of which 4 were waited for; matrix products, arithmetic and copies ran while one was open for 0% of the time, Pallas kernels for 32%

profile of v7, /device:TPU:0, one launch (start us, length us, event | category | flops | bytes accessed | tf_op | source)
XLA Modules:
  0.0 58.5 jit_solution(9715404849964772489)
XLA Ops:
  0.0 0.0 copy-start.3
  0.0 0.1 pad_add_fusion.ids
  0.1 0.0 copy-start.1
  0.1 0.0 copy-start.2
  0.1 6.3 %decimate.1 = (bf16[8,256,128]{2,1,0:T(8,128)(2,1)S(1)}, bf16[8,256,128]{2,1,0:T(8,128)(2,1)S(1)}, bf16[2,256,128]{2,1,0:T(8,128)(2,1)S(1)}, bf16[2,256,128]{2,1,0:T(8,128)(2,1)S(1)}, s32[10]{0:T(128)S(1)}) custom-call(s32[2]{0:T(128)S(1)} %pad_add_fusion.ids, s32[4]{0:T(128)} %owner.1, s32[4]{0:T(128)} %delay.1, s32[4]{0:T(128)} %doppler.1, ...), custom_call_target="tpu_custom_call" | custom-call | tf_op jit(solution)/shard_map/decimate/pallas_call | solution.py:183
  6.4 0.0 copy-start
  6.4 0.5 collective-permute-start
  6.9 2.7 %collective-permute-start.7 = (bf16[8,256,128]{2,1,0:T(8,128)(2,1)S(1)}, bf16[8,256,128]{2,1,0:T(8,128)(2,1)S(1)}, u32[]{:S(2)}, u32[]{:S(2)}) collective-permute-start(bf16[8,256,128]{2,1,0:T(8,128)(2,1)S(1)} %get-tuple-element.48), channel_id=1, source_target_pairs={{0,1},{1,0},{2,3},{3,2},{4,5},{5,4},{6,7},{7,6},{8,9},{9,8},{10,11... | collective-permute-start | bytes 1572872 | tf_op jit(solution)/shard_map/ppermute | solution.py:392
  9.5 0.0 collective-permute-done
  9.6 1.6 %collective-permute-start.1 = (bf16[2,256,128]{2,1,0:T(8,128)(2,1)S(1)}, bf16[2,256,128]{2,1,0:T(8,128)(2,1)S(1)}, u32[]{:S(2)}, u32[]{:S(2)}) collective-permute-start(bf16[2,256,128]{2,1,0:T(8,128)(2,1)S(1)} %add.12), channel_id=1, source_target_pairs={{0,8},{4,12},{8,0},{12,4},{16,24},{20,28},{24,16},{28,20},{1,9},{5... | collective-permute-start | bytes 393224 | tf_op jit(solution)/shard_map/ppermute | solution.py:392
  11.1 1.5 %collective-permute-start.2 = (bf16[2,256,128]{2,1,0:T(8,128)(2,1)S(1)}, bf16[2,256,128]{2,1,0:T(8,128)(2,1)S(1)}, u32[]{:S(2)}, u32[]{:S(2)}) collective-permute-start(bf16[2,256,128]{2,1,0:T(8,128)(2,1)S(1)} %add.12), channel_id=1, source_target_pairs={{0,16},{4,20},{8,24},{12,28},{16,0},{20,4},{24,8},{28,12},{1,17},{... | collective-permute-start | bytes 393224 | tf_op jit(solution)/shard_map/ppermute | solution.py:392
  12.7 0.5 collective-permute-start.3
  13.1 0.0 copy-done.3
  13.1 0.7 %own_spectra.1.spec = f32[8,512,256]{2,1,0:T(8,128)S(1)} custom-call(bf16[512,256]{1,0:T(8,128)(2,1)S(1)} %copy-done.3, bf16[8,256,128]{2,1,0:T(8,128)(2,1)S(1)} %get-tuple-element.41.s_ref), custom_call_target="tpu_custom_call" | custom-call | tf_op jit(solution)/shard_map/own_spectra/pallas_call | solution.py:265
  13.9 0.0 copy-done.1
  13.9 0.0 copy-done.2
  13.9 1.0 %tables.1 = (bf16[4,256,512]{2,1,0:T(8,128)(2,1)S(1)}, bf16[4,512,256]{2,1,0:T(8,128)(2,1)S(1)}) custom-call(s32[10]{0:T(128)S(1)} %get-tuple-element.37.params, f32[2,4,192,128]{3,2,1,0:T(8,128)S(1)} %copy-done.2, f32[2,4,256,128]{3,2,1,0:T(8,128)S(1)} %copy-done.1), custom_call_target="tpu_custom_call" | custom-call | tf_op jit(solution)/shard_map/tables/pallas_call | solution.py:222
  14.9 0.7 %collective-permute-done.1 = bf16[2,256,128]{2,1,0:T(8,128)(2,1)S(1)} collective-permute-done((bf16[2,256,128]{2,1,0:T(8,128)(2,1)S(1)}, bf16[2,256,128]{2,1,0:T(8,128)(2,1)S(1)}, u32[]{:S(2)}, u32[]{:S(2)}) %collective-permute-start.1) | collective-permute-done | bytes 131104 | tf_op jit(solution)/shard_map/ppermute | solution.py:392
  15.6 3.7 %collective-permute-done.2 = bf16[2,256,128]{2,1,0:T(8,128)(2,1)S(1)} collective-permute-done((bf16[2,256,128]{2,1,0:T(8,128)(2,1)S(1)}, bf16[2,256,128]{2,1,0:T(8,128)(2,1)S(1)}, u32[]{:S(2)}, u32[]{:S(2)}) %collective-permute-start.2) | collective-permute-done | bytes 131104 | tf_op jit(solution)/shard_map/ppermute | solution.py:392
  19.2 0.0 collective-permute-done.3
  19.3 1.3 %collective-permute-start.6 = (bf16[2,256,128]{2,1,0:T(8,128)(2,1)S(1)}, bf16[2,256,128]{2,1,0:T(8,128)(2,1)S(1)}, u32[]{:S(2)}, u32[]{:S(2)}) collective-permute-start(bf16[2,256,128]{2,1,0:T(8,128)(2,1)S(1)} %add_add_fusion.mine), channel_id=1, source_target_pairs={{0,1},{1,0},{2,3},{3,2},{4,5},{5,4},{6,7},{7,6},{8,9},{9,8},{10,11... | collective-permute-start | bytes 393224 | tf_op jit(solution)/shard_map/ppermute | solution.py:392
  20.6 0.0 collective-permute-start.4
  20.6 0.0 copy-done
  20.6 4.1 %own_part.1.part_ref = f32[2,8,128,128]{3,2,1,0:T(8,128)S(1)} custom-call(s32[10]{0:T(128)S(1)} %get-tuple-element.37.params, bf16[512,1024]{1,0:T(8,128)(2,1)S(1)} %copy-done, bf16[2,256,128]{2,1,0:T(8,128)(2,1)S(1)} %add_add_fusion.mine, f32[8,512,256]{2,1,0:T(8,128)S(1)} %own_spectra.1.spec, bf16[4,256,512]{2,1,0:T(8,128)(2,1)S(1)} %get-tuple-element.46.lags, ...), custom_call_target="tpu_custom_call" | custom-call | flops 1600000000 | bytes 1048576 | tf_op jit(solution)/shard_map/own_part/pallas_call | solution.py:373
  24.7 0.0 collective-permute-done.4.mine
  24.7 0.8 %collective-permute-start.5 = (bf16[2,256,128]{2,1,0:T(8,128)(2,1)S(1)}, bf16[2,256,128]{2,1,0:T(8,128)(2,1)S(1)}, u32[]{:S(2)}, u32[]{:S(2)}) collective-permute-start(bf16[2,256,128]{2,1,0:T(8,128)(2,1)S(1)} %collective-permute-done.4.mine), channel_id=1, source_target_pairs={{0,1},{1,0},{2,3},{3,2},{4,5},{5,4},{6,7},{7,6},{8,9},{9,8},{10,11... | collective-permute-start | bytes 393224 | tf_op jit(solution)/shard_map/ppermute | solution.py:392
  25.6 0.0 collective-permute-done.7.there
  25.6 0.0 collective-permute-done.6.far
  25.6 5.0 %far_part.1 = (f32[8,512,256]{2,1,0:T(8,128)S(1)}, f32[2,8,32,128]{3,2,1,0:T(8,128)S(1)}, bf16[2,8,32,128]{3,2,1,0:T(8,128)(2,1)S(1)}, bf16[2,8,32,128]{3,2,1,0:T(8,128)(2,1)S(1)}, bf16[2,8,32,128]{3,2,1,0:T(8,128)(2,1)S(1)}) custom-call(s32[10]{0:T(128)S(1)} %get-tuple-element.37.params, bf16[512,1024]{1,0:T(8,128)(2,1)S(1)} %copy-done, ...), custom_call_target="tpu_custom_call" | custom-call | flops 1600000000 | bytes 1048576 | tf_op jit(solution)/shard_map/far_part/pallas_call | solution.py:373
  30.5 3.3 %collective-permute-start.10 = (bf16[2,8,32,128]{3,2,1,0:T(8,128)(2,1)S(1)}, bf16[2,8,32,128]{3,2,1,0:T(8,128)(2,1)S(1)}, u32[]{:S(2)}, u32[]{:S(2)}) collective-permute-start(bf16[2,8,32,128]{3,2,1,0:T(8,128)(2,1)S(1)} %get-tuple-element.56), channel_id=1, source_target_pairs={{0,3},{1,2},{2,1},{3,0},{4,7},{5,6},{6,5},{7,4},{8,11},{9,10},{10,... | collective-permute-start | bytes 393224 | tf_op jit(solution)/shard_map/ppermute | solution.py:392
  33.9 0.0 collective-permute-start.9
  33.9 0.0 collective-permute-done.5.far
  33.9 8.0 %both.1 = (f32[2,8,32,128]{3,2,1,0:T(8,128)S(1)}, bf16[4,8,32,128]{3,2,1,0:T(8,128)(2,1)S(1)}, bf16[2,8,32,128]{3,2,1,0:T(8,128)(2,1)S(1)}, bf16[2,8,32,128]{3,2,1,0:T(8,128)(2,1)S(1)}) custom-call(s32[10]{0:T(128)S(1)} %get-tuple-element.37.params, bf16[512,1024]{1,0:T(8,128)(2,1)S(1)} %copy-done, bf16[2,256,128]{2,1,0:T(8,128)(2,1)S(1)} %collective-permute-done.4.mine, ...), custom_call_target="tpu_custom_call" | custom-call | flops 3200000000 | bytes 1048576 | tf_op jit(solution)/shard_map/both/pallas_call | solution.py:373
  41.9 1.2 %collective-permute-start.8 = (bf16[4,8,32,128]{3,2,1,0:T(8,128)(2,1)S(1)}, bf16[4,8,32,128]{3,2,1,0:T(8,128)(2,1)S(1)}, u32[]{:S(2)}, u32[]{:S(2)}) collective-permute-start(bf16[4,8,32,128]{3,2,1,0:T(8,128)(2,1)S(1)} %get-tuple-element.53), channel_id=1, source_target_pairs={{0,1},{1,0},{2,3},{3,2},{4,5},{5,4},{6,7},{7,6},{8,9},{9,8},{10,11... | collective-permute-start | bytes 786440 | tf_op jit(solution)/shard_map/ppermute | solution.py:392
  43.1 3.3 %collective-permute-start.12 = (bf16[2,8,32,128]{3,2,1,0:T(8,128)(2,1)S(1)}, bf16[2,8,32,128]{3,2,1,0:T(8,128)(2,1)S(1)}, u32[]{:S(2)}, u32[]{:S(2)}) collective-permute-start(bf16[2,8,32,128]{3,2,1,0:T(8,128)(2,1)S(1)} %get-tuple-element.60), channel_id=1, source_target_pairs={{0,3},{1,2},{2,1},{3,0},{4,7},{5,6},{6,5},{7,4},{8,11},{9,10},{10,... | collective-permute-start | bytes 393224 | tf_op jit(solution)/shard_map/ppermute | solution.py:392
  46.3 0.0 collective-permute-done.10.refs_2_
  46.3 0.0 collective-permute-done.9.refs_1_
  46.4 0.0 collective-permute-start.11
  46.4 10.0 %collective-permute-done.12.refs_5_ = bf16[2,8,32,128]{3,2,1,0:T(8,128)(2,1)S(1)} collective-permute-done((bf16[2,8,32,128]{3,2,1,0:T(8,128)(2,1)S(1)}, bf16[2,8,32,128]{3,2,1,0:T(8,128)(2,1)S(1)}, u32[]{:S(2)}, u32[]{:S(2)}) %collective-permute-start.12) | collective-permute-done | bytes 131104 | tf_op jit(solution)/shard_map/ppermute | solution.py:392
  56.4 0.4 collective-permute-done.8.near_ref
  56.7 0.0 collective-permute-done.11.refs_4_
  56.7 1.6 %assemble.1 = f32[4,16,32,128]{3,2,1,0:T(8,128)} custom-call(s32[10]{0:T(128)S(1)} %get-tuple-element.37.params, bf16[4,8,32,128]{3,2,1,0:T(8,128)(2,1)S(1)} %collective-permute-done.8.near_ref, f32[2,8,32,128]{3,2,1,0:T(8,128)S(1)} %get-tuple-element.54.refs_0_, bf16[2,8,32,128]{3,2,1,0:T(8,128)(2,1)S(1)} %collective-permute-done.9.refs_1_, ...), custom_call_target="tpu_custom_call" | custom-call | tf_op jit(solution)/shard_map/assemble/pallas_call | solution.py:461
  (2 shorter events, 0.1 us)
Async XLA Ops:
  0.0 13.1 %copy-start.3 = (bf16[512,256]{1,0:T(8,128)(2,1)S(1)}, bf16[512,256]{1,0:T(8,128)(2,1)}, u32[]{:S(2)}) copy-start(bf16[512,256]{1,0:T(8,128)(2,1)} %constant.17.clone.table_ref.stab) | copy-start | bytes 786436
  0.1 13.8 %copy-start.1 = (f32[2,4,256,128]{3,2,1,0:T(8,128)S(1)}, f32[2,4,256,128]{3,2,1,0:T(8,128)}, u32[]{:S(2)}) copy-start(f32[2,4,256,128]{3,2,1,0:T(8,128)} %constant.20.clone.dop_ref) | copy-start | bytes 3145732
  0.1 13.8 %copy-start.2 = (f32[2,4,192,128]{3,2,1,0:T(8,128)S(1)}, f32[2,4,192,128]{3,2,1,0:T(8,128)}, u32[]{:S(2)}) copy-start(f32[2,4,192,128]{3,2,1,0:T(8,128)} %constant.19.clone.lag_ref) | copy-start | bytes 2359300
  6.4 14.2 %copy-start = (bf16[512,1024]{1,0:T(8,128)(2,1)S(1)}, bf16[512,1024]{1,0:T(8,128)(2,1)}, u32[]{:S(2)}) copy-start(bf16[512,1024]{1,0:T(8,128)(2,1)} %constant.18.clone.rtab) | copy-start | bytes 3145732
  6.4 3.2 %collective-permute-start = (bf16[2,256,128]{2,1,0:T(8,128)(2,1)S(1)}, bf16[2,256,128]{2,1,0:T(8,128)(2,1)S(1)}, u32[]{:S(2)}, u32[]{:S(2)}) collective-permute-start(bf16[2,256,128]{2,1,0:T(8,128)(2,1)S(1)} %get-tuple-element.34), channel_id=1, source_target_pairs={{0,4},{4,0},{8,12},{12,8},{16,20},{20,16},{24,28},{28,24},{1,5},{5... | collective-permute-start | bytes 393224 | tf_op jit(solution)/shard_map/ppermute | solution.py:392
  6.9 18.7 %collective-permute-start.7 = (bf16[8,256,128]{2,1,0:T(8,128)(2,1)S(1)}, bf16[8,256,128]{2,1,0:T(8,128)(2,1)S(1)}, u32[]{:S(2)}, u32[]{:S(2)}) collective-permute-start(bf16[8,256,128]{2,1,0:T(8,128)(2,1)S(1)} %get-tuple-element.48), channel_id=1, source_target_pairs={{0,1},{1,0},{2,3},{3,2},{4,5},{5,4},{6,7},{7,6},{8,9},{9,8},{10,11... | collective-permute-start | bytes 1572872 | tf_op jit(solution)/shard_map/ppermute | solution.py:392
  9.6 6.0 %collective-permute-start.1 = (bf16[2,256,128]{2,1,0:T(8,128)(2,1)S(1)}, bf16[2,256,128]{2,1,0:T(8,128)(2,1)S(1)}, u32[]{:S(2)}, u32[]{:S(2)}) collective-permute-start(bf16[2,256,128]{2,1,0:T(8,128)(2,1)S(1)} %add.12), channel_id=1, source_target_pairs={{0,8},{4,12},{8,0},{12,4},{16,24},{20,28},{24,16},{28,20},{1,9},{5... | collective-permute-start | bytes 393224 | tf_op jit(solution)/shard_map/ppermute | solution.py:392
  11.1 8.1 %collective-permute-start.2 = (bf16[2,256,128]{2,1,0:T(8,128)(2,1)S(1)}, bf16[2,256,128]{2,1,0:T(8,128)(2,1)S(1)}, u32[]{:S(2)}, u32[]{:S(2)}) collective-permute-start(bf16[2,256,128]{2,1,0:T(8,128)(2,1)S(1)} %add.12), channel_id=1, source_target_pairs={{0,16},{4,20},{8,24},{12,28},{16,0},{20,4},{24,8},{28,12},{1,17},{... | collective-permute-start | bytes 393224 | tf_op jit(solution)/shard_map/ppermute | solution.py:392
  12.7 6.6 %collective-permute-start.3 = (bf16[2,256,128]{2,1,0:T(8,128)(2,1)S(1)}, bf16[2,256,128]{2,1,0:T(8,128)(2,1)S(1)}, u32[]{:S(2)}, u32[]{:S(2)}) collective-permute-start(bf16[2,256,128]{2,1,0:T(8,128)(2,1)S(1)} %add.12), channel_id=1, source_target_pairs={{0,24},{4,28},{8,16},{12,20},{16,8},{20,12},{24,0},{28,4},{1,25},{... | collective-permute-start | bytes 393224 | tf_op jit(solution)/shard_map/ppermute | solution.py:392
  19.3 6.3 %collective-permute-start.6 = (bf16[2,256,128]{2,1,0:T(8,128)(2,1)S(1)}, bf16[2,256,128]{2,1,0:T(8,128)(2,1)S(1)}, u32[]{:S(2)}, u32[]{:S(2)}) collective-permute-start(bf16[2,256,128]{2,1,0:T(8,128)(2,1)S(1)} %add_add_fusion.mine), channel_id=1, source_target_pairs={{0,1},{1,0},{2,3},{3,2},{4,5},{5,4},{6,7},{7,6},{8,9},{9,8},{10,11... | collective-permute-start | bytes 393224 | tf_op jit(solution)/shard_map/ppermute | solution.py:392
  20.6 4.1 %collective-permute-start.4 = (bf16[2,256,128]{2,1,0:T(8,128)(2,1)S(1)}, bf16[2,256,128]{2,1,0:T(8,128)(2,1)S(1)}, u32[]{:S(2)}, u32[]{:S(2)}) collective-permute-start(bf16[2,256,128]{2,1,0:T(8,128)(2,1)S(1)} %add_add_fusion.mine), channel_id=1, source_target_pairs={{0,4},{4,0},{8,12},{12,8},{16,20},{20,16},{24,28},{28,24},{1,5},{5... | collective-permute-start | bytes 393224 | tf_op jit(solution)/shard_map/ppermute | solution.py:392
  24.7 9.2 %collective-permute-start.5 = (bf16[2,256,128]{2,1,0:T(8,128)(2,1)S(1)}, bf16[2,256,128]{2,1,0:T(8,128)(2,1)S(1)}, u32[]{:S(2)}, u32[]{:S(2)}) collective-permute-start(bf16[2,256,128]{2,1,0:T(8,128)(2,1)S(1)} %collective-permute-done.4.mine), channel_id=1, source_target_pairs={{0,1},{1,0},{2,3},{3,2},{4,5},{5,4},{6,7},{7,6},{8,9},{9,8},{10,11... | collective-permute-start | bytes 393224 | tf_op jit(solution)/shard_map/ppermute | solution.py:392
  30.5 15.8 %collective-permute-start.10 = (bf16[2,8,32,128]{3,2,1,0:T(8,128)(2,1)S(1)}, bf16[2,8,32,128]{3,2,1,0:T(8,128)(2,1)S(1)}, u32[]{:S(2)}, u32[]{:S(2)}) collective-permute-start(bf16[2,8,32,128]{3,2,1,0:T(8,128)(2,1)S(1)} %get-tuple-element.56), channel_id=1, source_target_pairs={{0,3},{1,2},{2,1},{3,0},{4,7},{5,6},{6,5},{7,4},{8,11},{9,10},{10,... | collective-permute-start | bytes 393224 | tf_op jit(solution)/shard_map/ppermute | solution.py:392
  33.9 12.5 %collective-permute-start.9 = (bf16[2,8,32,128]{3,2,1,0:T(8,128)(2,1)S(1)}, bf16[2,8,32,128]{3,2,1,0:T(8,128)(2,1)S(1)}, u32[]{:S(2)}, u32[]{:S(2)}) collective-permute-start(bf16[2,8,32,128]{3,2,1,0:T(8,128)(2,1)S(1)} %get-tuple-element.55), channel_id=1, source_target_pairs={{0,2},{1,3},{2,0},{3,1},{4,6},{5,7},{6,4},{7,5},{8,10},{9,11},{10,... | collective-permute-start | bytes 393224 | tf_op jit(solution)/shard_map/ppermute | solution.py:392
  41.9 14.8 %collective-permute-start.8 = (bf16[4,8,32,128]{3,2,1,0:T(8,128)(2,1)S(1)}, bf16[4,8,32,128]{3,2,1,0:T(8,128)(2,1)S(1)}, u32[]{:S(2)}, u32[]{:S(2)}) collective-permute-start(bf16[4,8,32,128]{3,2,1,0:T(8,128)(2,1)S(1)} %get-tuple-element.53), channel_id=1, source_target_pairs={{0,1},{1,0},{2,3},{3,2},{4,5},{5,4},{6,7},{7,6},{8,9},{9,8},{10,11... | collective-permute-start | bytes 786440 | tf_op jit(solution)/shard_map/ppermute | solution.py:392
  43.1 13.3 %collective-permute-start.12 = (bf16[2,8,32,128]{3,2,1,0:T(8,128)(2,1)S(1)}, bf16[2,8,32,128]{3,2,1,0:T(8,128)(2,1)S(1)}, u32[]{:S(2)}, u32[]{:S(2)}) collective-permute-start(bf16[2,8,32,128]{3,2,1,0:T(8,128)(2,1)S(1)} %get-tuple-element.60), channel_id=1, source_target_pairs={{0,3},{1,2},{2,1},{3,0},{4,7},{5,6},{6,5},{7,4},{8,11},{9,10},{10,... | collective-permute-start | bytes 393224 | tf_op jit(solution)/shard_map/ppermute | solution.py:392
  46.4 10.4 %collective-permute-start.11 = (bf16[2,8,32,128]{3,2,1,0:T(8,128)(2,1)S(1)}, bf16[2,8,32,128]{3,2,1,0:T(8,128)(2,1)S(1)}, u32[]{:S(2)}, u32[]{:S(2)}) collective-permute-start(bf16[2,8,32,128]{3,2,1,0:T(8,128)(2,1)S(1)} %get-tuple-element.59), channel_id=1, source_target_pairs={{0,2},{1,3},{2,0},{3,1},{4,6},{5,7},{6,4},{7,5},{8,10},{9,11},{10,... | collective-permute-start | bytes 393224 | tf_op jit(solution)/shard_map/ppermute | solution.py:392

commit v8 on v7

--- a/solution.py
+++ b/solution.py
@@ -240,16 +240,19 @@
     return (core if group == 0 else 1 - core) * HALF_TX
 
 
-def write_ref_spectra(params, first, table_ref, ref, out_ref, padded):
+def ref_spectra_writer(params, first, table_ref, ref, out_ref, padded):
     padded[:PAD] = jnp.zeros((PAD, PAIR), jnp.float32)
     padded[PAD + BLOCKS :] = jnp.zeros((PAD, PAIR), jnp.float32)
-    for k in range(HALF_TX):
+
+    def write(k):
         padded[PAD : PAD + BLOCKS] = ref[k].astype(jnp.float32)
         start = PAD - 1 - (params[first + k] + DELAYS - 1) // BLOCK_LEN
         window = jnp.concatenate(
             [padded[pl.ds(start + e, BLOCKS), :].astype(jnp.bfloat16) for e in range(4)], axis=1
         )
         out_ref[k] = nt_dot(table_ref[...], jnp.concatenate([window, window], axis=1))
+
+    return write
 
 
 def surv_spectrum(table_ref, s):
@@ -272,10 +275,12 @@
     )(table, surv)
 
 
-def sum_powers(segments, first, lag_ref, dop_ref, prods, corrs, emit):
+def sum_powers(writers, segments, first, lag_ref, dop_ref, prods, corrs, emit):
     count = segments[0][0].shape[0]
     rows = count * DELAYS
     for k in range(HALF_TX):
+        for write in writers:
+            write(k)
         corr = corrs.at[k]
         for n, (s_ref, r_ref) in enumerate(segments):
             r_re, r_im = r_ref[k, :FFT], r_ref[k, FFT:]
@@ -314,22 +319,26 @@
 
 def own_part_kernel(params, rtab, mine, spec, lags, dops, part_ref, padded, r_here, prods, corrs):
     first = first_tx(params, 0)
-    write_ref_spectra(params, first, rtab, mine, r_here, padded)
+    write = ref_spectra_writer(params, first, rtab, mine, r_here, padded)
+    for k in range(HALF_TX):
+        write(k)
 
     def emit(k, at, power):
         part_ref[k, at] = power
 
-    sum_powers([(spec, r_here)], first, lags, dops, prods, corrs, emit)
+    sum_powers([], [(spec, r_here)], first, lags, dops, prods, corrs, emit)
 
 
 def far_part_kernel(params, rtab, far, stab, there, part_ref, lags, dops, far_spec, own_ref, *refs):
     send_refs, (padded, r_there, prods, corrs) = refs[:-4], refs[-4:]
     first = first_tx(params, 0)
-    write_ref_spectra(params, first, rtab, far, r_there, padded)
+    write = ref_spectra_writer(params, first, rtab, far, r_there, padded)
+    for k in range(HALF_TX):
+        write(k)
     surv_spectra_kernel(stab, there, far_spec)
     store = emit_chunks(own_ref, send_refs)
     emit = lambda k, at, power: store(k, at, power + part_ref[k, at])
-    sum_powers([(far_spec, r_there)], first, lags, dops, prods, corrs, emit)
+    sum_powers([], [(far_spec, r_there)], first, lags, dops, prods, corrs, emit)
 
 
 def both_kernel(
@@ -337,11 +346,13 @@
 ):
     send_refs, (padded, r_here, r_there, prods, corrs) = refs[:-5], refs[-5:]
     first = first_tx(params, 1)
-    write_ref_spectra(params, first, rtab, mine, r_here, padded)
-    write_ref_spectra(params, first, rtab, far, r_there, padded)
+    writers = [
+        ref_spectra_writer(params, first, rtab, ref, out, padded)
+        for ref, out in ((mine, r_here), (far, r_there))
+    ]
     near_all[:HALF_TX] = near_ref[...]
     emit = emit_chunks(own_ref, (near_all.at[HALF_TX:], *send_refs))
-    sum_powers([(spec, r_here), (far_spec, r_there)], first, lags, dops, prods, corrs, emit)
+    sum_powers(writers, [(spec, r_here), (far_spec, r_there)], first, lags, dops, prods, corrs, emit)
 
 
 def assemble_kernel(n_seg, params, near_ref, *refs):

time: 58.6 us -> 58.6 us (level)
  Pallas kernels: 26.6 us -> 26 us
  waiting for transfers between devices: 14.7 us -> 15.3 us
    pallas_call x3, Pallas kernels: 17.1 us -> 16.4 us  [call_powers(): pl.pallas_call(kernel, in_specs=[SMEM if a.ndim == 1 else VMEM for a in a...]
    ppermute x13, waiting for transfers between devices: 14.7 us -> 15.3 us  [swap(): return lax.ppermute(value, axis, [(i, i ^ flip) for i in range(size)])]
  transfers between devices with their start and end apart: 13 -> 13, of which waited for: 4 -> 5; matrix products, arithmetic and copies ran while one was open for 0% -> 0% of each run, Pallas kernels for 32% -> 31%
where the time goes in v8:
time: 58.6 us; the launch traced here: 58.5 us
  Pallas kernels  26 us (44%)
  starting transfers between devices  16.7 us (28%)
  waiting for transfers between devices  15.3 us (26%)
    ppermute x13, starting transfers between devices, swap(): return lax.ppermute(value, axis, [(i, i ^ flip) for i in range(size)])  16.7 us
    pallas_call x3, Pallas kernels, call_powers(): pl.pallas_call(kernel, in_specs=[SMEM if a.ndim == 1 else VMEM for a in a...  16.4 us
    ppermute x13, waiting for transfers between devices, swap(): return lax.ppermute(value, axis, [(i, i ^ flip) for i in range(size)])  15.3 us
    pallas_call x1, Pallas kernels, decimate(): pl.pallas_call(functools.partial(decimate_kernel, beams), in_specs=[SMEM]...  6.26 us
    pallas_call x1, Pallas kernels, shards(): pl.pallas_call(functools.partial(assemble_kernel, n_seg), in_specs=[SMEM]...  1.57 us
  transfers between devices with their start and end apart: 13, of which 5 were waited for; matrix products, arithmetic and copies ran while one was open for 0% of the time, Pallas kernels for 31%

profile of v8, /device:TPU:0, one launch (start us, length us, event | category | flops | bytes accessed | tf_op | source)
XLA Modules:
  0.0 58.5 jit_solution(1833681070200091947)
XLA Ops:
  0.0 0.0 copy-start.3
  0.0 0.1 pad_add_fusion.ids
  0.1 0.0 copy-start.1
  0.1 0.0 copy-start.2
  0.1 6.3 %decimate.1 = (bf16[8,256,128]{2,1,0:T(8,128)(2,1)S(1)}, bf16[8,256,128]{2,1,0:T(8,128)(2,1)S(1)}, bf16[2,256,128]{2,1,0:T(8,128)(2,1)S(1)}, bf16[2,256,128]{2,1,0:T(8,128)(2,1)S(1)}, s32[10]{0:T(128)S(1)}) custom-call(s32[2]{0:T(128)S(1)} %pad_add_fusion.ids, s32[4]{0:T(128)} %owner.1, s32[4]{0:T(128)} %delay.1, s32[4]{0:T(128)} %doppler.1, ...), custom_call_target="tpu_custom_call" | custom-call | tf_op jit(solution)/shard_map/decimate/pallas_call | solution.py:183
  6.4 0.0 copy-start
  6.4 0.5 collective-permute-start
  6.9 2.7 %collective-permute-start.7 = (bf16[8,256,128]{2,1,0:T(8,128)(2,1)S(1)}, bf16[8,256,128]{2,1,0:T(8,128)(2,1)S(1)}, u32[]{:S(2)}, u32[]{:S(2)}) collective-permute-start(bf16[8,256,128]{2,1,0:T(8,128)(2,1)S(1)} %get-tuple-element.48), channel_id=1, source_target_pairs={{0,1},{1,0},{2,3},{3,2},{4,5},{5,4},{6,7},{7,6},{8,9},{9,8},{10,11... | collective-permute-start | bytes 1572872 | tf_op jit(solution)/shard_map/ppermute | solution.py:403
  9.5 0.0 collective-permute-done
  9.6 1.6 %collective-permute-start.1 = (bf16[2,256,128]{2,1,0:T(8,128)(2,1)S(1)}, bf16[2,256,128]{2,1,0:T(8,128)(2,1)S(1)}, u32[]{:S(2)}, u32[]{:S(2)}) collective-permute-start(bf16[2,256,128]{2,1,0:T(8,128)(2,1)S(1)} %add.12), channel_id=1, source_target_pairs={{0,8},{4,12},{8,0},{12,4},{16,24},{20,28},{24,16},{28,20},{1,9},{5... | collective-permute-start | bytes 393224 | tf_op jit(solution)/shard_map/ppermute | solution.py:403
  11.1 1.5 %collective-permute-start.2 = (bf16[2,256,128]{2,1,0:T(8,128)(2,1)S(1)}, bf16[2,256,128]{2,1,0:T(8,128)(2,1)S(1)}, u32[]{:S(2)}, u32[]{:S(2)}) collective-permute-start(bf16[2,256,128]{2,1,0:T(8,128)(2,1)S(1)} %add.12), channel_id=1, source_target_pairs={{0,16},{4,20},{8,24},{12,28},{16,0},{20,4},{24,8},{28,12},{1,17},{... | collective-permute-start | bytes 393224 | tf_op jit(solution)/shard_map/ppermute | solution.py:403
  12.7 0.5 collective-permute-start.3
  13.1 0.0 copy-done.3
  13.1 0.7 %own_spectra.1.spec = f32[8,512,256]{2,1,0:T(8,128)S(1)} custom-call(bf16[512,256]{1,0:T(8,128)(2,1)S(1)} %copy-done.3, bf16[8,256,128]{2,1,0:T(8,128)(2,1)S(1)} %get-tuple-element.41.s_ref), custom_call_target="tpu_custom_call" | custom-call | tf_op jit(solution)/shard_map/own_spectra/pallas_call | solution.py:268
  13.9 0.0 copy-done.1
  13.9 0.0 copy-done.2
  13.9 1.0 %tables.1 = (bf16[4,256,512]{2,1,0:T(8,128)(2,1)S(1)}, bf16[4,512,256]{2,1,0:T(8,128)(2,1)S(1)}) custom-call(s32[10]{0:T(128)S(1)} %get-tuple-element.37.params, f32[2,4,192,128]{3,2,1,0:T(8,128)S(1)} %copy-done.2, f32[2,4,256,128]{3,2,1,0:T(8,128)S(1)} %copy-done.1), custom_call_target="tpu_custom_call" | custom-call | tf_op jit(solution)/shard_map/tables/pallas_call | solution.py:222
  14.9 0.7 %collective-permute-done.1 = bf16[2,256,128]{2,1,0:T(8,128)(2,1)S(1)} collective-permute-done((bf16[2,256,128]{2,1,0:T(8,128)(2,1)S(1)}, bf16[2,256,128]{2,1,0:T(8,128)(2,1)S(1)}, u32[]{:S(2)}, u32[]{:S(2)}) %collective-permute-start.1) | collective-permute-done | bytes 131104 | tf_op jit(solution)/shard_map/ppermute | solution.py:403
  15.6 3.7 %collective-permute-done.2 = bf16[2,256,128]{2,1,0:T(8,128)(2,1)S(1)} collective-permute-done((bf16[2,256,128]{2,1,0:T(8,128)(2,1)S(1)}, bf16[2,256,128]{2,1,0:T(8,128)(2,1)S(1)}, u32[]{:S(2)}, u32[]{:S(2)}) %collective-permute-start.2) | collective-permute-done | bytes 131104 | tf_op jit(solution)/shard_map/ppermute | solution.py:403
  19.2 0.0 collective-permute-done.3
  19.3 1.3 %collective-permute-start.6 = (bf16[2,256,128]{2,1,0:T(8,128)(2,1)S(1)}, bf16[2,256,128]{2,1,0:T(8,128)(2,1)S(1)}, u32[]{:S(2)}, u32[]{:S(2)}) collective-permute-start(bf16[2,256,128]{2,1,0:T(8,128)(2,1)S(1)} %add_add_fusion.mine), channel_id=1, source_target_pairs={{0,1},{1,0},{2,3},{3,2},{4,5},{5,4},{6,7},{7,6},{8,9},{9,8},{10,11... | collective-permute-start | bytes 393224 | tf_op jit(solution)/shard_map/ppermute | solution.py:403
  20.6 0.0 collective-permute-start.4
  20.6 0.0 copy-done
  20.6 4.1 %own_part.1.part_ref = f32[2,8,128,128]{3,2,1,0:T(8,128)S(1)} custom-call(s32[10]{0:T(128)S(1)} %get-tuple-element.37.params, bf16[512,1024]{1,0:T(8,128)(2,1)S(1)} %copy-done, bf16[2,256,128]{2,1,0:T(8,128)(2,1)S(1)} %add_add_fusion.mine, f32[8,512,256]{2,1,0:T(8,128)S(1)} %own_spectra.1.spec, bf16[4,256,512]{2,1,0:T(8,128)(2,1)S(1)} %get-tuple-element.46.lags, ...), custom_call_target="tpu_custom_call" | custom-call | flops 1600000000 | bytes 1048576 | tf_op jit(solution)/shard_map/own_part/pallas_call | solution.py:384
  24.7 0.0 collective-permute-done.4.mine
  24.7 0.8 %collective-permute-start.5 = (bf16[2,256,128]{2,1,0:T(8,128)(2,1)S(1)}, bf16[2,256,128]{2,1,0:T(8,128)(2,1)S(1)}, u32[]{:S(2)}, u32[]{:S(2)}) collective-permute-start(bf16[2,256,128]{2,1,0:T(8,128)(2,1)S(1)} %collective-permute-done.4.mine), channel_id=1, source_target_pairs={{0,1},{1,0},{2,3},{3,2},{4,5},{5,4},{6,7},{7,6},{8,9},{9,8},{10,11... | collective-permute-start | bytes 393224 | tf_op jit(solution)/shard_map/ppermute | solution.py:403
  25.6 0.0 collective-permute-done.7.there
  25.6 0.0 collective-permute-done.6.far
  25.6 5.0 %far_part.1 = (f32[8,512,256]{2,1,0:T(8,128)S(1)}, f32[2,8,32,128]{3,2,1,0:T(8,128)S(1)}, bf16[2,8,32,128]{3,2,1,0:T(8,128)(2,1)S(1)}, bf16[2,8,32,128]{3,2,1,0:T(8,128)(2,1)S(1)}, bf16[2,8,32,128]{3,2,1,0:T(8,128)(2,1)S(1)}) custom-call(s32[10]{0:T(128)S(1)} %get-tuple-element.37.params, bf16[512,1024]{1,0:T(8,128)(2,1)S(1)} %copy-done, ...), custom_call_target="tpu_custom_call" | custom-call | flops 1600000000 | bytes 1048576 | tf_op jit(solution)/shard_map/far_part/pallas_call | solution.py:384
  30.5 3.3 %collective-permute-start.10 = (bf16[2,8,32,128]{3,2,1,0:T(8,128)(2,1)S(1)}, bf16[2,8,32,128]{3,2,1,0:T(8,128)(2,1)S(1)}, u32[]{:S(2)}, u32[]{:S(2)}) collective-permute-start(bf16[2,8,32,128]{3,2,1,0:T(8,128)(2,1)S(1)} %get-tuple-element.56), channel_id=1, source_target_pairs={{0,3},{1,2},{2,1},{3,0},{4,7},{5,6},{6,5},{7,4},{8,11},{9,10},{10,... | collective-permute-start | bytes 393224 | tf_op jit(solution)/shard_map/ppermute | solution.py:403
  33.9 0.0 collective-permute-start.9
  33.9 0.0 collective-permute-done.5.far
  33.9 7.4 %both.1 = (f32[2,8,32,128]{3,2,1,0:T(8,128)S(1)}, bf16[4,8,32,128]{3,2,1,0:T(8,128)(2,1)S(1)}, bf16[2,8,32,128]{3,2,1,0:T(8,128)(2,1)S(1)}, bf16[2,8,32,128]{3,2,1,0:T(8,128)(2,1)S(1)}) custom-call(s32[10]{0:T(128)S(1)} %get-tuple-element.37.params, bf16[512,1024]{1,0:T(8,128)(2,1)S(1)} %copy-done, bf16[2,256,128]{2,1,0:T(8,128)(2,1)S(1)} %collective-permute-done.4.mine, ...), custom_call_target="tpu_custom_call" | custom-call | flops 3200000000 | bytes 1048576 | tf_op jit(solution)/shard_map/both/pallas_call | solution.py:384
  41.3 1.2 %collective-permute-start.8 = (bf16[4,8,32,128]{3,2,1,0:T(8,128)(2,1)S(1)}, bf16[4,8,32,128]{3,2,1,0:T(8,128)(2,1)S(1)}, u32[]{:S(2)}, u32[]{:S(2)}) collective-permute-start(bf16[4,8,32,128]{3,2,1,0:T(8,128)(2,1)S(1)} %get-tuple-element.53), channel_id=1, source_target_pairs={{0,1},{1,0},{2,3},{3,2},{4,5},{5,4},{6,7},{7,6},{8,9},{9,8},{10,11... | collective-permute-start | bytes 786440 | tf_op jit(solution)/shard_map/ppermute | solution.py:403
  42.5 3.3 %collective-permute-start.12 = (bf16[2,8,32,128]{3,2,1,0:T(8,128)(2,1)S(1)}, bf16[2,8,32,128]{3,2,1,0:T(8,128)(2,1)S(1)}, u32[]{:S(2)}, u32[]{:S(2)}) collective-permute-start(bf16[2,8,32,128]{3,2,1,0:T(8,128)(2,1)S(1)} %get-tuple-element.60), channel_id=1, source_target_pairs={{0,3},{1,2},{2,1},{3,0},{4,7},{5,6},{6,5},{7,4},{8,11},{9,10},{10,... | collective-permute-start | bytes 393224 | tf_op jit(solution)/shard_map/ppermute | solution.py:403
  45.7 0.0 collective-permute-done.10.refs_2_
  45.7 0.1 collective-permute-done.9.refs_1_
  45.9 0.0 collective-permute-start.11
  45.9 10.0 %collective-permute-done.12.refs_5_ = bf16[2,8,32,128]{3,2,1,0:T(8,128)(2,1)S(1)} collective-permute-done((bf16[2,8,32,128]{3,2,1,0:T(8,128)(2,1)S(1)}, bf16[2,8,32,128]{3,2,1,0:T(8,128)(2,1)S(1)}, u32[]{:S(2)}, u32[]{:S(2)}) %collective-permute-start.12) | collective-permute-done | bytes 131104 | tf_op jit(solution)/shard_map/ppermute | solution.py:403
  55.8 0.9 %collective-permute-done.8.near_ref = bf16[4,8,32,128]{3,2,1,0:T(8,128)(2,1)S(1)} collective-permute-done((bf16[4,8,32,128]{3,2,1,0:T(8,128)(2,1)S(1)}, bf16[4,8,32,128]{3,2,1,0:T(8,128)(2,1)S(1)}, u32[]{:S(2)}, u32[]{:S(2)}) %collective-permute-start.8) | collective-permute-done | bytes 262176 | tf_op jit(solution)/shard_map/ppermute | solution.py:403
  56.7 0.0 collective-permute-done.11.refs_4_
  56.7 1.6 %assemble.1 = f32[4,16,32,128]{3,2,1,0:T(8,128)} custom-call(s32[10]{0:T(128)S(1)} %get-tuple-element.37.params, bf16[4,8,32,128]{3,2,1,0:T(8,128)(2,1)S(1)} %collective-permute-done.8.near_ref, f32[2,8,32,128]{3,2,1,0:T(8,128)S(1)} %get-tuple-element.54.refs_0_, bf16[2,8,32,128]{3,2,1,0:T(8,128)(2,1)S(1)} %collective-permute-done.9.refs_1_, ...), custom_call_target="tpu_custom_call" | custom-call | tf_op jit(solution)/shard_map/assemble/pallas_call | solution.py:472
  (2 shorter events, 0.1 us)
Async XLA Ops:
  0.0 13.1 %copy-start.3 = (bf16[512,256]{1,0:T(8,128)(2,1)S(1)}, bf16[512,256]{1,0:T(8,128)(2,1)}, u32[]{:S(2)}) copy-start(bf16[512,256]{1,0:T(8,128)(2,1)} %constant.17.clone.table_ref.stab) | copy-start | bytes 786436
  0.1 13.8 %copy-start.1 = (f32[2,4,256,128]{3,2,1,0:T(8,128)S(1)}, f32[2,4,256,128]{3,2,1,0:T(8,128)}, u32[]{:S(2)}) copy-start(f32[2,4,256,128]{3,2,1,0:T(8,128)} %constant.20.clone.dop_ref) | copy-start | bytes 3145732
  0.1 13.8 %copy-start.2 = (f32[2,4,192,128]{3,2,1,0:T(8,128)S(1)}, f32[2,4,192,128]{3,2,1,0:T(8,128)}, u32[]{:S(2)}) copy-start(f32[2,4,192,128]{3,2,1,0:T(8,128)} %constant.19.clone.lag_ref) | copy-start | bytes 2359300
  6.4 14.2 %copy-start = (bf16[512,1024]{1,0:T(8,128)(2,1)S(1)}, bf16[512,1024]{1,0:T(8,128)(2,1)}, u32[]{:S(2)}) copy-start(bf16[512,1024]{1,0:T(8,128)(2,1)} %constant.18.clone.rtab) | copy-start | bytes 3145732
  6.4 3.2 %collective-permute-start = (bf16[2,256,128]{2,1,0:T(8,128)(2,1)S(1)}, bf16[2,256,128]{2,1,0:T(8,128)(2,1)S(1)}, u32[]{:S(2)}, u32[]{:S(2)}) collective-permute-start(bf16[2,256,128]{2,1,0:T(8,128)(2,1)S(1)} %get-tuple-element.34), channel_id=1, source_target_pairs={{0,4},{4,0},{8,12},{12,8},{16,20},{20,16},{24,28},{28,24},{1,5},{5... | collective-permute-start | bytes 393224 | tf_op jit(solution)/shard_map/ppermute | solution.py:403
  6.9 18.7 %collective-permute-start.7 = (bf16[8,256,128]{2,1,0:T(8,128)(2,1)S(1)}, bf16[8,256,128]{2,1,0:T(8,128)(2,1)S(1)}, u32[]{:S(2)}, u32[]{:S(2)}) collective-permute-start(bf16[8,256,128]{2,1,0:T(8,128)(2,1)S(1)} %get-tuple-element.48), channel_id=1, source_target_pairs={{0,1},{1,0},{2,3},{3,2},{4,5},{5,4},{6,7},{7,6},{8,9},{9,8},{10,11... | collective-permute-start | bytes 1572872 | tf_op jit(solution)/shard_map/ppermute | solution.py:403
  9.6 6.0 %collective-permute-start.1 = (bf16[2,256,128]{2,1,0:T(8,128)(2,1)S(1)}, bf16[2,256,128]{2,1,0:T(8,128)(2,1)S(1)}, u32[]{:S(2)}, u32[]{:S(2)}) collective-permute-start(bf16[2,256,128]{2,1,0:T(8,128)(2,1)S(1)} %add.12), channel_id=1, source_target_pairs={{0,8},{4,12},{8,0},{12,4},{16,24},{20,28},{24,16},{28,20},{1,9},{5... | collective-permute-start | bytes 393224 | tf_op jit(solution)/shard_map/ppermute | solution.py:403
  11.1 8.1 %collective-permute-start.2 = (bf16[2,256,128]{2,1,0:T(8,128)(2,1)S(1)}, bf16[2,256,128]{2,1,0:T(8,128)(2,1)S(1)}, u32[]{:S(2)}, u32[]{:S(2)}) collective-permute-start(bf16[2,256,128]{2,1,0:T(8,128)(2,1)S(1)} %add.12), channel_id=1, source_target_pairs={{0,16},{4,20},{8,24},{12,28},{16,0},{20,4},{24,8},{28,12},{1,17},{... | collective-permute-start | bytes 393224 | tf_op jit(solution)/shard_map/ppermute | solution.py:403
  12.7 6.6 %collective-permute-start.3 = (bf16[2,256,128]{2,1,0:T(8,128)(2,1)S(1)}, bf16[2,256,128]{2,1,0:T(8,128)(2,1)S(1)}, u32[]{:S(2)}, u32[]{:S(2)}) collective-permute-start(bf16[2,256,128]{2,1,0:T(8,128)(2,1)S(1)} %add.12), channel_id=1, source_target_pairs={{0,24},{4,28},{8,16},{12,20},{16,8},{20,12},{24,0},{28,4},{1,25},{... | collective-permute-start | bytes 393224 | tf_op jit(solution)/shard_map/ppermute | solution.py:403
  19.3 6.3 %collective-permute-start.6 = (bf16[2,256,128]{2,1,0:T(8,128)(2,1)S(1)}, bf16[2,256,128]{2,1,0:T(8,128)(2,1)S(1)}, u32[]{:S(2)}, u32[]{:S(2)}) collective-permute-start(bf16[2,256,128]{2,1,0:T(8,128)(2,1)S(1)} %add_add_fusion.mine), channel_id=1, source_target_pairs={{0,1},{1,0},{2,3},{3,2},{4,5},{5,4},{6,7},{7,6},{8,9},{9,8},{10,11... | collective-permute-start | bytes 393224 | tf_op jit(solution)/shard_map/ppermute | solution.py:403
  20.6 4.1 %collective-permute-start.4 = (bf16[2,256,128]{2,1,0:T(8,128)(2,1)S(1)}, bf16[2,256,128]{2,1,0:T(8,128)(2,1)S(1)}, u32[]{:S(2)}, u32[]{:S(2)}) collective-permute-start(bf16[2,256,128]{2,1,0:T(8,128)(2,1)S(1)} %add_add_fusion.mine), channel_id=1, source_target_pairs={{0,4},{4,0},{8,12},{12,8},{16,20},{20,16},{24,28},{28,24},{1,5},{5... | collective-permute-start | bytes 393224 | tf_op jit(solution)/shard_map/ppermute | solution.py:403
  24.7 9.2 %collective-permute-start.5 = (bf16[2,256,128]{2,1,0:T(8,128)(2,1)S(1)}, bf16[2,256,128]{2,1,0:T(8,128)(2,1)S(1)}, u32[]{:S(2)}, u32[]{:S(2)}) collective-permute-start(bf16[2,256,128]{2,1,0:T(8,128)(2,1)S(1)} %collective-permute-done.4.mine), channel_id=1, source_target_pairs={{0,1},{1,0},{2,3},{3,2},{4,5},{5,4},{6,7},{7,6},{8,9},{9,8},{10,11... | collective-permute-start | bytes 393224 | tf_op jit(solution)/shard_map/ppermute | solution.py:403
  30.5 15.2 %collective-permute-start.10 = (bf16[2,8,32,128]{3,2,1,0:T(8,128)(2,1)S(1)}, bf16[2,8,32,128]{3,2,1,0:T(8,128)(2,1)S(1)}, u32[]{:S(2)}, u32[]{:S(2)}) collective-permute-start(bf16[2,8,32,128]{3,2,1,0:T(8,128)(2,1)S(1)} %get-tuple-element.56), channel_id=1, source_target_pairs={{0,3},{1,2},{2,1},{3,0},{4,7},{5,6},{6,5},{7,4},{8,11},{9,10},{10,... | collective-permute-start | bytes 393224 | tf_op jit(solution)/shard_map/ppermute | solution.py:403
  33.9 12.0 %collective-permute-start.9 = (bf16[2,8,32,128]{3,2,1,0:T(8,128)(2,1)S(1)}, bf16[2,8,32,128]{3,2,1,0:T(8,128)(2,1)S(1)}, u32[]{:S(2)}, u32[]{:S(2)}) collective-permute-start(bf16[2,8,32,128]{3,2,1,0:T(8,128)(2,1)S(1)} %get-tuple-element.55), channel_id=1, source_target_pairs={{0,2},{1,3},{2,0},{3,1},{4,6},{5,7},{6,4},{7,5},{8,10},{9,11},{10,... | collective-permute-start | bytes 393224 | tf_op jit(solution)/shard_map/ppermute | solution.py:403
  41.3 15.5 %collective-permute-start.8 = (bf16[4,8,32,128]{3,2,1,0:T(8,128)(2,1)S(1)}, bf16[4,8,32,128]{3,2,1,0:T(8,128)(2,1)S(1)}, u32[]{:S(2)}, u32[]{:S(2)}) collective-permute-start(bf16[4,8,32,128]{3,2,1,0:T(8,128)(2,1)S(1)} %get-tuple-element.53), channel_id=1, source_target_pairs={{0,1},{1,0},{2,3},{3,2},{4,5},{5,4},{6,7},{7,6},{8,9},{9,8},{10,11... | collective-permute-start | bytes 786440 | tf_op jit(solution)/shard_map/ppermute | solution.py:403
  42.5 13.4 %collective-permute-start.12 = (bf16[2,8,32,128]{3,2,1,0:T(8,128)(2,1)S(1)}, bf16[2,8,32,128]{3,2,1,0:T(8,128)(2,1)S(1)}, u32[]{:S(2)}, u32[]{:S(2)}) collective-permute-start(bf16[2,8,32,128]{3,2,1,0:T(8,128)(2,1)S(1)} %get-tuple-element.60), channel_id=1, source_target_pairs={{0,3},{1,2},{2,1},{3,0},{4,7},{5,6},{6,5},{7,4},{8,11},{9,10},{10,... | collective-permute-start | bytes 393224 | tf_op jit(solution)/shard_map/ppermute | solution.py:403
  45.9 10.9 %collective-permute-start.11 = (bf16[2,8,32,128]{3,2,1,0:T(8,128)(2,1)S(1)}, bf16[2,8,32,128]{3,2,1,0:T(8,128)(2,1)S(1)}, u32[]{:S(2)}, u32[]{:S(2)}) collective-permute-start(bf16[2,8,32,128]{3,2,1,0:T(8,128)(2,1)S(1)} %get-tuple-element.59), channel_id=1, source_target_pairs={{0,2},{1,3},{2,0},{3,1},{4,6},{5,7},{6,4},{7,5},{8,10},{9,11},{10,... | collective-permute-start | bytes 393224 | tf_op jit(solution)/shard_map/ppermute | solution.py:403
